TPU v7x, 32 devices: a whole 2x2x4 slice. The times are simulated.
32 devices in a mesh: dp: 4 (over y, core), fsdp: 8 (over z, x).
Axes of the slice: x: 2, y: 2, z: 4, core: 2. Of those that a mesh axis runs over, the one named last changes fastest.
Arguments:
- tokens: bfloat16 [32, 256, 2048], P(('dp', 'fsdp')), may hold values from -6 to 6
- labels: int32 [32], P(('dp', 'fsdp')), may hold values from 0 to 2
- counts: int32 [3], replicated, may hold values from 1365 to 4095
- grad_out: bfloat16 [32, 256, 2048], P(('dp', 'fsdp')), may hold values from -6 to 6
- w_query: bfloat16 [2048, 2048], P(('dp', 'fsdp')), may hold values from -0.125 to 0.125
- w_key: bfloat16 [2048, 2048], P(('dp', 'fsdp')), may hold values from -0.125 to 0.125
- w_value: bfloat16 [2048, 2048], P(('dp', 'fsdp')), may hold values from -0.125 to 0.125
- w_out: bfloat16 [2048, 2048], P(('dp', 'fsdp')), may hold values from -0.375 to 0.375
- gain_attn: bfloat16 [2048], P(('dp', 'fsdp')), may hold values from 0.099609375 to 1.8984375
- gain_mlp: bfloat16 [2048], P(('dp', 'fsdp')), may hold values from 0.099609375 to 1.8984375
- w_gate: bfloat16 [2048, 8192], P(('dp', 'fsdp')), may hold values from -0.125 to 0.125
- w_up: bfloat16 [2048, 8192], P(('dp', 'fsdp')), may hold values from -0.125 to 0.125
- w_down: bfloat16 [8192, 2048], P(('dp', 'fsdp')), may hold values from -0.0625 to 0.0625
Outputs:
- layer_out: bfloat16 [32, 256, 2048], P(('dp', 'fsdp'))
- grad_tokens: float32 [32, 256, 2048], P(('dp', 'fsdp'))
- grad_query: float32 [2048, 2048], P(('dp', 'fsdp'))
- grad_key: float32 [2048, 2048], P(('dp', 'fsdp'))
- grad_value: float32 [2048, 2048], P(('dp', 'fsdp'))
- grad_out_proj: float32 [2048, 2048], P(('dp', 'fsdp'))
- grad_gain_attn: float32 [2048], P(('dp', 'fsdp'))
- grad_gain_mlp: float32 [2048], P(('dp', 'fsdp'))
- grad_gate: float32 [2048, 8192], P(('dp', 'fsdp'))
- grad_up: float32 [2048, 8192], P(('dp', 'fsdp'))
- grad_down: float32 [8192, 2048], P(('dp', 'fsdp'))
All inputs are finite; a program needn't handle non-finite values.
Results may differ from a plain program's by a relative error of at most 0.014.
Values may be sent and summed in bfloat16 or wider, within the bound.
A program may use at most 704 MiB of HBM per device.

v0:
```python
import jax
import jax.numpy as jnp
from jax import lax
from jax.sharding import PartitionSpec as P

HEAD_DIM = 64


epsilon = 1e-05
rope_base = 130000.0


def rope_tables(seq_len, head_dim):
    half_dim = head_dim // 2
    frequency = rope_base ** (-(jnp.arange(half_dim).astype(jnp.float32) * 2.0) / head_dim)
    angles = jnp.arange(seq_len).astype(jnp.float32)[:, None] * frequency[None, :]
    angles = jnp.concatenate([angles, angles], axis=1)
    return (jnp.cos(angles), jnp.sin(angles))


def rotate(tensor, cosine, sine):
    half_dim = tensor.shape[-1] // 2
    turned = jnp.concatenate([-tensor[..., half_dim:], tensor[..., :half_dim]], axis=-1)
    return tensor * cosine[:, None, :] + turned * sine[:, None, :]


def unrotate(grads, cosine, sine):
    half_dim = grads.shape[-1] // 2
    turned = grads * sine[:, None, :]
    return grads * cosine[:, None, :] + jnp.concatenate(
        [turned[..., half_dim:], -turned[..., :half_dim]], axis=-1
    )


def outer_sum(left, right):
    return lax.dot_general(
        left, right, (((0,), (0,)), ((), ())), preferred_element_type=jnp.float32
    )


def times_transposed(left, weight):
    return lax.dot_general(
        left, weight, (((1,), (1,)), ((), ())), preferred_element_type=jnp.float32
    )


def causal_mask(seq_len):
    return lax.broadcasted_iota(jnp.int32, (seq_len, seq_len), 1) <= lax.broadcasted_iota(
        jnp.int32, (seq_len, seq_len), 0
    )


def heads_first(tensor, groups):
    batch_size, seq_len, head_count, head_dim = tensor.shape
    return tensor.reshape(batch_size, seq_len, groups, head_count // groups, head_dim).transpose(
        2, 0, 3, 1, 4
    )


def heads_back(tensor):
    groups, batch_size, per_group, seq_len, head_dim = tensor.shape
    return tensor.transpose(1, 3, 0, 2, 4).reshape(
        batch_size, seq_len, groups * per_group, head_dim
    )


def attend(block_items):
    queries, keys_rot, values = block_items
    scale_factor = queries.shape[-1] ** (-0.5)
    scores = (
        jnp.einsum("bhqd,bhkd->bhqk", queries, keys_rot, preferred_element_type=jnp.float32)
        * scale_factor
    )
    scores = jnp.where(causal_mask(scores.shape[-1]), scores, -1e30)
    row_max = jnp.max(scores, axis=-1, keepdims=True)
    exp_scores = jnp.exp(scores - row_max)
    row_total = jnp.sum(exp_scores, axis=-1, keepdims=True)
    soft = (exp_scores / row_total).astype(jnp.bfloat16)
    mixed = jnp.einsum("bhqk,bhkd->bhqd", soft, values, preferred_element_type=jnp.float32)
    return (mixed, (row_max + jnp.log(row_total))[..., 0])


def attend_back(block_items):
    queries, keys_rot, values, grad_mixed, log_total = block_items
    scale_factor = queries.shape[-1] ** (-0.5)
    scores = (
        jnp.einsum("bhqd,bhkd->bhqk", queries, keys_rot, preferred_element_type=jnp.float32)
        * scale_factor
    )
    soft = jnp.where(causal_mask(scores.shape[-1]), jnp.exp(scores - log_total[..., None]), 0.0)
    grad_soft = jnp.einsum(
        "bhqd,bhkd->bhqk", grad_mixed, values, preferred_element_type=jnp.float32
    )
    grad_scores = (soft * (grad_soft - jnp.sum(soft * grad_soft, axis=-1, keepdims=True))).astype(
        jnp.bfloat16
    )
    grad_queries = (
        jnp.einsum("bhqk,bhkd->bhqd", grad_scores, keys_rot, preferred_element_type=jnp.float32)
        * scale_factor
    )
    grad_keys = (
        jnp.einsum("bhqk,bhqd->bhkd", grad_scores, queries, preferred_element_type=jnp.float32)
        * scale_factor
    )
    grad_values = jnp.einsum(
        "bhqk,bhqd->bhkd", soft.astype(jnp.bfloat16), grad_mixed, preferred_element_type=jnp.float32
    )
    return (grad_queries, grad_keys, grad_values)


def on_device(
    tokens,
    labels,
    counts,
    grad_out,
    w_query,
    w_key,
    w_value,
    w_out,
    gain_attn,
    gain_mlp,
    w_gate,
    w_up,
    w_down,
):
    batch_size, seq_len, model_width = tokens.shape
    head_count = model_width // HEAD_DIM
    groups = max(1, min(head_count, head_count * seq_len // 8192))
    four_shape = (batch_size, seq_len, head_count, HEAD_DIM)
    rows_in = tokens.reshape(-1, model_width).astype(jnp.float32)
    row_count = rows_in.shape[0]
    hidden_width = w_gate.shape[1]
    outer_count = lax.axis_size("dp")
    inner_count = lax.axis_size("fsdp")
    attn_set = (
        lax.all_gather(w_query, ("dp", "fsdp"), axis=0, tiled=True),
        lax.all_gather(w_key, ("dp", "fsdp"), axis=0, tiled=True),
        lax.all_gather(w_value, ("dp", "fsdp"), axis=0, tiled=True),
        lax.all_gather(w_out, ("dp", "fsdp"), axis=0, tiled=True),
        lax.all_gather(gain_attn, ("dp", "fsdp"), axis=0, tiled=True),
        lax.all_gather(gain_mlp, ("dp", "fsdp"), axis=0, tiled=True),
    )
    gain_one = attn_set[4].astype(jnp.float32)
    gain_two = attn_set[5].astype(jnp.float32)
    inv_one = lax.rsqrt(jnp.mean(rows_in * rows_in, axis=-1, keepdims=True) + epsilon)
    act_one = (rows_in * inv_one * gain_one).astype(jnp.bfloat16)
    queries = jnp.dot(act_one, attn_set[0], preferred_element_type=jnp.float32)
    keys_raw = jnp.dot(act_one, attn_set[1], preferred_element_type=jnp.float32)
    values = jnp.dot(act_one, attn_set[2], preferred_element_type=jnp.float32).astype(jnp.bfloat16)
    cosine, sine = rope_tables(seq_len, HEAD_DIM)
    q_rot = rotate(queries.reshape(four_shape), cosine, sine).astype(jnp.bfloat16)
    k_rot = rotate(keys_raw.reshape(four_shape), cosine, sine).astype(jnp.bfloat16)
    q_heads = heads_first(q_rot, groups)
    k_heads = heads_first(k_rot, groups)
    v_heads = heads_first(values.reshape(four_shape), groups)
    mixed, log_total = lax.map(attend, (q_heads, k_heads, v_heads))
    attended = heads_back(mixed).reshape(row_count, model_width).astype(jnp.bfloat16)
    resid = rows_in + jnp.dot(attended, attn_set[3], preferred_element_type=jnp.float32)
    inv_two = lax.rsqrt(jnp.mean(resid * resid, axis=-1, keepdims=True) + epsilon)
    act_two = (resid * inv_two * gain_two).astype(jnp.bfloat16)
    pieces = (
        lax.all_gather(w_gate, ("dp", "fsdp"), axis=0, tiled=True),
        lax.all_gather(w_up, ("dp", "fsdp"), axis=0, tiled=True),
    )
    columns = act_two
    gate_pre = jnp.dot(columns, pieces[0], preferred_element_type=jnp.float32)
    up_proj = jnp.dot(columns, pieces[1], preferred_element_type=jnp.float32)
    middle = (jax.nn.silu(gate_pre) * up_proj).astype(jnp.bfloat16)
    columns = middle
    down_out = jnp.dot(
        columns,
        lax.all_gather(w_down, ("dp", "fsdp"), axis=0, tiled=True),
        preferred_element_type=jnp.float32,
    )
    layer_out = (resid + down_out).astype(jnp.bfloat16).reshape(tokens.shape)
    token_total = float(seq_len * outer_count * inner_count)
    picked_counts = jnp.sum(
        jnp.where(labels[:, None] == jnp.arange(3)[None, :], counts[None, :], 0), axis=1
    ).astype(jnp.float32)
    factor = token_total / (3.0 * picked_counts)
    cotangent = (grad_out.astype(jnp.float32) * factor[:, None, None]).reshape(
        row_count, model_width
    )
    dy_rows = cotangent.astype(jnp.bfloat16)
    down_grad = lax.psum_scatter(
        outer_sum(middle, dy_rows), ("dp", "fsdp"), scatter_dimension=0, tiled=True
    )
    grad_middle = times_transposed(
        dy_rows, lax.all_gather(w_down, ("dp", "fsdp"), axis=0, tiled=True)
    )
    sigmoid_gate = jax.nn.sigmoid(gate_pre)
    grad_gate_pre = (
        grad_middle * up_proj * sigmoid_gate * (1.0 + gate_pre * (1.0 - sigmoid_gate))
    ).astype(jnp.bfloat16)
    grad_up_proj = (grad_middle * gate_pre * sigmoid_gate).astype(jnp.bfloat16)
    grad_both = jnp.concatenate([grad_gate_pre, grad_up_proj], axis=1)
    both_grads = lax.psum_scatter(
        outer_sum(act_two, grad_both), ("dp", "fsdp"), scatter_dimension=0, tiled=True
    )
    gate_grad = both_grads[:, :hidden_width]
    up_grad = both_grads[:, hidden_width:]
    pieces = (
        lax.all_gather(w_gate, ("dp", "fsdp"), axis=0, tiled=True),
        lax.all_gather(w_up, ("dp", "fsdp"), axis=0, tiled=True),
    )
    added = times_transposed(grad_gate_pre, pieces[0]) + times_transposed(grad_up_proj, pieces[1])
    grad_gain_two = jnp.sum(added * resid * inv_two, axis=0)
    scaled_two = gain_two * added
    grad_resid = (
        cotangent
        + inv_two * scaled_two
        - resid * inv_two**3 * jnp.mean(scaled_two * resid, axis=-1, keepdims=True)
    )
    grad_branch = grad_resid.astype(jnp.bfloat16)
    back_set = (
        lax.all_gather(w_query, ("dp", "fsdp"), axis=0, tiled=True),
        lax.all_gather(w_key, ("dp", "fsdp"), axis=0, tiled=True),
        lax.all_gather(w_value, ("dp", "fsdp"), axis=0, tiled=True),
        lax.all_gather(w_out, ("dp", "fsdp"), axis=0, tiled=True),
        lax.all_gather(gain_attn, ("dp", "fsdp"), axis=0, tiled=True),
        lax.all_gather(gain_mlp, ("dp", "fsdp"), axis=0, tiled=True),
    )
    grad_attended = times_transposed(grad_branch, back_set[3]).astype(jnp.bfloat16)
    grad_heads = heads_first(grad_attended.reshape(four_shape), groups)
    grad_q_rot, grad_k_rot, grad_v_heads = lax.map(
        attend_back, (q_heads, k_heads, v_heads, grad_heads, log_total)
    )
    grad_queries = (
        unrotate(heads_back(grad_q_rot), cosine, sine)
        .reshape(row_count, model_width)
        .astype(jnp.bfloat16)
    )
    grad_keys = (
        unrotate(heads_back(grad_k_rot), cosine, sine)
        .reshape(row_count, model_width)
        .astype(jnp.bfloat16)
    )
    grad_values = heads_back(grad_v_heads).reshape(row_count, model_width).astype(jnp.bfloat16)
    grad_act_one = (
        times_transposed(grad_queries, back_set[0])
        + times_transposed(grad_keys, back_set[1])
        + times_transposed(grad_values, back_set[2])
    )
    grad_gain_one = jnp.sum(grad_act_one * rows_in * inv_one, axis=0)
    scaled_one = gain_one * grad_act_one
    grad_rows = (
        grad_resid
        + inv_one * scaled_one
        - rows_in * inv_one**3 * jnp.mean(scaled_one * rows_in, axis=-1, keepdims=True)
    )
    attn_grads = (
        lax.psum_scatter(
            outer_sum(act_one, grad_queries), ("dp", "fsdp"), scatter_dimension=0, tiled=True
        ),
        lax.psum_scatter(
            outer_sum(act_one, grad_keys), ("dp", "fsdp"), scatter_dimension=0, tiled=True
        ),
        lax.psum_scatter(
            outer_sum(act_one, grad_values), ("dp", "fsdp"), scatter_dimension=0, tiled=True
        ),
        lax.psum_scatter(
            outer_sum(attended, grad_branch), ("dp", "fsdp"), scatter_dimension=0, tiled=True
        ),
        lax.psum_scatter(grad_gain_one, ("dp", "fsdp"), scatter_dimension=0, tiled=True),
        lax.psum_scatter(grad_gain_two, ("dp", "fsdp"), scatter_dimension=0, tiled=True),
    )
    grad_tokens = grad_rows.reshape(tokens.shape)
    return (
        layer_out,
        grad_tokens,
        attn_grads[0],
        attn_grads[1],
        attn_grads[2],
        attn_grads[3],
        attn_grads[4],
        attn_grads[5],
        gate_grad,
        up_grad,
        down_grad,
    )


def solution(mesh):
    in_specs = (
        P(("dp", "fsdp"), None, None),
        P(("dp", "fsdp")),
        P(),
        P(("dp", "fsdp"), None, None),
        P(("dp", "fsdp"), None),
        P(("dp", "fsdp"), None),
        P(("dp", "fsdp"), None),
        P(("dp", "fsdp"), None),
        P(("dp", "fsdp")),
        P(("dp", "fsdp")),
        P(("dp", "fsdp"), None),
        P(("dp", "fsdp"), None),
        P(("dp", "fsdp"), None),
    )
    out_specs = (
        P(("dp", "fsdp"), None, None),
        P(("dp", "fsdp"), None, None),
        P(("dp", "fsdp"), None),
        P(("dp", "fsdp"), None),
        P(("dp", "fsdp"), None),
        P(("dp", "fsdp"), None),
        P(("dp", "fsdp")),
        P(("dp", "fsdp")),
        P(("dp", "fsdp"), None),
        P(("dp", "fsdp"), None),
        P(("dp", "fsdp"), None),
    )
    return jax.shard_map(
        on_device, mesh=mesh, in_specs=in_specs, out_specs=out_specs, check_vma=False
    )
```

profile of v0, /device:TPU:1, one launch (start us, length us, event | category | flops | bytes accessed | tf_op | source)
XLA Modules:
  0.0 5715.2 jit_solution(15285784957963753207)
XLA Ops:
  14.5 41.7 all-reduce.6
  57.4 33.6 all-gather.12.cloned.1.call-done
  98.3 71.8 %all-gather.8.cloned.1.call-done = bf16[2048,2048]{1,0:T(8,128)(2,1)} async-done(((bf16[64,2048]{1,0:T(8,128)(2,1)}), bf16[2048,2048]{1,0:T(8,128)(2,1)}) %all-gather.8.cloned.1.call-update) | async-done | bytes 8388624 | tf_op jit(solution)/shard_map/all_gather | solution.py:136
  170.1 6.8 fusion.76
  178.4 70.7 %all-gather.10.cloned.1.call-done = bf16[2048,2048]{1,0:T(8,128)(2,1)} async-done(((bf16[64,2048]{1,0:T(8,128)(2,1)}), bf16[2048,2048]{1,0:T(8,128)(2,1)}) %all-gather.10.cloned.1.call-update) | async-done | bytes 8388624 | tf_op jit(solution)/shard_map/all_gather | solution.py:137
  249.1 6.8 fusion.74
  266.5 61.5 %all-gather.14.cloned.1.call-done = bf16[2048,2048]{1,0:T(8,128)(2,1)} async-done(((bf16[64,2048]{1,0:T(8,128)(2,1)}), bf16[2048,2048]{1,0:T(8,128)(2,1)}) %all-gather.14.cloned.1.call-update) | async-done | bytes 8388624 | tf_op jit(solution)/shard_map/all_gather | solution.py:139
  328.0 5.8 multiply_reduce_fusion.3
  335.4 188.9 %all-gather.18.cloned.1.call-done = bf16[2048,8192]{1,0:T(8,128)(2,1)} async-done(((bf16[64,8192]{1,0:T(8,128)(2,1)}), bf16[2048,8192]{1,0:T(8,128)(2,1)}) %all-gather.18.cloned.1.call-update) | async-done | bytes 33554448 | tf_op jit(solution)/shard_map/all_gather | solution.py:163
  524.2 17.8 fusion.82
  542.0 178.1 %all-gather.16.cloned.1.call-done = bf16[2048,8192]{1,0:T(8,128)(2,1)} async-done(((bf16[64,8192]{1,0:T(8,128)(2,1)}), bf16[2048,8192]{1,0:T(8,128)(2,1)}) %all-gather.16.cloned.1.call-update) | async-done | bytes 33554448 | tf_op jit(solution)/shard_map/all_gather | solution.py:162
  720.1 17.7 fusion.81
  737.8 178.3 %all-gather.20.cloned.1.call-done = bf16[8192,2048]{1,0:T(8,128)(2,1)} async-done(((bf16[256,2048]{1,0:T(8,128)(2,1)}), bf16[8192,2048]{1,0:T(8,128)(2,1)}) %all-gather.20.cloned.1.call-update) | async-done | bytes 33554448 | tf_op jit(solution)/shard_map/all_gather | solution.py:172
  916.1 23.3 multiply_convert_fusion.1
  939.4 46.7 fusion
  986.2 19.0 fusion.83
  1005.3 16.7 multiply_reduce_fusion.1
  1023.3 8.3 fusion.56
  1032.5 6.9 convolution_convert_fusion
  1047.1 8.4 fusion.67
  1073.9 8.6 fusion.71
  1082.6 10.7 fusion.69
  1093.4 27.7 fusion.54
  1124.8 6.2 fusion.84
  1137.7 39.8 all-reduce.5
  1183.1 18.4 fusion.20
  1201.4 1661.7 %all-reduce.9.cloned.1.call-done = f32[2048,16384]{1,0:T(8,128)} async-done(((f32[2048,16384]{1,0:T(8,128)}), f32[2048,16384]{1,0:T(8,128)}) %all-reduce.9.cloned.1.call-update) | async-done | bytes 134217744
  2868.1 354.5 %reduce-scatter.12.cloned.1.call-done = f32[64,2048]{1,0:T(8,128)} async-done(((f32[2048,2048]{1,0:T(8,128)}), f32[64,2048]{1,0:T(8,128)}) %reduce-scatter.12.cloned.1.call-update) | async-done | bytes 524304 | tf_op jit(solution)/shard_map/reduce_scatter | solution.py:261
  3222.6 360.1 %reduce-scatter.10.cloned.1.call-done = f32[64,2048]{1,0:T(8,128)} async-done(((f32[2048,2048]{1,0:T(8,128)}), f32[64,2048]{1,0:T(8,128)}) %reduce-scatter.10.cloned.1.call-update) | async-done | bytes 524304 | tf_op jit(solution)/shard_map/reduce_scatter | solution.py:258
  3582.6 360.2 %reduce-scatter.6.cloned.1.call-done = f32[64,2048]{1,0:T(8,128)} async-done(((f32[2048,2048]{1,0:T(8,128)}), f32[64,2048]{1,0:T(8,128)}) %reduce-scatter.6.cloned.1.call-update) | async-done | bytes 524304 | tf_op jit(solution)/shard_map/reduce_scatter | solution.py:252
  3942.9 360.1 %reduce-scatter.8.cloned.1.call-done = f32[64,2048]{1,0:T(8,128)} async-done(((f32[2048,2048]{1,0:T(8,128)}), f32[64,2048]{1,0:T(8,128)}) %reduce-scatter.8.cloned.1.call-update) | async-done | bytes 524304 | tf_op jit(solution)/shard_map/reduce_scatter | solution.py:255
  4303.0 1405.5 %reduce-scatter.14.cloned.1.call-done = f32[256,2048]{1,0:T(8,128)} async-done(((f32[8192,2048]{1,0:T(8,128)}), f32[256,2048]{1,0:T(8,128)}) %reduce-scatter.14.cloned.1.call-update) | async-done | bytes 2097168 | tf_op jit(solution)/shard_map/reduce_scatter | solution.py:185
  (173 shorter events, 76.7 us)
Async XLA Ops:
  7.2 83.8 %all-gather.12.cloned.1.call-start = ((), (), s32[]{:S(2)}) async-start(), calls=%async_computation.7 | async-start | bytes 8650752 | tf_op jit(solution)/shard_map/all_gather | solution.py:138
  7.9 48.6 copy-start.1
  8.0 162.1 %all-gather.8.cloned.1.call-start = ((), (), s32[]{:S(2)}) async-start(), calls=%async_computation.5 | async-start | bytes 8650752 | tf_op jit(solution)/shard_map/all_gather | solution.py:136
  8.7 240.4 %all-gather.10.cloned.1.call-start = ((), (), s32[]{:S(2)}) async-start(), calls=%async_computation.6 | async-start | bytes 8650752 | tf_op jit(solution)/shard_map/all_gather | solution.py:137
  9.4 318.5 %all-gather.14.cloned.1.call-start = ((), (), s32[]{:S(2)}) async-start(), calls=%async_computation.8 | async-start | bytes 8650752 | tf_op jit(solution)/shard_map/all_gather | solution.py:139
  10.0 514.2 %all-gather.18.cloned.1.call-start = ((), (), s32[]{:S(2)}) async-start(), calls=%async_computation.10 | async-start | bytes 34603008 | tf_op jit(solution)/shard_map/all_gather | solution.py:163
  10.6 709.5 %all-gather.16.cloned.1.call-start = ((), (), s32[]{:S(2)}) async-start(), calls=%async_computation.9 | async-start | bytes 34603008 | tf_op jit(solution)/shard_map/all_gather | solution.py:162
  11.2 904.9 %all-gather.20.cloned.1.call-start = ((), (), s32[]{:S(2)}) async-start(), calls=%async_computation.11 | async-start | bytes 34603008 | tf_op jit(solution)/shard_map/all_gather | solution.py:172
  11.9 2851.3 %all-reduce.9.cloned.1.call-start = ((), (), s32[]{:S(2)}) async-start(), calls=%async_computation.17 | async-start | bytes 268435456
  56.1 193.0 %copy-start.30 = (f32[2048]{0:T(1024)}, f32[2048]{0:T(1024)S(1)}, u32[]{:S(2)}) copy-start(f32[2048]{0:T(1024)S(1)} %convert_element_type.187) | copy-start | bytes 24580
  56.2 278.3 %copy-start.36 = (f32[2048]{0:T(1024)}, f32[2048]{0:T(1024)S(1)}, u32[]{:S(2)}) copy-start(f32[2048]{0:T(1024)S(1)} %convert_element_type.199) | copy-start | bytes 24580
  56.3 205.6 %copy-start.22 = (pred[256,256]{0,1:T(8,128)(4,1)}, pred[256,256]{0,1:T(8,128)(4,1)S(1)}, u32[]{:S(2)}) copy-start(pred[256,256]{0,1:T(8,128)(4,1)S(1)} %iota_compare_fusion) | copy-start | bytes 196612
  56.5 199.6 %copy-start.26 = (f32[256,64]{0,1:T(8,128)}, f32[256,64]{0,1:T(8,128)S(1)}, u32[]{:S(2)}) copy-start(f32[256,64]{0,1:T(8,128)S(1)} %get-tuple-element.89) | copy-start | bytes 196612
  56.5 199.6 %copy-start.28 = (f32[256,64]{0,1:T(8,128)}, f32[256,64]{0,1:T(8,128)S(1)}, u32[]{:S(2)}) copy-start(f32[256,64]{0,1:T(8,128)S(1)} %get-tuple-element.90) | copy-start | bytes 196612
  57.4 191.7 %copy-start.38 = (f32[256]{0:T(256)}, f32[256]{0:T(256)S(1)}, u32[]{:S(2)}) copy-start(f32[256]{0:T(256)S(1)} %get-tuple-element.92) | copy-start | bytes 3076
  266.5 67.3 %copy-start.14 = (bf16[32,256,64]{1,2,0:T(8,128)(2,1)}, bf16[32,256,64]{1,2,0:T(8,128)(2,1)S(1)}, u32[]{:S(2)}) copy-start(bf16[32,256,64]{1,2,0:T(8,128)(2,1)S(1)} %fusion.45) | copy-start | bytes 3145732
  334.4 207.6 %copy-start.40 = (f32[256]{0:T(256)}, f32[256]{0:T(256)S(1)}, u32[]{:S(2)}) copy-start(f32[256]{0:T(256)S(1)} %get-tuple-element.94) | copy-start | bytes 3076
  542.0 374.1 %copy-start.17 = (bf16[1,256,2048]{2,1,0:T(8,128)(2,1)S(1)}, bf16[1,256,2048]{2,1,0:T(8,128)(2,1)}, u32[]{:S(2)}) copy-start(bf16[1,256,2048]{2,1,0:T(8,128)(2,1)} %param.16) | copy-start | bytes 3145732
  986.2 19.1 copy-start.7
  986.2 19.1 copy-start.37
  986.2 19.1 copy-start.41
  986.2 2236.4 %reduce-scatter.12.cloned.1.call-start = ((), (), s32[]{:S(2)}) async-start(), calls=%async_computation.15 | async-start | bytes 17301504 | tf_op jit(solution)/shard_map/reduce_scatter | solution.py:261
  1005.3 16.8 copy-start.8
  1005.3 16.8 copy-start.43
  1023.3 9.1 copy-start.3
  1031.7 2551.0 %reduce-scatter.10.cloned.1.call-start = ((), (), s32[]{:S(2)}) async-start(), calls=%async_computation.14 | async-start | bytes 17301504 | tf_op jit(solution)/shard_map/reduce_scatter | solution.py:258
  1055.5 2887.3 %reduce-scatter.6.cloned.1.call-start = ((), (), s32[]{:S(2)}) async-start(), calls=%async_computation.12 | async-start | bytes 17301504 | tf_op jit(solution)/shard_map/reduce_scatter | solution.py:252
  1082.6 3220.4 %reduce-scatter.8.cloned.1.call-start = ((), (), s32[]{:S(2)}) async-start(), calls=%async_computation.13 | async-start | bytes 17301504 | tf_op jit(solution)/shard_map/reduce_scatter | solution.py:255
  1093.4 4615.1 %reduce-scatter.14.cloned.1.call-start = ((), (), s32[]{:S(2)}) async-start(), calls=%async_computation.16 | async-start | bytes 69206016 | tf_op jit(solution)/shard_map/reduce_scatter | solution.py:185
  1121.1 9.9 slice-start.2
  1133.6 45.2 copy-start.4
  1133.6 45.2 copy-start.42
  (32 other events, 110.7 us)
Sparse Core Ops, SparseCore 0:
  11.0 79.9 all-gather.11
  94.0 75.9 all-gather.7
  173.1 75.9 all-gather.9
  251.9 75.9 all-gather.13
  330.8 193.3 all-gather.17
  527.1 192.9 all-gather.15
  723.1 192.9 all-gather.19
  986.3 1876.8 all-reduce.8
  2866.1 356.4 reduce-scatter.11
  3225.3 357.2 reduce-scatter.9
  3585.5 357.3 reduce-scatter.5
  3945.6 357.3 reduce-scatter.7
  4305.9 1402.4 reduce-scatter.13
where the time goes:
time: 5720 us
  waiting for transfers between devices  5290 us (92%)
  matrix products  286 us (5%)
  blocking collectives  81.5 us (1%)
    unnamed x14, waiting for transfers between devices  1670 us
    reduce_scatter x1, waiting for transfers between devices, on_device(): lax.psum_scatter(outer_sum(middle, dy_rows), ('dp', 'fsdp'), scatter_dime...  1410 us
    reduce_scatter x1, waiting for transfers between devices, on_device(): lax.psum_scatter(outer_sum(act_one, grad_queries), ('dp', 'fsdp'), scatte...  360 us
    reduce_scatter x1, waiting for transfers between devices, on_device(): lax.psum_scatter(outer_sum(act_one, grad_keys), ('dp', 'fsdp'), scatter_d...  360 us
    reduce_scatter x1, waiting for transfers between devices, on_device(): lax.psum_scatter(outer_sum(act_one, grad_values), ('dp', 'fsdp'), scatter...  360 us
    reduce_scatter x1, waiting for transfers between devices, on_device(): lax.psum_scatter(outer_sum(attended, grad_branch), ('dp', 'fsdp'), scatte...  354 us
    all_gather x1, waiting for transfers between devices, on_device(): lax.all_gather(w_up, ('dp', 'fsdp'), axis=0, tiled=True)  189 us
    all_gather x1, waiting for transfers between devices, on_device(): lax.all_gather(w_down, ('dp', 'fsdp'), axis=0, tiled=True)  178 us
  transfers between devices with their start and end apart: 13, of which 13 were waited for; matrix products, arithmetic and copies ran while one was open for 4% of the time, Pallas kernels for 0%

commit v1 on v0

v1 whole, which is shorter than its diff:
```python
import jax
import jax.numpy as jnp
from jax import lax
from jax.sharding import PartitionSpec as P

HEAD_DIM = 64
AXES = ("dp", "fsdp")
QUAD = 4

epsilon = 1e-05
rope_base = 130000.0
bf16 = jnp.bfloat16
f32 = jnp.float32


def rope_tables(seq_len, head_dim):
    half_dim = head_dim // 2
    frequency = rope_base ** (-(jnp.arange(half_dim).astype(f32) * 2.0) / head_dim)
    angles = jnp.arange(seq_len).astype(f32)[:, None] * frequency[None, :]
    angles = jnp.concatenate([angles, angles], axis=1)
    return (jnp.cos(angles), jnp.sin(angles))


def rotate(tensor, cosine, sine):
    half_dim = tensor.shape[-1] // 2
    turned = jnp.concatenate([-tensor[..., half_dim:], tensor[..., :half_dim]], axis=-1)
    return tensor * cosine[:, None, :] + turned * sine[:, None, :]


def unrotate(grads, cosine, sine):
    half_dim = grads.shape[-1] // 2
    turned = grads * sine[:, None, :]
    return grads * cosine[:, None, :] + jnp.concatenate(
        [turned[..., half_dim:], -turned[..., :half_dim]], axis=-1
    )


def mm(left, right):
    return jnp.dot(left, right, preferred_element_type=f32)


def outer_sum(left, right):
    return lax.dot_general(left, right, (((0,), (0,)), ((), ())), preferred_element_type=f32)


def times_transposed(left, weight):
    return lax.dot_general(left, weight, (((1,), (1,)), ((), ())), preferred_element_type=f32)


def causal_mask(seq_len):
    return lax.broadcasted_iota(jnp.int32, (seq_len, seq_len), 1) <= lax.broadcasted_iota(
        jnp.int32, (seq_len, seq_len), 0
    )


def attend(queries, keys_rot, values):
    scale_factor = queries.shape[-1] ** (-0.5)
    scores = (
        jnp.einsum("bqhd,bkhd->bhqk", queries, keys_rot, preferred_element_type=f32) * scale_factor
    )
    scores = jnp.where(causal_mask(scores.shape[-1]), scores, -1e30)
    row_max = jnp.max(scores, axis=-1, keepdims=True)
    exp_scores = jnp.exp(scores - row_max)
    row_total = jnp.sum(exp_scores, axis=-1, keepdims=True)
    soft = (exp_scores / row_total).astype(bf16)
    mixed = jnp.einsum("bhqk,bkhd->bqhd", soft, values, preferred_element_type=f32)
    return (mixed, (row_max + jnp.log(row_total))[..., 0])


def attend_back(queries, keys_rot, values, grad_mixed, log_total):
    scale_factor = queries.shape[-1] ** (-0.5)
    scores = (
        jnp.einsum("bqhd,bkhd->bhqk", queries, keys_rot, preferred_element_type=f32) * scale_factor
    )
    soft = jnp.where(causal_mask(scores.shape[-1]), jnp.exp(scores - log_total[..., None]), 0.0)
    grad_soft = jnp.einsum("bqhd,bkhd->bhqk", grad_mixed, values, preferred_element_type=f32)
    grad_scores = (soft * (grad_soft - jnp.sum(soft * grad_soft, axis=-1, keepdims=True))).astype(
        bf16
    )
    grad_queries = (
        jnp.einsum("bhqk,bkhd->bqhd", grad_scores, keys_rot, preferred_element_type=f32)
        * scale_factor
    )
    grad_keys = (
        jnp.einsum("bhqk,bqhd->bkhd", grad_scores, queries, preferred_element_type=f32)
        * scale_factor
    )
    grad_values = jnp.einsum(
        "bhqk,bqhd->bkhd", soft.astype(bf16), grad_mixed, preferred_element_type=f32
    )
    return (grad_queries, grad_keys, grad_values)


class Plan:
    def __init__(self, outer, inner, rows):
        self.count = outer * inner
        self.inner = inner
        self.span = max(1, HEAD_DIM // rows)
        self.bit_a = self.span
        self.bit_b = 2 * self.span
        self.bit_core = inner
        flat = lax.axis_index("dp") * inner + lax.axis_index("fsdp")
        self.flat = flat
        self.core = (flat // inner) % 2
        self.quad = (flat // self.span) % QUAD
        self.me = self.core * QUAD + self.quad
        dims = []
        bit = outer * inner // 2
        while bit > inner:
            dims.append(bit)
            bit //= 2
        self.upper = dims
        mid = []
        bit = inner // 2
        while bit >= QUAD * self.span:
            mid.append(bit)
            bit //= 2
        self.mid = mid
        low = []
        bit = self.span // 2
        while bit >= 1:
            low.append(bit)
            bit //= 2
        self.low = low
        self.data_bits = low + mid + dims
        self.deltas = [
            c * self.bit_core + q * self.span for c in range(2) for q in range(QUAD)
        ]

    def send(self, array, bit):
        return lax.ppermute(array, AXES, [(r, r ^ bit) for r in range(self.count)])

    def mine(self, bit):
        return (self.flat // bit) % 2

    def column_dims(self):
        return (
            (2,) * len(self.upper) + (2,) + (2,) * len(self.mid) + (QUAD,) + (2,) * len(self.low)
        )

    def row_dims(self):
        return (2,) * (len(self.upper) + len(self.mid) + len(self.low))

    def axes(self, with_columns):
        skip_core = 1 if with_columns else 0
        skip_quad = skip_core + (1 if with_columns else 0)
        found = {}
        place = 0
        for bit in self.upper:
            found[bit] = place
            place += 1
        place += skip_core
        for bit in self.mid:
            found[bit] = place
            place += 1
        place += skip_quad - skip_core
        for bit in self.low:
            found[bit] = place
            place += 1
        return found

    def cut_columns(self, weight):
        rows, width = weight.shape
        chunk = width // (self.count // self.span)
        ahead = 2 ** len(self.upper)
        middle = 2 ** len(self.mid)
        parts = weight.reshape(rows, ahead, 2, middle, QUAD, chunk)
        return parts.transpose(2, 4, 0, 1, 3, 5).reshape(2 * QUAD, rows, width // (2 * QUAD))

    def join_columns(self, parts):
        eight, rows, narrow = parts.shape
        width = eight * narrow
        chunk = width // (self.count // self.span)
        ahead = 2 ** len(self.upper)
        middle = 2 ** len(self.mid)
        parts = parts.reshape(2, QUAD, rows, ahead, middle, chunk)
        return parts.transpose(2, 3, 0, 4, 1, 5).reshape(rows, width)

    def swap(self, parts):
        got = jnp.zeros_like(parts)
        for index, delta in enumerate(self.deltas):
            other = self.me ^ index
            block = lax.dynamic_index_in_dim(parts, other, 0, keepdims=True)
            if index:
                block = self.send(block, delta)
            got = lax.dynamic_update_slice_in_dim(got, block, other, 0)
        return got

    def gather(self, block, with_columns):
        held = {0: block}
        for bit in self.data_bits:
            for key in list(held):
                held[key ^ bit] = self.send(held[key], bit)
        found = self.axes(with_columns)
        if with_columns:
            dims = self.column_dims()
            piece = [1] * len(dims)
            piece[len(self.upper)] = 2
            piece[len(self.upper) + 1 + len(self.mid)] = QUAD
        else:
            dims = self.row_dims()
            piece = [1] * len(dims)
        tail = block.shape[-2:]
        whole = jnp.zeros(tuple(dims) + tail, block.dtype)
        for key, array in held.items():
            start = [0] * (len(dims) + 2)
            for bit, place in found.items():
                start[place] = self.mine(bit) ^ (1 if key & bit else 0)
            whole = lax.dynamic_update_slice(whole, array.reshape(tuple(piece) + tail), start)
        return whole.reshape(-1, tail[1])

    def scatter(self, total, rows, with_columns):
        dims = self.column_dims() if with_columns else self.row_dims()
        found = self.axes(with_columns)
        total = total.reshape(dims + (rows, total.shape[-1]))
        for bit in reversed(self.data_bits):
            place = found[bit]
            here = self.mine(bit)
            away = lax.dynamic_slice_in_dim(total, 1 - here, 1, place).astype(bf16)
            kept = lax.dynamic_slice_in_dim(total, here, 1, place)
            total = kept + self.send(away, bit).astype(f32)
        if with_columns:
            return total.reshape(2 * QUAD, rows, total.shape[-1])
        return total.reshape(rows, total.shape[-1])

    def share_tokens(self, block):
        half = block.shape[0] // 2
        from_a = self.send(block, self.bit_a)
        from_b = self.send(block, self.bit_b)
        first = self.send(from_a[:half], self.bit_b)
        second = self.send(from_b[half:], self.bit_a)
        four = jnp.concatenate([block, from_a, from_b, first, second], axis=0)
        return jnp.concatenate([four, self.send(four, self.bit_core)], axis=0)

    def sum_tokens(self, left, product):
        count = left.shape[0] // 2
        far = product(left[count:]).astype(bf16)
        four = product(left[:count]) + self.send(far, self.bit_core).astype(f32)
        size = count // 4
        half = size // 2
        own, for_a, for_b, for_ab = (four[i * size : (i + 1) * size] for i in range(4))
        first = self.send(for_ab[:half].astype(bf16), self.bit_b)
        second = self.send(for_ab[half:].astype(bf16), self.bit_a)
        for_a = jnp.concatenate([for_a[:half] + first.astype(f32), for_a[half:]]).astype(bf16)
        for_b = jnp.concatenate([for_b[:half], for_b[half:] + second.astype(f32)]).astype(bf16)
        return (
            own
            + self.send(for_a, self.bit_a).astype(f32)
            + self.send(for_b, self.bit_b).astype(f32)
        )

    def gather_gains(self, gains):
        bits = []
        bit = self.count // 2
        while bit >= 1:
            bits.append(bit)
            bit //= 2
        for bit in reversed(bits):
            other = self.send(gains, bit)
            low = self.mine(bit) == 0
            gains = jnp.concatenate(
                [jnp.where(low, gains, other), jnp.where(low, other, gains)], axis=1
            )
        return gains

    def scatter_gains(self, totals):
        bit = self.count // 2
        while bit >= 1:
            half = totals.shape[1] // 2
            low = self.mine(bit) == 0
            kept = jnp.where(low, totals[:, :half], totals[:, half:])
            away = jnp.where(low, totals[:, half:], totals[:, :half])
            totals = kept + self.send(away, bit)
            bit //= 2
        return totals


def on_device(
    tokens,
    labels,
    counts,
    grad_out,
    w_query,
    w_key,
    w_value,
    w_out,
    gain_attn,
    gain_mlp,
    w_gate,
    w_up,
    w_down,
):
    batch_size, seq_len, width = tokens.shape
    outer_count = lax.axis_size("dp")
    inner_count = lax.axis_size("fsdp")
    rows = w_query.shape[0]
    hidden_rows = w_down.shape[0]
    plan = Plan(outer_count, inner_count, rows)
    x_rows = tokens.reshape(-1, width).astype(f32)

    gains = plan.gather_gains(jnp.stack([gain_attn, gain_mlp])).astype(f32)
    gain_one, gain_two = gains[0:1], gains[1:2]

    inv_one = lax.rsqrt(jnp.mean(x_rows * x_rows, axis=-1, keepdims=True) + epsilon)
    act_one_own = (x_rows * inv_one * gain_one).astype(bf16)
    act_one = plan.share_tokens(act_one_own)

    qkv_parts = plan.swap(
        jnp.concatenate([plan.cut_columns(w) for w in (w_query, w_key, w_value)], axis=2)
    )
    w_qkv = plan.gather(qkv_parts, True)
    w_o = plan.gather(w_out, False)
    gu_parts = plan.swap(jnp.concatenate([plan.cut_columns(w) for w in (w_gate, w_up)], axis=2))
    w_gu = plan.gather(gu_parts, True)
    w_d = plan.gather(w_down, False)

    token_total = float(seq_len * batch_size * outer_count * inner_count)
    picked_counts = jnp.sum(
        jnp.where(labels[:, None] == jnp.arange(3)[None, :], counts[None, :], 0), axis=1
    ).astype(f32)
    factor = token_total / (3.0 * picked_counts)
    cotangent = (grad_out.astype(f32) * factor[:, None, None]).reshape(-1, width)
    dy = plan.share_tokens(cotangent.astype(bf16))

    narrow = w_qkv.shape[1] // 3
    hidden = w_gu.shape[1] // 2
    head_count = narrow // HEAD_DIM
    four_shape = (-1, seq_len, head_count, HEAD_DIM)
    cosine, sine = rope_tables(seq_len, HEAD_DIM)

    qkv = mm(act_one, w_qkv)
    q_rot = rotate(qkv[:, :narrow].reshape(four_shape), cosine, sine).astype(bf16)
    k_rot = rotate(qkv[:, narrow : 2 * narrow].reshape(four_shape), cosine, sine).astype(bf16)
    values = qkv[:, 2 * narrow :].astype(bf16).reshape(four_shape)
    mixed, log_total = attend(q_rot, k_rot, values)
    attended = mixed.reshape(-1, narrow).astype(bf16)

    resid = x_rows + plan.sum_tokens(attended, lambda part: mm(part, w_o))
    inv_two = lax.rsqrt(jnp.mean(resid * resid, axis=-1, keepdims=True) + epsilon)
    act_two = plan.share_tokens((resid * inv_two * gain_two).astype(bf16))

    gu = mm(act_two, w_gu)
    gate_pre, up_proj = gu[:, :hidden], gu[:, hidden:]
    sigmoid_gate = jax.nn.sigmoid(gate_pre)
    middle = (gate_pre * sigmoid_gate * up_proj).astype(bf16)

    grad_middle = times_transposed(dy, w_d)
    grad_gate_pre = (
        grad_middle * up_proj * sigmoid_gate * (1.0 + gate_pre * (1.0 - sigmoid_gate))
    ).astype(bf16)
    grad_up_proj = (grad_middle * gate_pre * sigmoid_gate).astype(bf16)
    grad_gu_cols = jnp.concatenate([grad_gate_pre, grad_up_proj], axis=1)

    added = plan.sum_tokens(grad_gu_cols, lambda part: times_transposed(part, w_gu))
    down_grad = plan.scatter(outer_sum(middle, dy), hidden_rows, False)
    gu_grad = plan.swap(plan.scatter(outer_sum(act_two, grad_gu_cols), rows, True).astype(bf16))
    gate_grad = plan.join_columns(gu_grad[:, :, :hidden]).astype(f32)
    up_grad = plan.join_columns(gu_grad[:, :, hidden:]).astype(f32)

    layer_out = (
        (resid + plan.sum_tokens(middle, lambda part: mm(part, w_d)))
        .astype(bf16)
        .reshape(tokens.shape)
    )

    grad_gain_two = jnp.sum(added * resid * inv_two, axis=0, keepdims=True)
    scaled_two = gain_two * added
    grad_resid = (
        cotangent
        + inv_two * scaled_two
        - resid * inv_two**3 * jnp.mean(scaled_two * resid, axis=-1, keepdims=True)
    )
    grad_branch = plan.share_tokens(grad_resid.astype(bf16))
    grad_attended = times_transposed(grad_branch, w_o).astype(bf16).reshape(four_shape)
    out_grad = plan.scatter(outer_sum(attended, grad_branch), rows, False)
    grad_q_rot, grad_k_rot, grad_v = attend_back(q_rot, k_rot, values, grad_attended, log_total)
    grad_qkv_cols = jnp.concatenate(
        [
            unrotate(grad_q_rot, cosine, sine).reshape(-1, narrow).astype(bf16),
            unrotate(grad_k_rot, cosine, sine).reshape(-1, narrow).astype(bf16),
            grad_v.reshape(-1, narrow).astype(bf16),
        ],
        axis=1,
    )
    qkv_grad = plan.swap(plan.scatter(outer_sum(act_one, grad_qkv_cols), rows, True).astype(bf16))
    query_grad, key_grad, value_grad = (
        plan.join_columns(qkv_grad[:, :, i * narrow : (i + 1) * narrow]).astype(f32)
        for i in range(3)
    )
    grad_act_one = plan.sum_tokens(grad_qkv_cols, lambda part: times_transposed(part, w_qkv))
    grad_gain_one = jnp.sum(grad_act_one * x_rows * inv_one, axis=0, keepdims=True)
    scaled_one = gain_one * grad_act_one
    grad_rows = (
        grad_resid
        + inv_one * scaled_one
        - x_rows * inv_one**3 * jnp.mean(scaled_one * x_rows, axis=-1, keepdims=True)
    )
    gain_grads = plan.scatter_gains(jnp.concatenate([grad_gain_one, grad_gain_two], axis=0))
    return (
        layer_out,
        grad_rows.reshape(tokens.shape),
        query_grad,
        key_grad,
        value_grad,
        out_grad,
        gain_grads[0],
        gain_grads[1],
        gate_grad,
        up_grad,
        down_grad,
    )


def solution(mesh):
    rows = P(AXES, None)
    vector = P(AXES)
    three = P(AXES, None, None)
    in_specs = (three, vector, P(), three, rows, rows, rows, rows, vector, vector, rows, rows, rows)
    out_specs = (three, three, rows, rows, rows, rows, vector, vector, rows, rows, rows)
    return jax.shard_map(
        on_device, mesh=mesh, in_specs=in_specs, out_specs=out_specs, check_vma=False
    )
```

time: 5720 us -> 1150 us (0.20)
  waiting for transfers between devices: 5290 us -> 567 us
  local copies, waits for them, and re-layouts: 18 us -> 193 us
  starting transfers between devices: 0.51 us -> 121 us
  blocking collectives: 81.5 us -> 0 us
  matrix products: 286 us -> 205 us
    reduce_scatter x5 -> x0, waiting for transfers between devices: 2840 us -> none  [the longest x1 1410 us: on_device(): lax.psum_scatter(outer_sum(middle, dy_rows), ('dp', 'fsdp'), scatter_dime...]
    unnamed x14 -> x0, waiting for transfers between devices: 1670 us -> none
    all_gather x7 -> x0, waiting for transfers between devices: 783 us -> none  [the longest x1 189 us: on_device(): lax.all_gather(w_up, ('dp', 'fsdp'), axis=0, tiled=True)]
    ppermute x0 -> x98, waiting for transfers between devices: none -> 567 us  [send(): return lax.ppermute(array, AXES, [(r, r ^ bit) for r in range(self.count)])]
    ppermute x0 -> x98, starting transfers between devices: none -> 121 us  [send(): return lax.ppermute(array, AXES, [(r, r ^ bit) for r in range(self.count)])]
    unnamed x2 -> x0, blocking collectives: 81.5 us -> none
    dot_general x6 -> x4, matrix products: 110 us -> 50.2 us  [outer_sum(): lax.dot_general(left, right, (((0,), (0,)), ((), ())), preferred_element_...]
  transfers between devices with their start and end apart: 13 -> 98, of which waited for: 13 -> 48; matrix products, arithmetic and copies ran while one was open for 4% -> 27% of each run, Pallas kernels for 0% -> 0%
where the time goes in v1:
time: 1150 us; the launch traced here: 1140 us
  waiting for transfers between devices  567 us (49%)
  matrix products  205 us (18%)
  local copies, waits for them, and re-layouts  193 us (17%)
  starting transfers between devices  121 us (11%)
  other arithmetic  53.3 us (5%)
    ppermute x98, waiting for transfers between devices, send(): return lax.ppermute(array, AXES, [(r, r ^ bit) for r in range(self.count)])  567 us
    ppermute x98, starting transfers between devices, send(): return lax.ppermute(array, AXES, [(r, r ^ bit) for r in range(self.count)])  121 us
    dot_general x6, matrix products, times_transposed(): lax.dot_general(left, weight, (((1,), (1,)), ((), ())), preferred_element...  72.3 us
    dot_general x6, matrix products, mm(): return jnp.dot(left, right, preferred_element_type=f32)  65.1 us
    dot_general x4, matrix products, outer_sum(): lax.dot_general(left, right, (((0,), (0,)), ((), ())), preferred_element_...  50.2 us
    unnamed x189, local copies, waits for them, and re-layouts  39.6 us
  transfers between devices with their start and end apart: 98, of which 48 were waited for; matrix products, arithmetic and copies ran while one was open for 27% of the time, Pallas kernels for 0%

profile of v1, /device:TPU:1, one launch (start us, length us, event | category | flops | bytes accessed | tf_op | source)
XLA Modules:
  0.0 1143.8 jit_solution(2777356955164633913)
XLA Ops:
  54.8 8.6 collective-permute-done.7
  97.0 30.4 %collective-permute-done.17 = bf16[8,64,768]{2,1,0:T(8,128)(2,1)S(1)} collective-permute-done((bf16[8,64,768]{2,1,0:T(8,128)(2,1)S(1)}, bf16[8,64,768]{2,1,0:T(8,128)(2,1)S(1)}, u32[]{:S(2)}, u32[]{:S(2)}) %collective-permute-start.17) | collective-permute-done | bytes 786464 | tf_op jit(solution)/shard_map/ppermute | solution.py:131
  130.1 15.5 %collective-permute-done.19 = bf16[8,64,768]{2,1,0:T(8,128)(2,1)S(1)} collective-permute-done((bf16[8,64,768]{2,1,0:T(8,128)(2,1)S(1)}, bf16[8,64,768]{2,1,0:T(8,128)(2,1)S(1)}, u32[]{:S(2)}, u32[]{:S(2)}) %collective-permute-start.19) | collective-permute-done | bytes 786464 | tf_op jit(solution)/shard_map/ppermute | solution.py:131
  149.4 16.7 %fusion.99 = f32[2048,768]{1,0:T(8,128)S(1)} fusion(bf16[2048,2048]{1,0:T(8,128)(2,1)S(1)} %constant_dynamic-update-slice_fusion.5, bf16[2048,768]{1,0:T(8,128)(2,1)S(1)} %bitcast.228), kind=kOutput, calls=%fused_computation.355 | convolution fusion | flops 6442450944 | bytes 17825792 | tf_op jit(solution)/shard_map/dot_general | solution.py:39
  238.7 14.6 %collective-permute-done.26 = bf16[128,2048]{1,0:T(8,128)(2,1)S(1)} collective-permute-done((bf16[128,2048]{1,0:T(8,128)(2,1)S(1)}, bf16[128,2048]{1,0:T(8,128)(2,1)S(1)}, u32[]{:S(2)}, u32[]{:S(2)}) %collective-permute-start.26) | collective-permute-done | bytes 524320 | tf_op jit(solution)/shard_map/ppermute | solution.py:131
  255.4 9.7 collective-permute-done.35
  276.2 26.4 %collective-permute-done.39 = bf16[1,64,2048]{2,1,0:T(8,128)(2,1)S(1)} collective-permute-done((bf16[1,64,2048]{2,1,0:T(8,128)(2,1)S(1)}, bf16[1,64,2048]{2,1,0:T(8,128)(2,1)S(1)}, u32[]{:S(2)}, u32[]{:S(2)}) %collective-permute-start.39) | collective-permute-done | bytes 262176 | tf_op jit(solution)/shard_map/ppermute | solution.py:131
  312.9 24.2 %collective-permute-done.53 = bf16[128,2048]{1,0:T(8,128)(2,1)S(1)} collective-permute-done((bf16[128,2048]{1,0:T(8,128)(2,1)S(1)}, bf16[128,2048]{1,0:T(8,128)(2,1)S(1)}, u32[]{:S(2)}, u32[]{:S(2)}) %collective-permute-start.53) | collective-permute-done | bytes 524320 | tf_op jit(solution)/shard_map/ppermute | solution.py:131
  346.2 26.7 %collective-permute-done.29 = bf16[256,2048]{1,0:T(8,128)(2,1)S(1)} collective-permute-done((bf16[256,2048]{1,0:T(8,128)(2,1)S(1)}, bf16[256,2048]{1,0:T(8,128)(2,1)S(1)}, u32[]{:S(2)}, u32[]{:S(2)}) %collective-permute-start.29) | collective-permute-done | bytes 1048608 | tf_op jit(solution)/shard_map/ppermute | solution.py:131
  377.6 38.1 %collective-permute-done.30 = bf16[128,2048]{1,0:T(8,128)(2,1)S(1)} collective-permute-done((bf16[128,2048]{1,0:T(8,128)(2,1)S(1)}, bf16[128,2048]{1,0:T(8,128)(2,1)S(1)}, u32[]{:S(2)}, u32[]{:S(2)}) %collective-permute-start.30) | collective-permute-done | bytes 524320 | tf_op jit(solution)/shard_map/ppermute | solution.py:131
  426.2 18.8 %collective-permute-done.44 = bf16[256,2048]{1,0:T(8,128)(2,1)} collective-permute-done((bf16[256,2048]{1,0:T(8,128)(2,1)S(1)}, bf16[256,2048]{1,0:T(8,128)(2,1)}, u32[]{:S(2)}, u32[]{:S(2)}) %collective-permute-start.44) | collective-permute-done | bytes 1048608 | tf_op jit(solution)/shard_map/ppermute | solution.py:131
  452.3 59.9 %collective-permute-done.45 = bf16[256,2048]{1,0:T(8,128)(2,1)S(1)} collective-permute-done((bf16[256,2048]{1,0:T(8,128)(2,1)}, bf16[256,2048]{1,0:T(8,128)(2,1)S(1)}, u32[]{:S(2)}, u32[]{:S(2)}) %collective-permute-start.45) | collective-permute-done | bytes 1048608 | tf_op jit(solution)/shard_map/ppermute | solution.py:131
  517.2 40.0 %collective-permute-done.42 = bf16[8,64,2048]{2,1,0:T(8,128)(2,1)S(1)} collective-permute-done((bf16[8,64,2048]{2,1,0:T(8,128)(2,1)}, bf16[8,64,2048]{2,1,0:T(8,128)(2,1)S(1)}, u32[]{:S(2)}, u32[]{:S(2)}) %collective-permute-start.42) | collective-permute-done | bytes 2097184 | tf_op jit(solution)/shard_map/ppermute | solution.py:131
  563.1 7.8 constant_dynamic-update-slice_fusion.19
  570.8 22.0 %fusion.100 = f32[2048,2048]{0,1:T(8,128)} fusion(bf16[2048,2048]{1,0:T(8,128)(2,1)} %constant_dynamic-update-slice_fusion.19, bf16[2048,2048]{1,0:T(8,128)(2,1)S(1)} %bitcast.198), kind=kOutput, calls=%fused_computation.356 | convolution fusion | flops 17179869184 | bytes 33554432 | tf_op jit(solution)/shard_map/dot_general | solution.py:39
  592.8 22.4 %multiply_convert_fusion.1 = (bf16[2048,1024]{0,1:T(8,128)(2,1)}, bf16[2048,1024]{0,1:T(8,128)(2,1)}, bf16[2048,1024]{0,1:T(8,128)(2,1)S(1)}) fusion(f32[2048,2048]{0,1:T(8,128)} %fusion.100, bf16[2048,2048]{1,0:T(8,128)(2,1)} %copy-done.55, bf16[1024,2048]{1,0:T(8,128)(2,1)} %bitcast.31), kind=kOutput, calls=%fused_computation.15 | convolution fusion | flops 8623489024 | bytes 41943040 | tf_op jit(solution)/shard_map/dot_general | solution.py:47
  615.3 16.0 %fusion.18 = bf16[1024,2048]{1,0:T(8,128)(2,1)} fusion(bf16[2048,2048]{1,0:T(8,128)(2,1)} %bitcast.199, bf16[2048,1024]{0,1:T(8,128)(2,1)} %get-tuple-element.27, bf16[2048,1024]{0,1:T(8,128)(2,1)} %get-tuple-element.26), kind=kOutput, calls=%fused_computation.49 | convolution fusion | flops 8600420352 | bytes 20971520 | tf_op jit(solution)/shard_map/dot_general | solution.py:47
  632.0 8.3 convolution_convert_fusion.2
  640.4 24.3 %fusion = f32[2048,2048]{1,0:T(8,128)S(1)} fusion(bf16[2048,2048]{1,0:T(8,128)(2,1)} %constant_dynamic-update-slice_fusion.19, bf16[2048,1024]{0,1:T(8,128)(2,1)} %get-tuple-element.26, bf16[2048,1024]{0,1:T(8,128)(2,1)} %get-tuple-element.27), kind=kOutput, calls=%fused_computation.5 | convolution fusion | flops 17196646400 | bytes 33554432 | tf_op jit(solution)/shard_map/dot_general | solution.py:43
  672.4 16.4 %fusion.96 = (bf16[1024,2048]{1,0:T(8,128)(2,1)}, f32[1024,2048]{1,0:T(8,128)}) fusion(bf16[1024,2048]{1,0:T(8,128)(2,1)} %collective-permute-done.56, bf16[2048,2048]{1,0:T(8,128)(2,1)} %bitcast.200, bf16[2048,1024]{0,1:T(8,128)(2,1)} %get-tuple-element.27, bf16[2048,1024]{0,1:T(8,128)(2,1)} %get-tuple-element.26), kind=kOutput, calls=%fused_computation.352 | convolution fusion | flops 8604614656 | bytes 33554432 | tf_op jit(solution)/shard_map/dot_general | solution.py:47
  693.8 11.2 fusion.97
  712.0 8.8 collective-permute-done.47
  724.0 12.9 %fusion.102 = f32[1024,2048]{1,0:T(8,128)S(1)} fusion(bf16[2048,1024]{0,1:T(8,128)(2,1)} %copy-done.69, bf16[2048,2048]{1,0:T(8,128)(2,1)} %copy-done.55), kind=kOutput, calls=%fused_computation.358 | convolution fusion | flops 8589934592 | bytes 20971520 | tf_op jit(solution)/shard_map/dot_general | solution.py:43
  743.5 22.2 %collective-permute-done.50 = bf16[256,2048]{1,0:T(8,128)(2,1)S(1)} collective-permute-done((bf16[256,2048]{1,0:T(8,128)(2,1)S(1)}, bf16[256,2048]{1,0:T(8,128)(2,1)S(1)}, u32[]{:S(2)}, u32[]{:S(2)}) %collective-permute-start.50) | collective-permute-done | bytes 1048608 | tf_op jit(solution)/shard_map/ppermute | solution.py:131
  780.5 14.8 %collective-permute-done.61 = bf16[256,2048]{1,0:T(8,128)(2,1)} collective-permute-done((bf16[256,2048]{1,0:T(8,128)(2,1)S(1)}, bf16[256,2048]{1,0:T(8,128)(2,1)}, u32[]{:S(2)}, u32[]{:S(2)}) %collective-permute-start.61) | collective-permute-done | bytes 1048608 | tf_op jit(solution)/shard_map/ppermute | solution.py:131
  797.4 12.6 %collective-permute-done.62 = bf16[256,2048]{1,0:T(8,128)(2,1)} collective-permute-done((bf16[256,2048]{1,0:T(8,128)(2,1)S(1)}, bf16[256,2048]{1,0:T(8,128)(2,1)}, u32[]{:S(2)}, u32[]{:S(2)}) %collective-permute-start.62) | collective-permute-done | bytes 1048608 | tf_op jit(solution)/shard_map/ppermute | solution.py:131
  817.7 32.4 %collective-permute-done.63 = bf16[128,2048]{1,0:T(8,128)(2,1)S(1)} collective-permute-done((bf16[128,2048]{1,0:T(8,128)(2,1)S(1)}, bf16[128,2048]{1,0:T(8,128)(2,1)S(1)}, u32[]{:S(2)}, u32[]{:S(2)}) %collective-permute-start.63) | collective-permute-done | bytes 524320 | tf_op jit(solution)/shard_map/ppermute | solution.py:131
  862.0 31.0 %collective-permute-done.88 = bf16[1,2,1,4,64,2048]{5,4,3,2,1,0:T(8,128)(2,1)S(1)} collective-permute-done((bf16[1,2,1,4,64,2048]{5,4,3,2,1,0:T(8,128)(2,1)S(1)}, bf16[1,2,1,4,64,2048]{5,4,3,2,1,0:T(8,128)(2,1)S(1)}, u32[]{:S(2)}, u32[]{:S(2)}) %collective-permute-start.88) | collective-permute-done | bytes 2097184 | tf_op jit(solution)/shard_map/ppermute | solution.py:131
  895.4 20.1 %collective-permute-done.97 = bf16[1,1,256,2048]{3,2,1,0:T(8,128)(2,1)S(1)} collective-permute-done((bf16[1,1,256,2048]{3,2,1,0:T(8,128)(2,1)S(1)}, bf16[1,1,256,2048]{3,2,1,0:T(8,128)(2,1)S(1)}, u32[]{:S(2)}, u32[]{:S(2)}) %collective-permute-start.97) | collective-permute-done | bytes 1048608 | tf_op jit(solution)/shard_map/ppermute | solution.py:131
  980.9 7.3 fusion.101
  1038.2 32.9 %collective-permute-done.72 = bf16[1,2,1,4,64,768]{5,4,3,2,1,0:T(8,128)(2,1)S(1)} collective-permute-done((bf16[1,2,1,4,64,768]{5,4,3,2,1,0:T(8,128)(2,1)S(1)}, bf16[1,2,1,4,64,768]{5,4,3,2,1,0:T(8,128)(2,1)S(1)}, u32[]{:S(2)}, u32[]{:S(2)}) %collective-permute-start.72) | collective-permute-done | bytes 786464 | tf_op jit(solution)/shard_map/ppermute | solution.py:131
  1079.9 18.0 %collective-permute-done.73 = bf16[1,64,768]{2,1,0:T(8,128)(2,1)S(1)} collective-permute-done((bf16[1,64,768]{2,1,0:T(8,128)(2,1)S(1)}, bf16[1,64,768]{2,1,0:T(8,128)(2,1)S(1)}, u32[]{:S(2)}, u32[]{:S(2)}) %collective-permute-start.73) | collective-permute-done | bytes 98336 | tf_op jit(solution)/shard_map/ppermute | solution.py:131
  (584 shorter events, 468.5 us)
Async XLA Ops:
  24.6 70.8 %collective-permute-start.20 = (bf16[64,2048]{1,0:T(8,128)(2,1)}, bf16[64,2048]{1,0:T(8,128)(2,1)}, u32[]{:S(2)}, u32[]{:S(2)}) collective-permute-start(bf16[64,2048]{1,0:T(8,128)(2,1)} %param.20), channel_id=1, source_target_pairs={{0,4},{1,5},{2,6},{3,7},{4,0},{5,1},{6,2},{7,3},{8,12},{9,13},{10,... | collective-permute-start | bytes 786440 | tf_op jit(solution)/shard_map/ppermute | solution.py:131
  27.0 102.0 %collective-permute-start.21 = (bf16[64,2048]{1,0:T(8,128)(2,1)}, bf16[64,2048]{1,0:T(8,128)(2,1)}, u32[]{:S(2)}, u32[]{:S(2)}) collective-permute-start(bf16[64,2048]{1,0:T(8,128)(2,1)} %param.20), channel_id=1, source_target_pairs={{0,16},{1,17},{2,18},{3,19},{4,20},{5,21},{6,22},{7,23},{8,24},{9,... | collective-permute-start | bytes 786440 | tf_op jit(solution)/shard_map/ppermute | solution.py:131
  65.2 80.5 %collective-permute-start.9 = (bf16[1024,2048]{1,0:T(8,128)(2,1)}, bf16[1024,2048]{1,0:T(8,128)(2,1)}, u32[]{:S(2)}, u32[]{:S(2)}) collective-permute-start(bf16[1024,2048]{1,0:T(8,128)(2,1)} %get-tuple-element.131), channel_id=1, source_target_pairs={{0,8},{1,9},{2,10},{3,11},{4,12},{5,13},{6,14},{7,15},{8,0},{9,1},... | collective-permute-start | bytes 12582920 | tf_op jit(solution)/shard_map/ppermute | solution.py:131
  217.9 86.7 %collective-permute-start.51 = (bf16[256,2048]{1,0:T(8,128)(2,1)S(1)}, bf16[256,2048]{1,0:T(8,128)(2,1)S(1)}, u32[]{:S(2)}, u32[]{:S(2)}) collective-permute-start(bf16[256,2048]{1,0:T(8,128)(2,1)S(1)} %get-tuple-element.19), channel_id=1, source_target_pairs={{0,1},{1,0},{2,3},{3,2},{4,5},{5,4},{6,7},{7,6},{8,9},{9,8},{10,11... | collective-permute-start | bytes 3145736 | tf_op jit(solution)/shard_map/ppermute | solution.py:131
  225.4 80.6 %collective-permute-start.52 = (bf16[256,2048]{1,0:T(8,128)(2,1)S(1)}, bf16[256,2048]{1,0:T(8,128)(2,1)S(1)}, u32[]{:S(2)}, u32[]{:S(2)}) collective-permute-start(bf16[256,2048]{1,0:T(8,128)(2,1)S(1)} %get-tuple-element.19), channel_id=1, source_target_pairs={{0,2},{1,3},{2,0},{3,1},{4,6},{5,7},{6,4},{7,5},{8,10},{9,11},{10,... | collective-permute-start | bytes 3145736 | tf_op jit(solution)/shard_map/ppermute | solution.py:131
  267.4 40.2 %collective-permute-start.27 = (bf16[256,2048]{1,0:T(8,128)(2,1)S(1)}, bf16[256,2048]{1,0:T(8,128)(2,1)S(1)}, u32[]{:S(2)}, u32[]{:S(2)}) collective-permute-start(bf16[256,2048]{1,0:T(8,128)(2,1)S(1)} %pad_maximum_fusion.3), channel_id=1, source_target_pairs={{0,2},{1,3},{2,0},{3,1},{4,6},{5,7},{6,4},{7,5},{8,10},{9,11},{10,... | collective-permute-start | bytes 3145736 | tf_op jit(solution)/shard_map/ppermute | solution.py:131
  268.4 39.2 %collective-permute-start.25 = (bf16[256,2048]{1,0:T(8,128)(2,1)S(1)}, bf16[256,2048]{1,0:T(8,128)(2,1)S(1)}, u32[]{:S(2)}, u32[]{:S(2)}) collective-permute-start(bf16[256,2048]{1,0:T(8,128)(2,1)S(1)} %pad_maximum_fusion.2), channel_id=1, source_target_pairs={{0,1},{1,0},{2,3},{3,2},{4,5},{5,4},{6,7},{7,6},{8,9},{9,8},{10,11... | collective-permute-start | bytes 3145736 | tf_op jit(solution)/shard_map/ppermute | solution.py:131
  302.6 118.7 %collective-permute-start.43 = (bf16[256,2048]{1,0:T(8,128)(2,1)S(1)}, bf16[256,2048]{1,0:T(8,128)(2,1)S(1)}, u32[]{:S(2)}, u32[]{:S(2)}) collective-permute-start(bf16[256,2048]{1,0:T(8,128)(2,1)S(1)} %copy-done.35), channel_id=1, source_target_pairs={{0,4},{1,5},{2,6},{3,7},{4,0},{5,1},{6,2},{7,3},{8,12},{9,13},{10,... | collective-permute-start | bytes 3145736 | tf_op jit(solution)/shard_map/ppermute | solution.py:131
  310.2 62.7 %collective-permute-start.29 = (bf16[256,2048]{1,0:T(8,128)(2,1)S(1)}, bf16[256,2048]{1,0:T(8,128)(2,1)S(1)}, u32[]{:S(2)}, u32[]{:S(2)}) collective-permute-start(bf16[256,2048]{1,0:T(8,128)(2,1)S(1)} %get-tuple-element.21), channel_id=1, source_target_pairs={{0,2},{1,3},{2,0},{3,1},{4,6},{5,7},{6,4},{7,5},{8,10},{9,11},{10,... | collective-permute-start | bytes 3145736 | tf_op jit(solution)/shard_map/ppermute | solution.py:131
  337.1 109.1 %collective-permute-start.40 = (bf16[8,64,2048]{2,1,0:T(8,128)(2,1)S(1)}, bf16[8,64,2048]{2,1,0:T(8,128)(2,1)}, u32[]{:S(2)}, u32[]{:S(2)}) collective-permute-start(bf16[8,64,2048]{2,1,0:T(8,128)(2,1)S(1)} %constant_dynamic-update-slice_fusion.70), channel_id=1, source_target_pairs={{0,4},{1,5},{2,6},{3,7},{4,0},{5,1},{6,2},{7,3},{8,12},{9,13},{10,... | collective-permute-start | bytes 6291464 | tf_op jit(solution)/shard_map/ppermute | solution.py:131
  342.0 215.5 %collective-permute-start.55 = (bf16[1024,2048]{1,0:T(8,128)(2,1)}, bf16[1024,2048]{1,0:T(8,128)(2,1)}, u32[]{:S(2)}, u32[]{:S(2)}) collective-permute-start(bf16[1024,2048]{1,0:T(8,128)(2,1)} %get-tuple-element.123), channel_id=1, source_target_pairs={{0,8},{1,9},{2,10},{3,11},{4,12},{5,13},{6,14},{7,15},{8,0},{9,1},... | collective-permute-start | bytes 12582920 | tf_op jit(solution)/shard_map/ppermute | solution.py:131
  345.8 70.0 %collective-permute-start.30 = (bf16[128,2048]{1,0:T(8,128)(2,1)S(1)}, bf16[128,2048]{1,0:T(8,128)(2,1)S(1)}, u32[]{:S(2)}, u32[]{:S(2)}) collective-permute-start(bf16[128,2048]{1,0:T(8,128)(2,1)S(1)} %slice.395), channel_id=1, source_target_pairs={{0,2},{1,3},{2,0},{3,1},{4,6},{5,7},{6,4},{7,5},{8,10},{9,11},{10,... | collective-permute-start | bytes 1572872 | tf_op jit(solution)/shard_map/ppermute | solution.py:131
  373.0 43.9 %collective-permute-start.31 = (bf16[128,2048]{1,0:T(8,128)(2,1)S(1)}, bf16[128,2048]{1,0:T(8,128)(2,1)S(1)}, u32[]{:S(2)}, u32[]{:S(2)}) collective-permute-start(bf16[128,2048]{1,0:T(8,128)(2,1)S(1)} %slice.396), channel_id=1, source_target_pairs={{0,1},{1,0},{2,3},{3,2},{4,5},{5,4},{6,7},{7,6},{8,9},{9,8},{10,11... | collective-permute-start | bytes 1572872 | tf_op jit(solution)/shard_map/ppermute | solution.py:131
  418.0 145.1 %collective-permute-start.32 = (bf16[1024,2048]{1,0:T(8,128)(2,1)}, bf16[1024,2048]{1,0:T(8,128)(2,1)}, u32[]{:S(2)}, u32[]{:S(2)}) collective-permute-start(bf16[1024,2048]{1,0:T(8,128)(2,1)} %get-tuple-element.127), channel_id=1, source_target_pairs={{0,8},{1,9},{2,10},{3,11},{4,12},{5,13},{6,14},{7,15},{8,0},{9,1},... | collective-permute-start | bytes 12582920 | tf_op jit(solution)/shard_map/ppermute | solution.py:131
  422.3 92.9 %collective-permute-start.41 = (bf16[8,64,2048]{2,1,0:T(8,128)(2,1)S(1)}, bf16[8,64,2048]{2,1,0:T(8,128)(2,1)}, u32[]{:S(2)}, u32[]{:S(2)}) collective-permute-start(bf16[8,64,2048]{2,1,0:T(8,128)(2,1)S(1)} %constant_dynamic-update-slice_fusion.70), channel_id=1, source_target_pairs={{0,16},{1,17},{2,18},{3,19},{4,20},{5,21},{6,22},{7,23},{8,24},{9,... | collective-permute-start | bytes 6291464 | tf_op jit(solution)/shard_map/ppermute | solution.py:131
  445.0 67.3 %collective-permute-start.45 = (bf16[256,2048]{1,0:T(8,128)(2,1)}, bf16[256,2048]{1,0:T(8,128)(2,1)S(1)}, u32[]{:S(2)}, u32[]{:S(2)}) collective-permute-start(bf16[256,2048]{1,0:T(8,128)(2,1)} %copy-done.36), channel_id=1, source_target_pairs={{0,16},{1,17},{2,18},{3,19},{4,20},{5,21},{6,22},{7,23},{8,24},{9,... | collective-permute-start | bytes 3145736 | tf_op jit(solution)/shard_map/ppermute | solution.py:131
  446.2 111.0 %collective-permute-start.42 = (bf16[8,64,2048]{2,1,0:T(8,128)(2,1)}, bf16[8,64,2048]{2,1,0:T(8,128)(2,1)S(1)}, u32[]{:S(2)}, u32[]{:S(2)}) collective-permute-start(bf16[8,64,2048]{2,1,0:T(8,128)(2,1)} %collective-permute-done.40), channel_id=1, source_target_pairs={{0,16},{1,17},{2,18},{3,19},{4,20},{5,21},{6,22},{7,23},{8,24},{9,... | collective-permute-start | bytes 6291464 | tf_op jit(solution)/shard_map/ppermute | solution.py:131
  631.2 41.1 %collective-permute-start.56 = (bf16[1024,2048]{1,0:T(8,128)(2,1)}, bf16[1024,2048]{1,0:T(8,128)(2,1)}, u32[]{:S(2)}, u32[]{:S(2)}) collective-permute-start(bf16[1024,2048]{1,0:T(8,128)(2,1)} %fusion.18), channel_id=1, source_target_pairs={{0,8},{1,9},{2,10},{3,11},{4,12},{5,13},{6,14},{7,15},{8,0},{9,1},... | collective-permute-start | bytes 12582920 | tf_op jit(solution)/shard_map/ppermute | solution.py:131
  640.3 53.5 %collective-permute-start.46 = (bf16[1024,2048]{1,0:T(8,128)(2,1)}, bf16[1024,2048]{1,0:T(8,128)(2,1)}, u32[]{:S(2)}, u32[]{:S(2)}) collective-permute-start(bf16[1024,2048]{1,0:T(8,128)(2,1)} %convolution_convert_fusion.2), channel_id=1, source_target_pairs={{0,8},{1,9},{2,10},{3,11},{4,12},{5,13},{6,14},{7,15},{8,0},{9,1},... | collective-permute-start | bytes 12582920 | tf_op jit(solution)/shard_map/ppermute | solution.py:131
  671.1 103.0 %collective-permute-start.87 = (bf16[1,2,2,4,64,2048]{5,4,3,2,1,0:T(8,128)(2,1)S(1)}, bf16[1,2,2,4,64,2048]{5,4,3,2,1,0:T(8,128)(2,1)}, u32[]{:S(2)}, u32[]{:S(2)}) collective-permute-start(bf16[1,2,2,4,64,2048]{5,4,3,2,1,0:T(8,128)(2,1)S(1)} %dynamic-slice_convert_fusion), channel_id=1, source_target_pairs={{0,16},{1,17},{2,18},{3,19},{4,20},{5,21},{6,22},{7,23},{8,24},{9,... | collective-permute-start | bytes 12582920 | tf_op jit(solution)/shard_map/ppermute | solution.py:131
  721.3 44.5 %collective-permute-start.50 = (bf16[256,2048]{1,0:T(8,128)(2,1)S(1)}, bf16[256,2048]{1,0:T(8,128)(2,1)S(1)}, u32[]{:S(2)}, u32[]{:S(2)}) collective-permute-start(bf16[256,2048]{1,0:T(8,128)(2,1)S(1)} %pad_maximum_fusion.5), channel_id=1, source_target_pairs={{0,2},{1,3},{2,0},{3,1},{4,6},{5,7},{6,4},{7,5},{8,10},{9,11},{10,... | collective-permute-start | bytes 3145736 | tf_op jit(solution)/shard_map/ppermute | solution.py:131
  723.5 42.3 %collective-permute-start.48 = (bf16[256,2048]{1,0:T(8,128)(2,1)}, bf16[256,2048]{1,0:T(8,128)(2,1)S(1)}, u32[]{:S(2)}, u32[]{:S(2)}) collective-permute-start(bf16[256,2048]{1,0:T(8,128)(2,1)} %pad_maximum_fusion.4), channel_id=1, source_target_pairs={{0,1},{1,0},{2,3},{3,2},{4,5},{5,4},{6,7},{7,6},{8,9},{9,8},{10,11... | collective-permute-start | bytes 3145736 | tf_op jit(solution)/shard_map/ppermute | solution.py:131
  743.3 114.1 %collective-permute-start.96 = (bf16[1,2,256,2048]{3,2,1,0:T(8,128)(2,1)}, bf16[1,2,256,2048]{3,2,1,0:T(8,128)(2,1)}, u32[]{:S(2)}, u32[]{:S(2)}) collective-permute-start(bf16[1,2,256,2048]{3,2,1,0:T(8,128)(2,1)} %dynamic-slice_convert_fusion.1), channel_id=1, source_target_pairs={{0,16},{1,17},{2,18},{3,19},{4,20},{5,21},{6,22},{7,23},{8,24},{9,... | collective-permute-start | bytes 6291464 | tf_op jit(solution)/shard_map/ppermute | solution.py:131
  780.3 112.7 %collective-permute-start.88 = (bf16[1,2,1,4,64,2048]{5,4,3,2,1,0:T(8,128)(2,1)S(1)}, bf16[1,2,1,4,64,2048]{5,4,3,2,1,0:T(8,128)(2,1)S(1)}, u32[]{:S(2)}, u32[]{:S(2)}) collective-permute-start(bf16[1,2,1,4,64,2048]{5,4,3,2,1,0:T(8,128)(2,1)S(1)} %dynamic-slice_convert_fusion.2), channel_id=1, source_target_pairs={{0,4},{1,5},{2,6},{3,7},{4,0},{5,1},{6,2},{7,3},{8,12},{9,13},{10,... | collective-permute-start | bytes 6291464 | tf_op jit(solution)/shard_map/ppermute | solution.py:131
  796.5 53.5 %collective-permute-start.63 = (bf16[128,2048]{1,0:T(8,128)(2,1)S(1)}, bf16[128,2048]{1,0:T(8,128)(2,1)S(1)}, u32[]{:S(2)}, u32[]{:S(2)}) collective-permute-start(bf16[128,2048]{1,0:T(8,128)(2,1)S(1)} %slice.421), channel_id=1, source_target_pairs={{0,2},{1,3},{2,0},{3,1},{4,6},{5,7},{6,4},{7,5},{8,10},{9,11},{10,... | collective-permute-start | bytes 1572872 | tf_op jit(solution)/shard_map/ppermute | solution.py:131
  811.0 39.9 %collective-permute-start.64 = (bf16[128,2048]{1,0:T(8,128)(2,1)S(1)}, bf16[128,2048]{1,0:T(8,128)(2,1)S(1)}, u32[]{:S(2)}, u32[]{:S(2)}) collective-permute-start(bf16[128,2048]{1,0:T(8,128)(2,1)S(1)} %slice.422), channel_id=1, source_target_pairs={{0,1},{1,0},{2,3},{3,2},{4,5},{5,4},{6,7},{7,6},{8,9},{9,8},{10,11... | collective-permute-start | bytes 1572872 | tf_op jit(solution)/shard_map/ppermute | solution.py:131
  851.8 84.1 %collective-permute-start.65 = (bf16[1024,2048]{1,0:T(8,128)(2,1)}, bf16[1024,2048]{1,0:T(8,128)(2,1)S(1)}, u32[]{:S(2)}, u32[]{:S(2)}) collective-permute-start(bf16[1024,2048]{1,0:T(8,128)(2,1)} %get-tuple-element.119), channel_id=1, source_target_pairs={{0,8},{1,9},{2,10},{3,11},{4,12},{5,13},{6,14},{7,15},{8,0},{9,1},... | collective-permute-start | bytes 12582920 | tf_op jit(solution)/shard_map/ppermute | solution.py:131
  860.0 55.4 %collective-permute-start.97 = (bf16[1,1,256,2048]{3,2,1,0:T(8,128)(2,1)S(1)}, bf16[1,1,256,2048]{3,2,1,0:T(8,128)(2,1)S(1)}, u32[]{:S(2)}, u32[]{:S(2)}) collective-permute-start(bf16[1,1,256,2048]{3,2,1,0:T(8,128)(2,1)S(1)} %dynamic-slice_convert_fusion.4), channel_id=1, source_target_pairs={{0,4},{1,5},{2,6},{3,7},{4,0},{5,1},{6,2},{7,3},{8,12},{9,13},{10,... | collective-permute-start | bytes 3145736 | tf_op jit(solution)/shard_map/ppermute | solution.py:131
  930.7 59.3 %collective-permute-start.95 = (bf16[1,64,2048]{2,1,0:T(8,128)(2,1)S(1)}, bf16[1,64,2048]{2,1,0:T(8,128)(2,1)}, u32[]{:S(2)}, u32[]{:S(2)}) collective-permute-start(bf16[1,64,2048]{2,1,0:T(8,128)(2,1)S(1)} %get-tuple-element.57), channel_id=1, source_target_pairs={{0,11},{1,10},{2,9},{3,8},{4,15},{5,14},{6,13},{7,12},{8,3},{9,2},... | collective-permute-start | bytes 786440 | tf_op jit(solution)/shard_map/ppermute | solution.py:131
  980.9 48.1 %collective-permute-start.66 = (bf16[1024,2048]{1,0:T(8,128)(2,1)}, bf16[1024,2048]{1,0:T(8,128)(2,1)}, u32[]{:S(2)}, u32[]{:S(2)}) collective-permute-start(bf16[1024,2048]{1,0:T(8,128)(2,1)} %convolution_convert_fusion.1), channel_id=1, source_target_pairs={{0,8},{1,9},{2,10},{3,11},{4,12},{5,13},{6,14},{7,15},{8,0},{9,1},... | collective-permute-start | bytes 12582920 | tf_op jit(solution)/shard_map/ppermute | solution.py:131
  1028.5 42.7 %collective-permute-start.72 = (bf16[1,2,1,4,64,768]{5,4,3,2,1,0:T(8,128)(2,1)S(1)}, bf16[1,2,1,4,64,768]{5,4,3,2,1,0:T(8,128)(2,1)S(1)}, u32[]{:S(2)}, u32[]{:S(2)}) collective-permute-start(bf16[1,2,1,4,64,768]{5,4,3,2,1,0:T(8,128)(2,1)S(1)} %dynamic-slice_convert_fusion.5), channel_id=1, source_target_pairs={{0,4},{1,5},{2,6},{3,7},{4,0},{5,1},{6,2},{7,3},{8,12},{9,13},{10,... | collective-permute-start | bytes 2359304 | tf_op jit(solution)/shard_map/ppermute | solution.py:131
  1037.2 39.6 %collective-permute-start.81 = (bf16[1,1,64,2048]{3,2,1,0:T(8,128)(2,1)S(1)}, bf16[1,1,64,2048]{3,2,1,0:T(8,128)(2,1)S(1)}, u32[]{:S(2)}, u32[]{:S(2)}) collective-permute-start(bf16[1,1,64,2048]{3,2,1,0:T(8,128)(2,1)S(1)} %dynamic-slice_convert_fusion.7), channel_id=1, source_target_pairs={{0,4},{1,5},{2,6},{3,7},{4,0},{5,1},{6,2},{7,3},{8,12},{9,13},{10,... | collective-permute-start | bytes 786440 | tf_op jit(solution)/shard_map/ppermute | solution.py:131
  (146 other events, 2993.6 us)

commit v2 on v1

--- a/solution.py
+++ b/solution.py
@@ -1,6 +1,10 @@
+import functools
+
 import jax
 import jax.numpy as jnp
 from jax import lax
+from jax.experimental import pallas as pl
+from jax.experimental.pallas import tpu as pltpu
 from jax.sharding import PartitionSpec as P
 
 HEAD_DIM = 64
@@ -11,6 +15,7 @@
 rope_base = 130000.0
 bf16 = jnp.bfloat16
 f32 = jnp.float32
+MESH = pl.DeviceIdType.MESH
 
 
 def rope_tables(seq_len, head_dim):
@@ -53,26 +58,12 @@
     )
 
 
-def attend(queries, keys_rot, values):
+def attend_back(queries, keys_rot, values, grad_mixed):
     scale_factor = queries.shape[-1] ** (-0.5)
     scores = (
         jnp.einsum("bqhd,bkhd->bhqk", queries, keys_rot, preferred_element_type=f32) * scale_factor
     )
-    scores = jnp.where(causal_mask(scores.shape[-1]), scores, -1e30)
-    row_max = jnp.max(scores, axis=-1, keepdims=True)
-    exp_scores = jnp.exp(scores - row_max)
-    row_total = jnp.sum(exp_scores, axis=-1, keepdims=True)
-    soft = (exp_scores / row_total).astype(bf16)
-    mixed = jnp.einsum("bhqk,bkhd->bqhd", soft, values, preferred_element_type=f32)
-    return (mixed, (row_max + jnp.log(row_total))[..., 0])
-
-
-def attend_back(queries, keys_rot, values, grad_mixed, log_total):
-    scale_factor = queries.shape[-1] ** (-0.5)
-    scores = (
-        jnp.einsum("bqhd,bkhd->bhqk", queries, keys_rot, preferred_element_type=f32) * scale_factor
-    )
-    soft = jnp.where(causal_mask(scores.shape[-1]), jnp.exp(scores - log_total[..., None]), 0.0)
+    soft = jax.nn.softmax(jnp.where(causal_mask(scores.shape[-1]), scores, -1e30), axis=-1)
     grad_soft = jnp.einsum("bqhd,bkhd->bhqk", grad_mixed, values, preferred_element_type=f32)
     grad_scores = (soft * (grad_soft - jnp.sum(soft * grad_soft, axis=-1, keepdims=True))).astype(
         bf16
@@ -275,6 +266,483 @@
         return totals
 
 
+class Ring:
+    def __init__(self, outer, inner, rows):
+        self.count = outer * inner
+        self.inner = inner
+        self.span = max(1, HEAD_DIM // rows)
+        self.bit_a = self.span
+        self.bit_b = 2 * self.span
+        self.bit_core = inner
+        self.low = powers(1, self.span)
+        self.mid = powers(QUAD * self.span, inner)
+        self.upper = powers(2 * inner, self.count)
+        self.data_bits = self.low + self.mid + self.upper
+        self.deltas = [
+            (self.bit_core if t // QUAD else 0) + (t % QUAD) * self.span for t in range(2 * QUAD)
+        ]
+        self.across = inner // (QUAD * self.span)
+        self.upper_size = outer // 2
+        self.flat = lax.axis_index("dp") * inner + lax.axis_index("fsdp")
+
+    def flip(self, flat, bits):
+        bit = 1
+        while bit <= bits:
+            if bits & bit:
+                flat = flat + bit * (1 - 2 * ((flat // bit) % 2))
+            bit *= 2
+        return flat
+
+    def where(self, bits):
+        other = self.flip(self.flat, bits)
+        return (other // self.inner, other % self.inner)
+
+    def team(self, flat):
+        return ((flat // self.inner) % 2) * QUAD + (flat // self.span) % QUAD
+
+    def place(self, flat):
+        return (
+            (flat // (2 * self.inner)) * self.across + (flat % self.inner) // (QUAD * self.span)
+        ) * self.span + flat % self.span
+
+    def runs(self, flat, rows):
+        lowest = flat - self.span * ((flat // self.span) % QUAD)
+        lowest = lowest - self.inner * ((flat // self.inner) % 2)
+        found = []
+        for core in range(2):
+            start = lowest + core * self.inner
+            if self.span == 1:
+                found.append((start * rows, QUAD * rows))
+            else:
+                found += [((start + q * self.span) * rows, rows) for q in range(QUAD)]
+        return found
+
+    def greet(self):
+        partners = self.deltas[1:] + self.data_bits
+        barrier = pltpu.get_barrier_semaphore()
+        for bits in partners:
+            pl.semaphore_signal(barrier, 1, device_id=self.where(bits), device_id_type=MESH)
+        pl.semaphore_wait(barrier, len(partners))
+
+
+def powers(first, end):
+    found = []
+    while first < end:
+        found.append(first)
+        first *= 2
+    return found
+
+
+class Mail:
+    def __init__(self, ring, send_sems, recv_sems, local_sems):
+        self.ring, self.send_sems, self.recv_sems, self.local_sems = ring, send_sems, recv_sems, local_sems
+        self.used = 0
+        self.used_local = 0
+        self.sent = []
+        self.kept = []
+
+    def post(self, src, dst, bits):
+        copy = pltpu.make_async_remote_copy(
+            src_ref=src,
+            dst_ref=dst,
+            send_sem=self.send_sems.at[self.used],
+            recv_sem=self.recv_sems.at[self.used],
+            device_id=self.ring.where(bits),
+            device_id_type=MESH,
+        )
+        self.used += 1
+        copy.start()
+        self.sent.append(copy)
+        return copy
+
+    def keep(self, src, dst):
+        copy = pltpu.make_async_copy(src, dst, self.local_sems.at[self.used_local])
+        self.used_local += 1
+        copy.start()
+        self.kept.append(copy)
+        return copy
+
+    def finish(self):
+        for copy in self.sent:
+            copy.wait_send()
+        for copy in self.kept:
+            copy.wait()
+
+
+class Spread:
+    def __init__(self, mail, views, bits):
+        self.mail, self.views, self.bits = mail, views, bits
+        self.came = {}
+
+    def start(self, key, stage):
+        bit = self.bits[stage]
+        self.came[key + bit] = [self.mail.post(ref, ref, bit) for ref in self.views(key)]
+
+    def start_from(self, key, first):
+        for stage in range(first, len(self.bits)):
+            self.start(key, stage)
+
+    def pass_on(self, stage):
+        for low in range(2**stage):
+            key = sum(b for i, b in enumerate(self.bits[:stage]) if low >> i & 1) + self.bits[stage]
+            for later in range(stage + 1, len(self.bits)):
+                self.came[key + self.bits[later]] = []
+            for copy, ref in zip(self.came[key], self.views(key)):
+                copy.wait_recv()
+                for later in range(stage + 1, len(self.bits)):
+                    bit = self.bits[later]
+                    self.came[key + bit].append(self.mail.post(ref, ref, bit))
+            self.came[key] = []
+
+    def pass_all(self):
+        for stage in range(len(self.bits) - 1):
+            self.pass_on(stage)
+
+    def done(self):
+        for copies in self.came.values():
+            for copy in copies:
+                copy.wait_recv()
+
+
+class Share:
+    def __init__(self, mail, whole, own):
+        self.mail, self.whole, self.own = mail, whole, own
+        self.half = own.shape[0] // 2
+
+    def first(self):
+        ring = self.mail.ring
+        self.from_a = self.mail.post(self.own, self.whole.at[1], ring.bit_a)
+        self.from_b = self.mail.post(self.own, self.whole.at[2], ring.bit_b)
+        self.core = [self.mail.post(self.own, self.whole.at[QUAD], ring.bit_core)]
+
+    def second(self):
+        ring = self.mail.ring
+        top, end = pl.ds(0, self.half), pl.ds(self.half, self.half)
+        self.from_a.wait_recv()
+        self.one = self.mail.post(self.whole.at[1, top], self.whole.at[3, top], ring.bit_b)
+        self.core.append(self.mail.post(self.whole.at[1], self.whole.at[QUAD + 1], ring.bit_core))
+        self.from_b.wait_recv()
+        self.two = self.mail.post(self.whole.at[2, end], self.whole.at[3, end], ring.bit_a)
+        self.core.append(self.mail.post(self.whole.at[2], self.whole.at[QUAD + 2], ring.bit_core))
+
+    def third(self):
+        self.one.wait_recv()
+        self.two.wait_recv()
+        self.core.append(
+            self.mail.post(self.whole.at[3], self.whole.at[QUAD + 3], self.mail.ring.bit_core)
+        )
+
+    def done(self):
+        for copy in self.core:
+            copy.wait_recv()
+
+
+def head_mask(width, head):
+    lanes = lax.broadcasted_iota(jnp.int32, (1, width), 1)
+    return (lanes >= head * HEAD_DIM) & (lanes < (head + 1) * HEAD_DIM)
+
+
+def turn(u, cosine, signed_sine):
+    width = u.shape[-1]
+    half = HEAD_DIM // 2
+    lanes = lax.broadcasted_iota(jnp.int32, (1, width), 1)
+    lower = lanes % HEAD_DIM < half
+    turned = jnp.where(lower, pltpu.roll(u, width - half, 1), pltpu.roll(u, half, 1))
+    return u * cosine + turned * signed_sine
+
+
+def front_kernel(
+    outer, inner, seq_len,
+    x_ref, go_ref, factor_ref, gain_ref, wq_ref, wk_ref, wv_ref, cos_ref, sin_ref,
+    wo_ref, wg_ref, wu_ref, wd_ref,
+    act_one, w_qkv, w_o, q_out, k_out, v_out, att_out, resid_out, gains_out,
+    act_two, dy, w_gu, w_d,
+    cut, gain_in, far, core_in, near, own_sum, half_a, half_b, in_a, in_b, act_two_own, dy_own,
+    send_sems, recv_sems, local_sems, far_send, far_recv,
+):
+    rows = wq_ref.shape[0]
+    width = wq_ref.shape[1]
+    hidden_rows = wd_ref.shape[0]
+    narrow = width // (2 * QUAD)
+    hidden = w_gu.shape[1] // 2
+    ring = Ring(outer, inner, rows)
+    mail = Mail(ring, send_sems, recv_sems, local_sems)
+    ring.greet()
+    bits = ring.data_bits
+    flat = ring.flat
+
+    def by_place(ref, size):
+        return lambda key: [ref.at[pl.ds(pl.multiple_of(ring.place(ring.flip(flat, key)) * size, 16), size)]]
+
+    def by_runs(ref):
+        return lambda key: [
+            ref.at[pl.ds(pl.multiple_of(start, 16), size)]
+            for start, size in ring.runs(ring.flip(flat, key), rows)
+        ]
+
+    mine_o = w_o.at[pl.ds(pl.multiple_of(ring.place(flat) * rows, 16), rows)]
+    mine_d = w_d.at[pl.ds(pl.multiple_of(ring.place(flat) * hidden_rows, 16), hidden_rows)]
+    keep_o = mail.keep(wo_ref, mine_o)
+    keep_d = mail.keep(wd_ref, mine_d)
+
+    heads = ring.upper_size * ring.across
+    chunk = HEAD_DIM
+    for t in range(2 * QUAD):
+        for j, ref in enumerate((wq_ref, wk_ref, wv_ref)):
+            parts = []
+            for y in range(ring.upper_size):
+                for o in range(ring.across):
+                    head = ((y * 2 + t // QUAD) * ring.across + o) * QUAD + t % QUAD
+                    parts.append(ref[:, head * chunk : (head + 1) * chunk])
+            cut[t, :, j * narrow : (j + 1) * narrow] = jnp.concatenate(parts, axis=1)
+    here = pl.ds(pl.multiple_of(flat * rows, 16), rows)
+    keep_qkv = mail.keep(cut.at[ring.team(flat)], w_qkv.at[here])
+    qkv_swap = []
+    for delta in ring.deltas[1:]:
+        other = ring.flip(flat, delta)
+        qkv_swap.append(mail.post(cut.at[ring.team(other)], w_qkv.at[here], delta))
+    keep_o.wait()
+    mail.kept = [c for c in mail.kept if c is not keep_o]
+    spread_o = Spread(mail, by_place(w_o, rows), bits)
+    spread_o.start_from(0, 0)
+
+    block = ring.span * hidden_rows
+    gu_swap = []
+    for delta in ring.deltas:
+        other = ring.flip(flat, delta)
+        team = ring.team(other)
+        pieces = []
+        for j, ref in enumerate((wg_ref, wu_ref)):
+            for y in range(ring.upper_size):
+                for o in range(ring.across):
+                    source = ((y * 2 + team // QUAD) * ring.across + o) * QUAD + team % QUAD
+                    target = j * hidden + (y * ring.across + o) * block
+                    src = ref.at[:, pl.ds(pl.multiple_of(source * block, 128), block)]
+                    dst = w_gu.at[here, pl.ds(target, block)]
+                    pieces.append(mail.post(src, dst, delta) if delta else mail.keep(src, dst))
+        gu_swap.append(pieces)
+
+    step = 0
+    gains_out[...] = gain_ref[...]
+    for bit in [ring.bit_core, ring.bit_a, ring.bit_b] + bits:
+        copy = mail.post(gains_out, gain_in.at[step], bit)
+        copy.wait()
+        mail.sent = [c for c in mail.sent if c is not copy]
+        gains_out[...] = gains_out[...] + gain_in[step]
+        step += 1
+    keep_qkv.wait()
+    mail.kept = [c for c in mail.kept if c is not keep_qkv]
+    for copy in qkv_swap:
+        copy.wait_recv()
+    spread_qkv = Spread(mail, by_runs(w_qkv), bits)
+    spread_qkv.start_from(0, 0)
+
+    size = act_one.shape[1]
+    strip = 32
+
+    def norm_one(i, carry):
+        part = pl.ds(pl.multiple_of(i * strip, strip), strip)
+        x = x_ref[part, :].astype(f32)
+        inv = lax.rsqrt(jnp.mean(x * x, axis=-1, keepdims=True) + epsilon)
+        act_one[0, part, :] = (x * inv * gains_out[0:1, :]).astype(bf16)
+        dy_own[part, :] = (go_ref[part, :].astype(f32) * factor_ref[part, :]).astype(bf16)
+        return carry
+
+    lax.fori_loop(0, size // strip, norm_one, 0)
+    share_one = Share(mail, act_one, act_one.at[0])
+    share_one.first()
+    mail.keep(dy_own, dy.at[0])
+    share_one.second()
+    spread_o.pass_all()
+    share_one.third()
+    share_dy = Share(mail, dy, dy_own)
+    share_dy.first()
+    spread_qkv.pass_all()
+    keep_d.wait()
+    mail.kept = [c for c in mail.kept if c is not keep_d]
+    for index, pieces in enumerate(gu_swap):
+        for copy in pieces:
+            if index:
+                copy.wait_recv()
+            else:
+                copy.wait()
+                mail.kept = [c for c in mail.kept if c is not copy]
+    spread_d = Spread(mail, by_place(w_d, hidden_rows), bits)
+    spread_gu = Spread(mail, by_runs(w_gu), bits)
+    spread_d.start_from(0, 0)
+    spread_gu.start_from(0, 0)
+    share_one.done()
+
+    scale = HEAD_DIM**-0.5
+    cosine, sine = cos_ref[...], sin_ref[...]
+    per_block = act_one.shape[1] // seq_len
+
+    def attend_block(place):
+        qkv = jnp.dot(act_one[place], w_qkv[...], preferred_element_type=f32)
+        causal = lax.broadcasted_iota(jnp.int32, (seq_len, seq_len), 1) <= lax.broadcasted_iota(
+            jnp.int32, (seq_len, seq_len), 0
+        )
+        for b in range(per_block):
+            span = slice(b * seq_len, (b + 1) * seq_len)
+            q = turn(qkv[span, :narrow], cosine, sine).astype(bf16)
+            k = turn(qkv[span, narrow : 2 * narrow], cosine, sine).astype(bf16)
+            v = qkv[span, 2 * narrow :].astype(bf16)
+            q_out[place, span] = q
+            k_out[place, span] = k
+            v_out[place, span] = v
+            mixed = jnp.zeros((seq_len, narrow), f32)
+            for head in range(narrow // HEAD_DIM):
+                mask = head_mask(narrow, head)
+                kh = jnp.where(mask, k, jnp.zeros_like(k))
+                vh = jnp.where(mask, v, jnp.zeros_like(v))
+                scores = lax.dot_general(
+                    q, kh, (((1,), (1,)), ((), ())), preferred_element_type=f32
+                )
+                scores = jnp.where(causal, scores * scale, -1e30)
+                top = jnp.max(scores, axis=-1, keepdims=True)
+                grown = jnp.exp(scores - top)
+                soft = (grown / jnp.sum(grown, axis=-1, keepdims=True)).astype(bf16)
+                mixed = mixed + jnp.dot(soft, vh, preferred_element_type=f32)
+            att_out[place, span] = mixed.astype(bf16)
+        return jnp.dot(att_out[place], w_o[...], preferred_element_type=f32)
+
+    def far_copy(j):
+        return pltpu.make_async_remote_copy(
+            src_ref=far.at[j],
+            dst_ref=core_in.at[j],
+            send_sem=far_send.at[j],
+            recv_sem=far_recv.at[j],
+            device_id=ring.where(ring.bit_core),
+            device_id_type=MESH,
+        )
+
+    spread_o.done()
+    spread_qkv.done()
+
+    def far_step(i, carry):
+        j = QUAD - 1 - i
+        far[j] = attend_block(QUAD + j).astype(bf16)
+        far_copy(j).start()
+        return carry
+
+    lax.fori_loop(0, QUAD, far_step, 0)
+    share_dy.second()
+
+    def near_step(i, carry):
+        j = QUAD - 1 - i
+        part = attend_block(j)
+        far_copy(j).wait_recv()
+        own_sum[...] = part + core_in[j].astype(f32)
+        near[j] = own_sum[...].astype(bf16)
+        return carry
+
+    lax.fori_loop(0, QUAD, near_step, 0)
+    for j in range(QUAD):
+        far_copy(j).wait_send()
+    half = size // 2
+    top, end = pl.ds(0, half), pl.ds(half, half)
+    sum_one = mail.post(near.at[3, top], half_a, ring.bit_b)
+    sum_two = mail.post(near.at[3, end], half_b, ring.bit_a)
+    share_dy.third()
+    sum_one.wait_recv()
+    near[1, :half] = (near[1, :half].astype(f32) + half_a[...].astype(f32)).astype(bf16)
+    for_a = mail.post(near.at[1], in_a, ring.bit_a)
+    sum_two.wait_recv()
+    near[2, half:] = (near[2, half:].astype(f32) + half_b[...].astype(f32)).astype(bf16)
+    for_b = mail.post(near.at[2], in_b, ring.bit_b)
+    spread_d.pass_on(0)
+    for_a.wait_recv()
+    for_b.wait_recv()
+
+    def norm_two(i, carry):
+        part = pl.ds(pl.multiple_of(i * strip, strip), strip)
+        resid = (
+            x_ref[part, :].astype(f32)
+            + own_sum[part, :]
+            + in_a[part, :].astype(f32)
+            + in_b[part, :].astype(f32)
+        )
+        resid_out[part, :] = resid
+        inv = lax.rsqrt(jnp.mean(resid * resid, axis=-1, keepdims=True) + epsilon)
+        act_two_own[part, :] = (resid * inv * gains_out[1:2, :]).astype(bf16)
+        return carry
+
+    lax.fori_loop(0, size // strip, norm_two, 0)
+    mail.keep(act_two_own, act_two.at[0])
+    share_two = Share(mail, act_two, act_two_own)
+    share_two.first()
+    share_two.second()
+    share_two.third()
+    for stage in range(1, len(bits) - 1):
+        spread_d.pass_on(stage)
+    spread_gu.pass_all()
+    spread_d.done()
+    spread_gu.done()
+    share_two.done()
+    share_dy.done()
+    mail.finish()
+
+
+def front(outer, inner, batch_size, seq_len, tokens, grad_out, factor_rows, gain_rows, w_query, w_key, w_value, cosine, signed_sine, w_out, w_gate, w_up, w_down):
+    size, width = tokens.shape
+    rows, hidden_all = w_gate.shape
+    hidden_rows = w_down.shape[0]
+    narrow, hidden = width // (2 * QUAD), hidden_all // (2 * QUAD)
+    span = max(1, HEAD_DIM // rows)
+    places = outer * inner // (2 * QUAD)
+    pieces = 2 if span == 1 else 2 * QUAD
+    remote = 2 * (places - 1) * (pieces + 1) + 7 + 14 * places // span + 8 + 24 + 8
+    local = 8 + 2 * places // span
+    vm = pl.BlockSpec(memory_space=pltpu.VMEM)
+    hbm = pl.BlockSpec(memory_space=pl.ANY)
+    eight = (2 * QUAD, size)
+    sds = jax.ShapeDtypeStruct
+    out_shape = (
+        sds(eight + (width,), bf16),
+        sds((width, 3 * narrow), bf16),
+        sds((narrow, width), bf16),
+        sds(eight + (narrow,), bf16),
+        sds(eight + (narrow,), bf16),
+        sds(eight + (narrow,), bf16),
+        sds(eight + (narrow,), bf16),
+        sds((size, width), f32),
+        sds((8, width), f32),
+        sds(eight + (width,), bf16),
+        sds(eight + (width,), bf16),
+        sds((width, 2 * hidden), bf16),
+        sds((hidden, width), bf16),
+    )
+    return pl.pallas_call(
+        functools.partial(front_kernel, outer, inner, seq_len),
+        out_shape=out_shape,
+        in_specs=[vm] * 9 + [hbm] * 4,
+        out_specs=tuple([vm] * 9 + [hbm] * 4),
+        scratch_shapes=[
+            pltpu.VMEM((2 * QUAD, rows, 3 * narrow), bf16),
+            pltpu.VMEM((8, 8, width), f32),
+            pltpu.VMEM((QUAD, size, width), bf16),
+            pltpu.VMEM((QUAD, size, width), bf16),
+            pltpu.VMEM((QUAD, size, width), bf16),
+            pltpu.VMEM((size, width), f32),
+            pltpu.VMEM((size // 2, width), bf16),
+            pltpu.VMEM((size // 2, width), bf16),
+            pltpu.VMEM((size, width), bf16),
+            pltpu.VMEM((size, width), bf16),
+            pltpu.VMEM((size, width), bf16),
+            pltpu.VMEM((size, width), bf16),
+            pltpu.SemaphoreType.DMA((remote,)),
+            pltpu.SemaphoreType.DMA((remote,)),
+            pltpu.SemaphoreType.DMA((local,)),
+            pltpu.SemaphoreType.DMA((QUAD,)),
+            pltpu.SemaphoreType.DMA((QUAD,)),
+        ],
+        compiler_params=pltpu.CompilerParams(
+            collective_id=0, has_side_effects=True, vmem_limit_bytes=60 * 1024 * 1024
+        ),
+        name="front",
+    )(tokens, grad_out, factor_rows, gain_rows, w_query, w_key, w_value, cosine, signed_sine, w_out, w_gate, w_up, w_down)
+
+
 def on_device(
     tokens,
     labels,
@@ -298,46 +766,39 @@
     plan = Plan(outer_count, inner_count, rows)
     x_rows = tokens.reshape(-1, width).astype(f32)
 
-    gains = plan.gather_gains(jnp.stack([gain_attn, gain_mlp])).astype(f32)
-    gain_one, gain_two = gains[0:1], gains[1:2]
-
-    inv_one = lax.rsqrt(jnp.mean(x_rows * x_rows, axis=-1, keepdims=True) + epsilon)
-    act_one_own = (x_rows * inv_one * gain_one).astype(bf16)
-    act_one = plan.share_tokens(act_one_own)
-
-    qkv_parts = plan.swap(
-        jnp.concatenate([plan.cut_columns(w) for w in (w_query, w_key, w_value)], axis=2)
-    )
-    w_qkv = plan.gather(qkv_parts, True)
-    w_o = plan.gather(w_out, False)
-    gu_parts = plan.swap(jnp.concatenate([plan.cut_columns(w) for w in (w_gate, w_up)], axis=2))
-    w_gu = plan.gather(gu_parts, True)
-    w_d = plan.gather(w_down, False)
-
     token_total = float(seq_len * batch_size * outer_count * inner_count)
     picked_counts = jnp.sum(
         jnp.where(labels[:, None] == jnp.arange(3)[None, :], counts[None, :], 0), axis=1
     ).astype(f32)
     factor = token_total / (3.0 * picked_counts)
     cotangent = (grad_out.astype(f32) * factor[:, None, None]).reshape(-1, width)
-    dy = plan.share_tokens(cotangent.astype(bf16))
-
-    narrow = w_qkv.shape[1] // 3
-    hidden = w_gu.shape[1] // 2
-    head_count = narrow // HEAD_DIM
+    cosine, sine = rope_tables(seq_len, HEAD_DIM)
+    head_count = width // (2 * QUAD) // HEAD_DIM
     four_shape = (-1, seq_len, head_count, HEAD_DIM)
-    cosine, sine = rope_tables(seq_len, HEAD_DIM)
-
-    qkv = mm(act_one, w_qkv)
-    q_rot = rotate(qkv[:, :narrow].reshape(four_shape), cosine, sine).astype(bf16)
-    k_rot = rotate(qkv[:, narrow : 2 * narrow].reshape(four_shape), cosine, sine).astype(bf16)
-    values = qkv[:, 2 * narrow :].astype(bf16).reshape(four_shape)
-    mixed, log_total = attend(q_rot, k_rot, values)
-    attended = mixed.reshape(-1, narrow).astype(bf16)
-
-    resid = x_rows + plan.sum_tokens(attended, lambda part: mm(part, w_o))
+    sign = jnp.where(jnp.arange(HEAD_DIM) < HEAD_DIM // 2, -1.0, 1.0)
+    gain_rows = lax.dynamic_update_slice(
+        jnp.zeros((8, width), f32),
+        jnp.stack([gain_attn, gain_mlp]).astype(f32),
+        (0, plan.flat * rows),
+    )
+    factor_rows = jnp.repeat(factor, seq_len)[:, None]
+    (
+        act_one, w_qkv, w_o, q_rot, k_rot, values, attended, resid, gains, act_two, dy, w_gu, w_d,
+    ) = front(
+        outer_count, inner_count, batch_size, seq_len,
+        tokens.reshape(-1, width), grad_out.reshape(-1, width), factor_rows, gain_rows,
+        w_query, w_key, w_value,
+        jnp.tile(cosine, (1, head_count)), jnp.tile(sine * sign, (1, head_count)),
+        w_out, w_gate, w_up, w_down,
+    )
+    narrow = w_o.shape[0]
+    hidden = w_d.shape[0]
+    gain_one, gain_two = gains[0:1], gains[1:2]
+    act_one, act_two, dy = (a.reshape(-1, width) for a in (act_one, act_two, dy))
+    attended = attended.reshape(-1, narrow)
+    q_rot, k_rot, values = (a.reshape(four_shape) for a in (q_rot, k_rot, values))
+    inv_one = lax.rsqrt(jnp.mean(x_rows * x_rows, axis=-1, keepdims=True) + epsilon)
     inv_two = lax.rsqrt(jnp.mean(resid * resid, axis=-1, keepdims=True) + epsilon)
-    act_two = plan.share_tokens((resid * inv_two * gain_two).astype(bf16))
 
     gu = mm(act_two, w_gu)
     gate_pre, up_proj = gu[:, :hidden], gu[:, hidden:]
@@ -373,7 +834,7 @@
     grad_branch = plan.share_tokens(grad_resid.astype(bf16))
     grad_attended = times_transposed(grad_branch, w_o).astype(bf16).reshape(four_shape)
     out_grad = plan.scatter(outer_sum(attended, grad_branch), rows, False)
-    grad_q_rot, grad_k_rot, grad_v = attend_back(q_rot, k_rot, values, grad_attended, log_total)
+    grad_q_rot, grad_k_rot, grad_v = attend_back(q_rot, k_rot, values, grad_attended)
     grad_qkv_cols = jnp.concatenate(
         [
             unrotate(grad_q_rot, cosine, sine).reshape(-1, narrow).astype(bf16),

time: 1150 us -> 1000 us (0.87)
  waiting for transfers between devices: 567 us -> 213 us
  Pallas kernels: 0 us -> 344 us
  starting transfers between devices: 121 us -> 52.3 us
  local copies, waits for them, and re-layouts: 193 us -> 152 us
  matrix products: 205 us -> 179 us
    ppermute x98 -> x47, waiting for transfers between devices: 567 us -> 213 us  [send(): return lax.ppermute(array, AXES, [(r, r ^ bit) for r in range(self.count)])]
    pallas_call x0 -> x1, Pallas kernels: none -> 344 us  [front(): pl.pallas_call(functools.partial(front_kernel, outer, inner, seq_len), ou...]
    ppermute x98 -> x47, starting transfers between devices: 121 us -> 52.3 us  [send(): return lax.ppermute(array, AXES, [(r, r ^ bit) for r in range(self.count)])]
    reshape x17 -> x0, local copies, waits for them, and re-layouts: 31.6 us -> none  [the longest x10 17.8 us: cut_columns(): parts = weight.reshape(rows, ahead, 2, middle, QUAD, chunk)]
    dot_general x0 -> x3, local copies, waits for them, and re-layouts: none -> 26.1 us  [outer_sum(): lax.dot_general(left, right, (((0,), (0,)), ((), ())), preferred_element_...]
    dot_general x6 -> x3, matrix products: 65.1 us -> 41 us  [mm(): return jnp.dot(left, right, preferred_element_type=f32)]
    unnamed x189 -> x74, local copies, waits for them, and re-layouts: 39.6 us -> 17.4 us
    concatenate x4 -> x1, local copies, waits for them, and re-layouts: 19.5 us -> 2.78 us  [share_tokens(): return jnp.concatenate([four, self.send(four, self.bit_core)], axis=0)]
  transfers between devices with their start and end apart: 98 -> 47, of which waited for: 48 -> 18; matrix products, arithmetic and copies ran while one was open for 27% -> 31% of each run, Pallas kernels for 0% -> 0%
where the time goes in v2:
time: 1000 us; the launch traced here: 990 us
  Pallas kernels  344 us (34%)
  waiting for transfers between devices  213 us (21%)
  matrix products  179 us (18%)
  local copies, waits for them, and re-layouts  152 us (15%)
  starting transfers between devices  52.3 us (5%)
  other arithmetic  45.6 us (5%)
    pallas_call x1, Pallas kernels, front(): pl.pallas_call(functools.partial(front_kernel, outer, inner, seq_len), ou...  344 us
    ppermute x47, waiting for transfers between devices, send(): return lax.ppermute(array, AXES, [(r, r ^ bit) for r in range(self.count)])  213 us
    dot_general x6, matrix products, times_transposed(): lax.dot_general(left, weight, (((1,), (1,)), ((), ())), preferred_element...  66 us
    dot_general x4, matrix products, outer_sum(): lax.dot_general(left, right, (((0,), (0,)), ((), ())), preferred_element_...  52.8 us
    ppermute x47, starting transfers between devices, send(): return lax.ppermute(array, AXES, [(r, r ^ bit) for r in range(self.count)])  52.3 us
    dot_general x3, matrix products, mm(): return jnp.dot(left, right, preferred_element_type=f32)  41 us
    dot_general x3, local copies, waits for them, and re-layouts, outer_sum(): lax.dot_general(left, right, (((0,), (0,)), ((), ())), preferred_element_...  26.1 us
    convert_element_type x9, local copies, waits for them, and re-layouts, on_device(): plan.join_columns(qkv_grad[:, :, i * narrow:(i + 1) * narrow]).astype(f32)  20.1 us
  transfers between devices with their start and end apart: 47, of which 18 were waited for; matrix products, arithmetic and copies ran while one was open for 31% of the time, Pallas kernels for 0%

profile of v2, /device:TPU:1, one launch (start us, length us, event | category | flops | bytes accessed | tf_op | source)
XLA Modules:
  0.0 989.9 jit_solution(6177289893666635652)
XLA Ops:
  7.7 344.3 %front.1 = (bf16[8,256,2048]{2,1,0:T(8,128)(2,1)}, bf16[2048,768]{1,0:T(8,128)(2,1)}, bf16[256,2048]{1,0:T(8,128)(2,1)}, bf16[8,256,256]{2,1,0:T(8,128)(2,1)}, b...) custom-call(bf16[256,2048]{1,0:T(8,128)(2,1)} %bitcast.116, ...), custom_call_target="tpu_custom_call" | custom-call | tf_op jit(solution)/shard_map/front/pallas_call | solution.py:715
  352.0 24.5 %fusion.87 = f32[2048,2048]{0,1:T(8,128)} fusion(bf16[2048,2048]{1,0:T(8,128)(2,1)} %bitcast.123, bf16[2048,2048]{1,0:T(8,128)(2,1)} %get-tuple-element.26), kind=kOutput, calls=%fused_computation.216 | convolution fusion | flops 17179869184 | bytes 33554432 | tf_op jit(solution)/shard_map/dot_general | solution.py:44
  376.5 19.5 %multiply_convert_fusion.1 = (bf16[2048,1024]{0,1:T(8,128)(2,1)}, bf16[2048,1024]{0,1:T(8,128)(2,1)}, bf16[2048,1024]{0,1:T(8,128)(2,1)}) fusion(f32[2048,2048]{0,1:T(8,128)} %fusion.87, bf16[2048,2048]{1,0:T(8,128)(2,1)} %bitcast.155, bf16[1024,2048]{1,0:T(8,128)(2,1)S(1)} %copy-done.24), kind=kOutput, calls=%fused_computation.18 | convolution fusion | flops 8623489024 | bytes 41943040 | tf_op jit(solution)/shard_map/dot_general | solution.py:52
  396.1 7.9 convolution_convert_fusion.1
  407.0 12.0 %fusion.18 = bf16[1024,2048]{1,0:T(8,128)(2,1)} fusion(bf16[2048,2048]{1,0:T(8,128)(2,1)S(1)} %copy-done.23, bf16[2048,1024]{0,1:T(8,128)(2,1)} %get-tuple-element.45, bf16[2048,1024]{0,1:T(8,128)(2,1)} %get-tuple-element.44), kind=kOutput, calls=%fused_computation.40 | convolution fusion | flops 8600420352 | bytes 20971520 | tf_op jit(solution)/shard_map/dot_general | solution.py:52
  419.0 12.2 %copy.83 = bf16[2048,2048]{1,0:T(8,128)(2,1)} copy(bf16[2048,2048]{0,1:T(8,128)(2,1)} %bitcast.124) | data formatting | bytes 16777216 | tf_op jit(solution)/shard_map/dot_general | solution.py:48
  431.2 25.2 %fusion.2 = f32[2,2,2,4,64,2048]{5,4,3,2,1,0:T(8,128)} fusion(bf16[2,2,2,4,64,2048]{5,4,3,2,1,0:T(8,128)(2,1)} %bitcast.125, bf16[2048,1024]{0,1:T(8,128)(2,1)} %get-tuple-element.44, bf16[2048,1024]{0,1:T(8,128)(2,1)} %get-tuple-element.45), kind=kOutput, calls=%fused_computation.7 | convolution fusion | flops 17196646400 | bytes 33554432 | tf_op jit(solution)/shard_map/dot_general | solution.py:48
  456.4 6.1 dynamic-slice_convert_fusion
  464.9 14.5 %fusion.89 = f32[2,2,256,2048]{3,2,1,0:T(8,128)} fusion(bf16[2,2,256,2048]{3,2,1,0:T(8,128)(2,1)} %bitcast.157, bf16[2048,2048,1,1]{1,0,3,2:T(8,128)(2,1)} %bitcast.156), kind=kOutput, calls=%fused_computation.218 | convolution fusion | flops 8589934592 | bytes 20971520 | tf_op jit(solution)/shard_map/dot_general | solution.py:48
  479.4 8.6 fusion.84
  490.4 15.9 %fusion.83 = (bf16[1024,2048]{1,0:T(8,128)(2,1)S(1)}, f32[1024,2048]{1,0:T(8,128)}) fusion(bf16[1024,2048]{1,0:T(8,128)(2,1)} %collective-permute-done.5, bf16[2048,2048]{1,0:T(8,128)(2,1)} %get-tuple-element.26, bf16[2048,1024]{0,1:T(8,128)(2,1)} %get-tuple-element.45, bf16[2048,1024]{0,1:T(8,128)(2,1)} %get-tuple-element.44), kind=kOutput, calls=%fused_computation.212 | convolution fusion | flops 8604614656 | bytes 33554432 | tf_op jit(solution)/shard_map/dot_general | solution.py:52
  512.1 7.0 collective-permute-done.6
  526.5 15.9 %collective-permute-done.2 = bf16[256,2048]{1,0:T(8,128)(2,1)S(1)} collective-permute-done((bf16[256,2048]{1,0:T(8,128)(2,1)S(1)}, bf16[256,2048]{1,0:T(8,128)(2,1)S(1)}, u32[]{:S(2)}, u32[]{:S(2)}) %collective-permute-start.2) | collective-permute-done | bytes 1048608 | tf_op jit(solution)/shard_map/ppermute | solution.py:122
  542.7 22.2 %collective-permute-done.7 = bf16[256,2048]{1,0:T(8,128)(2,1)S(1)} collective-permute-done((bf16[256,2048]{1,0:T(8,128)(2,1)S(1)}, bf16[256,2048]{1,0:T(8,128)(2,1)S(1)}, u32[]{:S(2)}, u32[]{:S(2)}) %collective-permute-start.7) | collective-permute-done | bytes 1048608 | tf_op jit(solution)/shard_map/ppermute | solution.py:122
  572.1 5.9 convert_add_fusion
  580.0 13.9 %collective-permute-done.10 = bf16[256,2048]{1,0:T(8,128)(2,1)S(1)} collective-permute-done((bf16[256,2048]{1,0:T(8,128)(2,1)S(1)}, bf16[256,2048]{1,0:T(8,128)(2,1)S(1)}, u32[]{:S(2)}, u32[]{:S(2)}) %collective-permute-start.10) | collective-permute-done | bytes 1048608 | tf_op jit(solution)/shard_map/ppermute | solution.py:122
  598.5 49.5 %collective-permute-done.12 = bf16[128,2048]{1,0:T(8,128)(2,1)S(1)} collective-permute-done((bf16[128,2048]{1,0:T(8,128)(2,1)S(1)}, bf16[128,2048]{1,0:T(8,128)(2,1)S(1)}, u32[]{:S(2)}, u32[]{:S(2)}) %collective-permute-start.12) | collective-permute-done | bytes 524320 | tf_op jit(solution)/shard_map/ppermute | solution.py:122
  663.4 12.4 %copy.78 = bf16[2048,2048]{1,0:T(8,128)(2,1)} copy(bf16[2048,2048]{0,1:T(8,128)(2,1)} %bitcast.117) | data formatting | bytes 16777216 | tf_op jit(solution)/shard_map/dot_general | solution.py:48
  676.2 5.0 fusion.85
  693.4 39.6 %collective-permute-done.46 = bf16[1,1,256,2048]{3,2,1,0:T(8,128)(2,1)S(1)} collective-permute-done((bf16[1,1,256,2048]{3,2,1,0:T(8,128)(2,1)S(1)}, bf16[1,1,256,2048]{3,2,1,0:T(8,128)(2,1)S(1)}, u32[]{:S(2)}, u32[]{:S(2)}) %collective-permute-start.46) | collective-permute-done | bytes 1048608 | tf_op jit(solution)/shard_map/ppermute | solution.py:122
  754.9 4.4 reshape.289
  763.3 6.1 fusion.53
  773.4 4.8 reshape.288
  778.3 5.6 multiply_reduce_fusion
  807.1 4.5 reshape.287
  816.5 7.9 convolution_convert_fusion
  826.9 7.0 fusion.23
  859.0 6.0 fusion.4
  866.1 5.5 collective-permute-done.20
  876.2 7.1 fusion.86
  886.5 29.1 %collective-permute-done.21 = bf16[1,2,1,4,64,768]{5,4,3,2,1,0:T(8,128)(2,1)S(1)} collective-permute-done((bf16[1,2,1,4,64,768]{5,4,3,2,1,0:T(8,128)(2,1)S(1)}, bf16[1,2,1,4,64,768]{5,4,3,2,1,0:T(8,128)(2,1)S(1)}, u32[]{:S(2)}, u32[]{:S(2)}) %collective-permute-start.21) | collective-permute-done | bytes 786464 | tf_op jit(solution)/shard_map/ppermute | solution.py:122
  926.1 16.2 %collective-permute-done.22 = bf16[1,64,768]{2,1,0:T(8,128)(2,1)S(1)} collective-permute-done((bf16[1,64,768]{2,1,0:T(8,128)(2,1)S(1)}, bf16[1,64,768]{2,1,0:T(8,128)(2,1)S(1)}, u32[]{:S(2)}, u32[]{:S(2)}) %collective-permute-start.22) | collective-permute-done | bytes 98336 | tf_op jit(solution)/shard_map/ppermute | solution.py:122
  (280 shorter events, 219.9 us)
Async XLA Ops:
  404.0 75.5 %collective-permute-start = (bf16[1024,2048]{1,0:T(8,128)(2,1)}, bf16[1024,2048]{1,0:T(8,128)(2,1)}, u32[]{:S(2)}, u32[]{:S(2)}) collective-permute-start(bf16[1024,2048]{1,0:T(8,128)(2,1)} %convolution_convert_fusion.1), channel_id=1, source_target_pairs={{0,8},{1,9},{2,10},{3,11},{4,12},{5,13},{6,14},{7,15},{8,0},{9,1},... | collective-permute-start | bytes 12582920 | tf_op jit(solution)/shard_map/ppermute | solution.py:122
  418.9 71.5 %collective-permute-start.5 = (bf16[1024,2048]{1,0:T(8,128)(2,1)}, bf16[1024,2048]{1,0:T(8,128)(2,1)}, u32[]{:S(2)}, u32[]{:S(2)}) collective-permute-start(bf16[1024,2048]{1,0:T(8,128)(2,1)} %fusion.18), channel_id=1, source_target_pairs={{0,8},{1,9},{2,10},{3,11},{4,12},{5,13},{6,14},{7,15},{8,0},{9,1},... | collective-permute-start | bytes 12582920 | tf_op jit(solution)/shard_map/ppermute | solution.py:122
  462.5 109.6 %collective-permute-start.36 = (bf16[1,2,2,4,64,2048]{5,4,3,2,1,0:T(8,128)(2,1)}, bf16[1,2,2,4,64,2048]{5,4,3,2,1,0:T(8,128)(2,1)}, u32[]{:S(2)}, u32[]{:S(2)}) collective-permute-start(bf16[1,2,2,4,64,2048]{5,4,3,2,1,0:T(8,128)(2,1)} %dynamic-slice_convert_fusion), channel_id=1, source_target_pairs={{0,16},{1,17},{2,18},{3,19},{4,20},{5,21},{6,22},{7,23},{8,24},{9,... | collective-permute-start | bytes 12582920 | tf_op jit(solution)/shard_map/ppermute | solution.py:122
  510.3 32.1 %collective-permute-start.2 = (bf16[256,2048]{1,0:T(8,128)(2,1)S(1)}, bf16[256,2048]{1,0:T(8,128)(2,1)S(1)}, u32[]{:S(2)}, u32[]{:S(2)}) collective-permute-start(bf16[256,2048]{1,0:T(8,128)(2,1)S(1)} %pad_maximum_fusion.1), channel_id=1, source_target_pairs={{0,1},{1,0},{2,3},{3,2},{4,5},{5,4},{6,7},{7,6},{8,9},{9,8},{10,11... | collective-permute-start | bytes 3145736 | tf_op jit(solution)/shard_map/ppermute | solution.py:122
  511.9 30.8 %collective-permute-start.4 = (bf16[256,2048]{1,0:T(8,128)(2,1)S(1)}, bf16[256,2048]{1,0:T(8,128)(2,1)S(1)}, u32[]{:S(2)}, u32[]{:S(2)}) collective-permute-start(bf16[256,2048]{1,0:T(8,128)(2,1)S(1)} %pad_maximum_fusion.2), channel_id=1, source_target_pairs={{0,2},{1,3},{2,0},{3,1},{4,6},{5,7},{6,4},{7,5},{8,10},{9,11},{10,... | collective-permute-start | bytes 3145736 | tf_op jit(solution)/shard_map/ppermute | solution.py:122
  520.4 44.5 %collective-permute-start.7 = (bf16[256,2048]{1,0:T(8,128)(2,1)S(1)}, bf16[256,2048]{1,0:T(8,128)(2,1)S(1)}, u32[]{:S(2)}, u32[]{:S(2)}) collective-permute-start(bf16[256,2048]{1,0:T(8,128)(2,1)S(1)} %pad_maximum_fusion.3), channel_id=1, source_target_pairs={{0,1},{1,0},{2,3},{3,2},{4,5},{5,4},{6,7},{7,6},{8,9},{9,8},{10,11... | collective-permute-start | bytes 3145736 | tf_op jit(solution)/shard_map/ppermute | solution.py:122
  520.6 44.3 %collective-permute-start.9 = (bf16[256,2048]{1,0:T(8,128)(2,1)S(1)}, bf16[256,2048]{1,0:T(8,128)(2,1)S(1)}, u32[]{:S(2)}, u32[]{:S(2)}) collective-permute-start(bf16[256,2048]{1,0:T(8,128)(2,1)S(1)} %pad_maximum_fusion.4), channel_id=1, source_target_pairs={{0,2},{1,3},{2,0},{3,1},{4,6},{5,7},{6,4},{7,5},{8,10},{9,11},{10,... | collective-permute-start | bytes 3145736 | tf_op jit(solution)/shard_map/ppermute | solution.py:122
  542.4 138.7 %collective-permute-start.45 = (bf16[1,2,256,2048]{3,2,1,0:T(8,128)(2,1)}, bf16[1,2,256,2048]{3,2,1,0:T(8,128)(2,1)}, u32[]{:S(2)}, u32[]{:S(2)}) collective-permute-start(bf16[1,2,256,2048]{3,2,1,0:T(8,128)(2,1)} %dynamic-slice_convert_fusion.1), channel_id=1, source_target_pairs={{0,16},{1,17},{2,18},{3,19},{4,20},{5,21},{6,22},{7,23},{8,24},{9,... | collective-permute-start | bytes 6291464 | tf_op jit(solution)/shard_map/ppermute | solution.py:122
  571.6 22.3 %collective-permute-start.10 = (bf16[256,2048]{1,0:T(8,128)(2,1)S(1)}, bf16[256,2048]{1,0:T(8,128)(2,1)S(1)}, u32[]{:S(2)}, u32[]{:S(2)}) collective-permute-start(bf16[256,2048]{1,0:T(8,128)(2,1)S(1)} %get-tuple-element.42), channel_id=1, source_target_pairs={{0,1},{1,0},{2,3},{3,2},{4,5},{5,4},{6,7},{7,6},{8,9},{9,8},{10,11... | collective-permute-start | bytes 3145736 | tf_op jit(solution)/shard_map/ppermute | solution.py:122
  571.7 23.0 %collective-permute-start.11 = (bf16[256,2048]{1,0:T(8,128)(2,1)S(1)}, bf16[256,2048]{1,0:T(8,128)(2,1)S(1)}, u32[]{:S(2)}, u32[]{:S(2)}) collective-permute-start(bf16[256,2048]{1,0:T(8,128)(2,1)S(1)} %get-tuple-element.42), channel_id=1, source_target_pairs={{0,2},{1,3},{2,0},{3,1},{4,6},{5,7},{6,4},{7,5},{8,10},{9,11},{10,... | collective-permute-start | bytes 3145736 | tf_op jit(solution)/shard_map/ppermute | solution.py:122
  579.9 104.9 %collective-permute-start.37 = (bf16[1,2,1,4,64,2048]{5,4,3,2,1,0:T(8,128)(2,1)}, bf16[1,2,1,4,64,2048]{5,4,3,2,1,0:T(8,128)(2,1)}, u32[]{:S(2)}, u32[]{:S(2)}) collective-permute-start(bf16[1,2,1,4,64,2048]{5,4,3,2,1,0:T(8,128)(2,1)} %dynamic-slice_convert_fusion.2), channel_id=1, source_target_pairs={{0,4},{1,5},{2,6},{3,7},{4,0},{5,1},{6,2},{7,3},{8,12},{9,13},{10,... | collective-permute-start | bytes 6291464 | tf_op jit(solution)/shard_map/ppermute | solution.py:122
  594.0 54.0 %collective-permute-start.12 = (bf16[128,2048]{1,0:T(8,128)(2,1)S(1)}, bf16[128,2048]{1,0:T(8,128)(2,1)S(1)}, u32[]{:S(2)}, u32[]{:S(2)}) collective-permute-start(bf16[128,2048]{1,0:T(8,128)(2,1)S(1)} %slice.287), channel_id=1, source_target_pairs={{0,2},{1,3},{2,0},{3,1},{4,6},{5,7},{6,4},{7,5},{8,10},{9,11},{10,... | collective-permute-start | bytes 1572872 | tf_op jit(solution)/shard_map/ppermute | solution.py:122
  594.8 54.1 %collective-permute-start.13 = (bf16[128,2048]{1,0:T(8,128)(2,1)S(1)}, bf16[128,2048]{1,0:T(8,128)(2,1)S(1)}, u32[]{:S(2)}, u32[]{:S(2)}) collective-permute-start(bf16[128,2048]{1,0:T(8,128)(2,1)S(1)} %slice.288), channel_id=1, source_target_pairs={{0,1},{1,0},{2,3},{3,2},{4,5},{5,4},{6,7},{7,6},{8,9},{9,8},{10,11... | collective-permute-start | bytes 1572872 | tf_op jit(solution)/shard_map/ppermute | solution.py:122
  653.1 92.1 %collective-permute-start.14 = (bf16[1024,2048]{1,0:T(8,128)(2,1)}, bf16[1024,2048]{1,0:T(8,128)(2,1)}, u32[]{:S(2)}, u32[]{:S(2)}) collective-permute-start(bf16[1024,2048]{1,0:T(8,128)(2,1)} %get-tuple-element.95), channel_id=1, source_target_pairs={{0,8},{1,9},{2,10},{3,11},{4,12},{5,13},{6,14},{7,15},{8,0},{9,1},... | collective-permute-start | bytes 12582920 | tf_op jit(solution)/shard_map/ppermute | solution.py:122
  684.8 48.2 %collective-permute-start.46 = (bf16[1,1,256,2048]{3,2,1,0:T(8,128)(2,1)S(1)}, bf16[1,1,256,2048]{3,2,1,0:T(8,128)(2,1)S(1)}, u32[]{:S(2)}, u32[]{:S(2)}) collective-permute-start(bf16[1,1,256,2048]{3,2,1,0:T(8,128)(2,1)S(1)} %dynamic-slice_convert_fusion.4), channel_id=1, source_target_pairs={{0,4},{1,5},{2,6},{3,7},{4,0},{5,1},{6,2},{7,3},{8,12},{9,13},{10,... | collective-permute-start | bytes 3145736 | tf_op jit(solution)/shard_map/ppermute | solution.py:122
  689.8 45.6 %collective-permute-start.38 = (bf16[1,64,2048]{2,1,0:T(8,128)(2,1)S(1)}, bf16[1,64,2048]{2,1,0:T(8,128)(2,1)S(1)}, u32[]{:S(2)}, u32[]{:S(2)}) collective-permute-start(bf16[1,64,2048]{2,1,0:T(8,128)(2,1)S(1)} %get-tuple-element.73), channel_id=1, source_target_pairs={{0,1},{1,0},{2,3},{3,2},{4,5},{5,4},{6,7},{7,6},{8,9},{9,8},{10,11... | collective-permute-start | bytes 786440 | tf_op jit(solution)/shard_map/ppermute | solution.py:122
  691.2 45.6 %collective-permute-start.39 = (bf16[1,64,2048]{2,1,0:T(8,128)(2,1)S(1)}, bf16[1,64,2048]{2,1,0:T(8,128)(2,1)S(1)}, u32[]{:S(2)}, u32[]{:S(2)}) collective-permute-start(bf16[1,64,2048]{2,1,0:T(8,128)(2,1)S(1)} %get-tuple-element.72), channel_id=1, source_target_pairs={{0,2},{1,3},{2,0},{3,1},{4,6},{5,7},{6,4},{7,5},{8,10},{9,11},{10,... | collective-permute-start | bytes 786440 | tf_op jit(solution)/shard_map/ppermute | solution.py:122
  735.4 89.5 %collective-permute-start.42 = (bf16[1,64,2048]{2,1,0:T(8,128)(2,1)}, bf16[1,64,2048]{2,1,0:T(8,128)(2,1)}, u32[]{:S(2)}, u32[]{:S(2)}) collective-permute-start(bf16[1,64,2048]{2,1,0:T(8,128)(2,1)} %get-tuple-element.69), channel_id=1, source_target_pairs={{0,9},{1,8},{2,11},{3,10},{4,13},{5,12},{6,15},{7,14},{8,1},{9,0},... | collective-permute-start | bytes 786440 | tf_op jit(solution)/shard_map/ppermute | solution.py:122
  736.8 89.0 %collective-permute-start.43 = (bf16[1,64,2048]{2,1,0:T(8,128)(2,1)}, bf16[1,64,2048]{2,1,0:T(8,128)(2,1)}, u32[]{:S(2)}, u32[]{:S(2)}) collective-permute-start(bf16[1,64,2048]{2,1,0:T(8,128)(2,1)} %get-tuple-element.68), channel_id=1, source_target_pairs={{0,10},{1,11},{2,8},{3,9},{4,14},{5,15},{6,12},{7,13},{8,2},{9,3},... | collective-permute-start | bytes 786440 | tf_op jit(solution)/shard_map/ppermute | solution.py:122
  742.6 93.0 %collective-permute-start.44 = (bf16[1,64,2048]{2,1,0:T(8,128)(2,1)S(1)}, bf16[1,64,2048]{2,1,0:T(8,128)(2,1)}, u32[]{:S(2)}, u32[]{:S(2)}) collective-permute-start(bf16[1,64,2048]{2,1,0:T(8,128)(2,1)S(1)} %get-tuple-element.67), channel_id=1, source_target_pairs={{0,11},{1,10},{2,9},{3,8},{4,15},{5,14},{6,13},{7,12},{8,3},{9,2},... | collective-permute-start | bytes 786440 | tf_op jit(solution)/shard_map/ppermute | solution.py:122
  824.4 51.7 %collective-permute-start.15 = (bf16[1024,2048]{1,0:T(8,128)(2,1)}, bf16[1024,2048]{1,0:T(8,128)(2,1)}, u32[]{:S(2)}, u32[]{:S(2)}) collective-permute-start(bf16[1024,2048]{1,0:T(8,128)(2,1)} %convolution_convert_fusion), channel_id=1, source_target_pairs={{0,8},{1,9},{2,10},{3,11},{4,12},{5,13},{6,14},{7,15},{8,0},{9,1},... | collective-permute-start | bytes 12582920 | tf_op jit(solution)/shard_map/ppermute | solution.py:122
  835.3 36.3 %collective-permute-start.20 = (bf16[1,2,2,4,64,768]{5,4,3,2,1,0:T(8,128)(2,1)}, bf16[1,2,2,4,64,768]{5,4,3,2,1,0:T(8,128)(2,1)}, u32[]{:S(2)}, u32[]{:S(2)}) collective-permute-start(bf16[1,2,2,4,64,768]{5,4,3,2,1,0:T(8,128)(2,1)} %dynamic-slice_convert_fusion.3), channel_id=1, source_target_pairs={{0,16},{1,17},{2,18},{3,19},{4,20},{5,21},{6,22},{7,23},{8,24},{9,... | collective-permute-start | bytes 4718600 | tf_op jit(solution)/shard_map/ppermute | solution.py:122
  874.5 41.2 %collective-permute-start.21 = (bf16[1,2,1,4,64,768]{5,4,3,2,1,0:T(8,128)(2,1)S(1)}, bf16[1,2,1,4,64,768]{5,4,3,2,1,0:T(8,128)(2,1)S(1)}, u32[]{:S(2)}, u32[]{:S(2)}) collective-permute-start(bf16[1,2,1,4,64,768]{5,4,3,2,1,0:T(8,128)(2,1)S(1)} %dynamic-slice_convert_fusion.5), channel_id=1, source_target_pairs={{0,4},{1,5},{2,6},{3,7},{4,0},{5,1},{6,2},{7,3},{8,12},{9,13},{10,... | collective-permute-start | bytes 2359304 | tf_op jit(solution)/shard_map/ppermute | solution.py:122
  883.5 32.4 %collective-permute-start.16 = (bf16[128,2048]{1,0:T(8,128)(2,1)S(1)}, bf16[128,2048]{1,0:T(8,128)(2,1)S(1)}, u32[]{:S(2)}, u32[]{:S(2)}) collective-permute-start(bf16[128,2048]{1,0:T(8,128)(2,1)S(1)} %get-tuple-element.53), channel_id=1, source_target_pairs={{0,2},{1,3},{2,0},{3,1},{4,6},{5,7},{6,4},{7,5},{8,10},{9,11},{10,... | collective-permute-start | bytes 1572872 | tf_op jit(solution)/shard_map/ppermute | solution.py:122
  883.9 32.0 %collective-permute-start.18 = (bf16[128,2048]{1,0:T(8,128)(2,1)S(1)}, bf16[128,2048]{1,0:T(8,128)(2,1)S(1)}, u32[]{:S(2)}, u32[]{:S(2)}) collective-permute-start(bf16[128,2048]{1,0:T(8,128)(2,1)S(1)} %get-tuple-element.54), channel_id=1, source_target_pairs={{0,1},{1,0},{2,3},{3,2},{4,5},{5,4},{6,7},{7,6},{8,9},{9,8},{10,11... | collective-permute-start | bytes 1572872 | tf_op jit(solution)/shard_map/ppermute | solution.py:122
  884.6 36.7 %collective-permute-start.30 = (bf16[1,1,64,2048]{3,2,1,0:T(8,128)(2,1)S(1)}, bf16[1,1,64,2048]{3,2,1,0:T(8,128)(2,1)S(1)}, u32[]{:S(2)}, u32[]{:S(2)}) collective-permute-start(bf16[1,1,64,2048]{3,2,1,0:T(8,128)(2,1)S(1)} %dynamic-slice_convert_fusion.7), channel_id=1, source_target_pairs={{0,4},{1,5},{2,6},{3,7},{4,0},{5,1},{6,2},{7,3},{8,12},{9,13},{10,... | collective-permute-start | bytes 786440 | tf_op jit(solution)/shard_map/ppermute | solution.py:122
  916.3 37.3 %collective-permute-start.17 = (bf16[256,2048]{1,0:T(8,128)(2,1)S(1)}, bf16[256,2048]{1,0:T(8,128)(2,1)S(1)}, u32[]{:S(2)}, u32[]{:S(2)}) collective-permute-start(bf16[256,2048]{1,0:T(8,128)(2,1)S(1)} %pad_maximum_fusion.5), channel_id=1, source_target_pairs={{0,1},{1,0},{2,3},{3,2},{4,5},{5,4},{6,7},{7,6},{8,9},{9,8},{10,11... | collective-permute-start | bytes 3145736 | tf_op jit(solution)/shard_map/ppermute | solution.py:122
  919.2 34.4 %collective-permute-start.19 = (bf16[256,2048]{1,0:T(8,128)(2,1)S(1)}, bf16[256,2048]{1,0:T(8,128)(2,1)S(1)}, u32[]{:S(2)}, u32[]{:S(2)}) collective-permute-start(bf16[256,2048]{1,0:T(8,128)(2,1)S(1)} %pad_maximum_fusion.6), channel_id=1, source_target_pairs={{0,2},{1,3},{2,0},{3,1},{4,6},{5,7},{6,4},{7,5},{8,10},{9,11},{10,... | collective-permute-start | bytes 3145736 | tf_op jit(solution)/shard_map/ppermute | solution.py:122
  919.4 22.9 %collective-permute-start.22 = (bf16[1,64,768]{2,1,0:T(8,128)(2,1)S(1)}, bf16[1,64,768]{2,1,0:T(8,128)(2,1)S(1)}, u32[]{:S(2)}, u32[]{:S(2)}) collective-permute-start(bf16[1,64,768]{2,1,0:T(8,128)(2,1)S(1)} %get-tuple-element.93), channel_id=1, source_target_pairs={{0,1},{1,0},{2,3},{3,2},{4,5},{5,4},{6,7},{7,6},{8,9},{9,8},{10,11... | collective-permute-start | bytes 294920 | tf_op jit(solution)/shard_map/ppermute | solution.py:122
  922.1 24.5 %collective-permute-start.23 = (bf16[1,64,768]{2,1,0:T(8,128)(2,1)S(1)}, bf16[1,64,768]{2,1,0:T(8,128)(2,1)S(1)}, u32[]{:S(2)}, u32[]{:S(2)}) collective-permute-start(bf16[1,64,768]{2,1,0:T(8,128)(2,1)S(1)} %get-tuple-element.92), channel_id=1, source_target_pairs={{0,2},{1,3},{2,0},{3,1},{4,6},{5,7},{6,4},{7,5},{8,10},{9,11},{10,... | collective-permute-start | bytes 294920 | tf_op jit(solution)/shard_map/ppermute | solution.py:122
  922.1 28.3 %collective-permute-start.24 = (bf16[1,64,768]{2,1,0:T(8,128)(2,1)S(1)}, bf16[1,64,768]{2,1,0:T(8,128)(2,1)S(1)}, u32[]{:S(2)}, u32[]{:S(2)}) collective-permute-start(bf16[1,64,768]{2,1,0:T(8,128)(2,1)S(1)} %get-tuple-element.91), channel_id=1, source_target_pairs={{0,3},{1,2},{2,1},{3,0},{4,7},{5,6},{6,5},{7,4},{8,11},{9,10},{10,... | collective-permute-start | bytes 294920 | tf_op jit(solution)/shard_map/ppermute | solution.py:122
  960.0 21.3 %collective-permute-start.33 = (f32[2,256]{1,0:T(2,128)S(1)}, f32[2,256]{1,0:T(2,128)S(1)}, u32[]{:S(2)}, u32[]{:S(2)}) collective-permute-start(f32[2,256]{1,0:T(2,128)S(1)} %broadcast_select_fusion.2), channel_id=1, source_target_pairs={{0,4},{1,5},{2,6},{3,7},{4,0},{5,1},{6,2},{7,3},{8,12},{9,13},{10,... | collective-permute-start | bytes 6152 | tf_op jit(solution)/shard_map/ppermute | solution.py:122
  (49 other events, 648.8 us)

commit v3 on v2

--- a/solution.py
+++ b/solution.py
@@ -743,6 +743,523 @@
     )(tokens, grad_out, factor_rows, gain_rows, w_query, w_key, w_value, cosine, signed_sine, w_out, w_gate, w_up, w_down)
 
 
+def add_far(target, left, right):
+    rows, width = left.shape
+    strip = min(64, rows)
+
+    def body(left_ref, right_ref, target_ref):
+        target_ref[...] = (left_ref[...].astype(f32) + right_ref[...].astype(f32)).astype(
+            target_ref.dtype
+        )
+
+    spec = pl.BlockSpec((strip, width), lambda i: (i, 0))
+    pltpu.emit_pipeline(body, grid=(rows // strip,), in_specs=[spec, spec], out_specs=[spec])(
+        left, right, target
+    )
+
+
+def add_near(target, left, right):
+    rows = left.shape[0]
+    strip = min(32, rows)
+
+    def step(i, carry):
+        part = pl.ds(pl.multiple_of(i * strip, strip), strip)
+        target[part, :] = (left[part, :].astype(f32) + right[part, :].astype(f32)).astype(
+            target.dtype
+        )
+        return carry
+
+    lax.fori_loop(0, rows // strip, step, 0)
+
+
+def keys_below(bits, stage):
+    return [
+        sum(b for i, b in enumerate(bits[:stage]) if low >> i & 1) for low in range(2**stage)
+    ]
+
+
+class Collect:
+    def __init__(self, mail, bits, views, landed, sums, last, add):
+        self.mail, self.bits, self.views = mail, bits, views
+        self.landed, self.sums, self.last, self.add = landed, sums, last, add
+        self.came = {}
+        self.added = set()
+        self.pieces = len(views(0))
+
+    def slot(self, stage, sub, piece):
+        return (2**stage - 1 + keys_below(self.bits, stage).index(sub)) * self.pieces + piece
+
+    def current(self, sub, piece):
+        if (sub, piece) not in self.added:
+            return self.views(sub)[piece]
+        return self.sums.at[keys_below(self.bits, len(self.bits)).index(sub) * self.pieces + piece]
+
+    def send(self, stage, sub, piece):
+        bit = self.bits[stage]
+        self.came[stage, sub, piece] = self.mail.post(
+            self.current(bit + sub, piece), self.landed.at[self.slot(stage, sub, piece)], bit
+        )
+
+    def start(self, which=None):
+        stage = len(self.bits) - 1
+        for sub in reversed(keys_below(self.bits, stage)):
+            if which is None or (sub != 0) == which:
+                for piece in range(self.pieces):
+                    self.send(stage, sub, piece)
+
+    def take(self, stage, sub, piece):
+        self.came[stage, sub, piece].wait_recv()
+        here = self.current(sub, piece)
+        landed = self.landed.at[self.slot(stage, sub, piece)]
+        if stage == 0:
+            self.add(self.last(piece), here, landed)
+            return
+        place = keys_below(self.bits, len(self.bits)).index(sub) * self.pieces + piece
+        self.add(self.sums.at[place], here, landed)
+        self.added.add((sub, piece))
+        below = self.bits[stage - 1]
+        if (sub // below) % 2:
+            self.send(stage - 1, sub - below, piece)
+
+    def take_away(self, stage, piece):
+        below = self.bits[stage - 1]
+        for sub in keys_below(self.bits, stage):
+            if (sub // below) % 2:
+                self.take(stage, sub, piece)
+
+    def take_here(self, stage, piece):
+        below = self.bits[stage - 1] if stage else 0
+        for sub in keys_below(self.bits, stage):
+            if not stage or not (sub // below) % 2:
+                self.take(stage, sub, piece)
+
+    def finish_piece(self, piece):
+        top = len(self.bits) - 1
+        for stage in range(top, -1, -1):
+            if stage and stage != top:
+                self.take_away(stage, piece)
+            self.take_here(stage, piece)
+
+
+class Total:
+    def __init__(self, mail, near, own, half_a, half_b, in_a, in_b):
+        self.mail, self.near, self.own = mail, near, own
+        self.half_a, self.half_b, self.in_a, self.in_b = half_a, half_b, in_a, in_b
+        self.half = near.shape[1] // 2
+        self.top, self.end = pl.ds(0, self.half), pl.ds(self.half, self.half)
+
+    def first(self):
+        ring = self.mail.ring
+        self.one = self.mail.post(self.near.at[3, self.top], self.half_a, ring.bit_b)
+        self.two = self.mail.post(self.near.at[3, self.end], self.half_b, ring.bit_a)
+
+    def second(self):
+        ring = self.mail.ring
+        self.one.wait_recv()
+        part = self.near.at[1, self.top]
+        add_near(part, part, self.half_a)
+        self.for_a = self.mail.post(self.near.at[1], self.in_a, ring.bit_a)
+        self.two.wait_recv()
+        part = self.near.at[2, self.end]
+        add_near(part, part, self.half_b)
+        self.for_b = self.mail.post(self.near.at[2], self.in_b, ring.bit_b)
+
+    def arrive(self):
+        self.for_a.wait_recv()
+        self.for_b.wait_recv()
+
+    def value(self, part):
+        return self.own[part, :] + self.in_a[part, :].astype(f32) + self.in_b[part, :].astype(f32)
+
+
+def norm_back(total, base, gain):
+    inv = lax.rsqrt(jnp.mean(base * base, axis=-1, keepdims=True) + epsilon)
+    scaled = gain * total
+    grads = inv * scaled - base * inv**3 * jnp.mean(scaled * base, axis=-1, keepdims=True)
+    return grads, total * base * inv
+
+
+def back_kernel(
+    outer, inner, seq_len,
+    x_ref, go_ref, factor_ref, gains_ref, q_ref, k_ref, v_ref, att_ref, w_qkv, w_o, cos_ref, sin_ref,
+    p_gu, p_d, far_two, near_two, act_one, resid_ref,
+    grad_tokens, out_q, out_k, out_v, out_o, gain_grads,
+    out_gate, out_up, out_d, land_gu, land_d, sum_gu, sum_d, fin_gu,
+    near, core_in, far, own_sum, grad_resid, branch,
+    half_a, half_b, in_a, in_b,
+    acts, d_qkv, p_qkv, p_o, p_o_sum, land_qkv, land_o, sum_qkv, sum_o, fin_qkv, qkv_in, gain_in,
+    send_sems, recv_sems, local_sems, core_send, core_recv, far_send, far_recv, act_sems, near_sems,
+):
+    size, width = x_ref.shape
+    rows = out_q.shape[0]
+    hidden_rows = out_d.shape[0]
+    narrow = w_o.shape[0]
+    hidden = p_d.shape[0]
+    ring = Ring(outer, inner, rows)
+    mail = Mail(ring, send_sems, recv_sems, local_sems)
+    ring.greet()
+    bits = ring.data_bits
+    flat = ring.flat
+    strip = 32
+    core_partner = ring.where(ring.bit_core)
+
+    def strips(step):
+        def run(i, carry):
+            step(pl.ds(pl.multiple_of(i * strip, strip), strip))
+            return carry
+
+        lax.fori_loop(0, size // strip, run, 0)
+
+    def by_place(ref, count):
+        return lambda key: [
+            ref.at[pl.ds(pl.multiple_of(ring.place(ring.flip(flat, key)) * count, 16), count)]
+        ]
+
+    def by_runs(ref):
+        return lambda key: [
+            ref.at[pl.ds(pl.multiple_of(start, 16), count)]
+            for start, count in ring.runs(ring.flip(flat, key), rows)
+        ]
+
+    run_rows = ring.runs(flat, rows)[0][1]
+    top_stage = len(bits) - 1
+    collect_gu = Collect(
+        mail, bits, by_runs(p_gu), land_gu, sum_gu,
+        lambda piece: fin_gu.at[pl.ds(piece * run_rows, run_rows)], add_far,
+    )
+    collect_d = Collect(
+        mail, bits, by_place(p_d, hidden_rows), land_d, sum_d, lambda piece: out_d, add_far
+    )
+
+    def core_copy(j):
+        return pltpu.make_async_remote_copy(
+            src_ref=far_two.at[j],
+            dst_ref=core_in.at[j],
+            send_sem=core_send.at[j],
+            recv_sem=core_recv.at[j],
+            device_id=core_partner,
+            device_id_type=MESH,
+        )
+
+    load_resid = mail.keep(resid_ref, grad_resid)
+    order = (3, 1, 2, 0)
+    for j in order:
+        core_copy(j).start()
+        pltpu.make_async_copy(near_two.at[j], near.at[j], near_sems.at[j]).start()
+    collect_gu.start(True)
+    collect_d.start(True)
+    collect_gu.start(False)
+    collect_d.start(False)
+
+    total_two = Total(mail, near, own_sum, half_a, half_b, in_a, in_b)
+    for j in order:
+        pltpu.make_async_copy(near_two.at[j], near.at[j], near_sems.at[j]).wait()
+        core_copy(j).wait_recv()
+        if j:
+            add_near(near.at[j], near.at[j], core_in.at[j])
+        else:
+            add_near(own_sum, near.at[j], core_in.at[j])
+        if j == 3:
+            total_two.first()
+    total_two.second()
+    collect_gu.take_away(top_stage, 0)
+    total_two.arrive()
+
+    gain_grads[...] = jnp.zeros_like(gain_grads)
+    load_resid.wait()
+    mail.kept = [c for c in mail.kept if c is not load_resid]
+
+    def second_norm(part):
+        resid = grad_resid[part, :]
+        grads, terms = norm_back(total_two.value(part), resid, gains_ref[1:2, :])
+        grads = grads + go_ref[part, :].astype(f32) * factor_ref[part, :]
+        grad_resid[part, :] = grads
+        branch[0, part, :] = grads.astype(bf16)
+        gain_grads[1:2, :] = gain_grads[1:2, :] + jnp.sum(terms, axis=0, keepdims=True)
+
+    strips(second_norm)
+    share = Share(mail, branch, branch.at[0])
+    share.first()
+    for piece in range(1, collect_gu.pieces):
+        collect_gu.take_away(top_stage, piece)
+    share.second()
+    share.third()
+    collect_d.take_away(top_stage, 0)
+    p_o_sum[...] = jnp.zeros_like(p_o_sum)
+    for j in range(QUAD):
+        core_copy(j).wait_send()
+    share.done()
+
+    scale = HEAD_DIM**-0.5
+    cosine, sine = cos_ref[...], sin_ref[...]
+    per_block = size // seq_len
+
+    def dot(left, right, left_dim, right_dim):
+        return lax.dot_general(
+            left, right, (((left_dim,), (right_dim,)), ((), ())), preferred_element_type=f32
+        )
+
+    def attend_block(place):
+        grads = branch[place]
+        grad_att = dot(grads, w_o[...], 1, 1).astype(bf16)
+        p_o_sum[...] = p_o_sum[...] + dot(att_ref[place], grads, 0, 0)
+        causal = lax.broadcasted_iota(jnp.int32, (seq_len, seq_len), 1) <= lax.broadcasted_iota(
+            jnp.int32, (seq_len, seq_len), 0
+        )
+        for b in range(per_block):
+            span = slice(b * seq_len, (b + 1) * seq_len)
+            q, k, v = q_ref[place, span], k_ref[place, span], v_ref[place, span]
+            ga = grad_att[span]
+            dq = jnp.zeros((seq_len, narrow), f32)
+            dk = jnp.zeros((seq_len, narrow), f32)
+            dv = jnp.zeros((seq_len, narrow), f32)
+            for head in range(narrow // HEAD_DIM):
+                mask = head_mask(narrow, head)
+                kh = jnp.where(mask, k, jnp.zeros_like(k))
+                vh = jnp.where(mask, v, jnp.zeros_like(v))
+                qh = jnp.where(mask, q, jnp.zeros_like(q))
+                gh = jnp.where(mask, ga, jnp.zeros_like(ga))
+                scores = jnp.where(causal, dot(q, kh, 1, 1) * scale, -1e30)
+                grown = jnp.exp(scores - jnp.max(scores, axis=-1, keepdims=True))
+                soft = grown / jnp.sum(grown, axis=-1, keepdims=True)
+                grad_soft = dot(ga, vh, 1, 1)
+                grad_scores = (
+                    soft * (grad_soft - jnp.sum(soft * grad_soft, axis=-1, keepdims=True))
+                ).astype(bf16)
+                dq = dq + dot(grad_scores, kh, 1, 0)
+                dk = dk + dot(grad_scores, qh, 0, 0)
+                dv = dv + dot(soft.astype(bf16), gh, 0, 0)
+            d_qkv[place, span, :narrow] = turn(dq * scale, cosine, -sine).astype(bf16)
+            d_qkv[place, span, narrow : 2 * narrow] = turn(dk * scale, cosine, -sine).astype(bf16)
+            d_qkv[place, span, 2 * narrow :] = dv.astype(bf16)
+        return dot(d_qkv[place], w_qkv[...], 1, 1)
+
+    def far_copy(j):
+        return pltpu.make_async_remote_copy(
+            src_ref=far.at[j % 2],
+            dst_ref=core_in.at[j],
+            send_sem=far_send.at[j],
+            recv_sem=far_recv.at[j],
+            device_id=core_partner,
+            device_id_type=MESH,
+        )
+
+    def far_step(i, carry):
+        j = QUAD - 1 - i
+        part = attend_block(QUAD + j).astype(bf16)
+
+        @pl.when(i >= 2)
+        def _():
+            far_copy(j + 2).wait_send()
+
+        far[j % 2] = part
+        far_copy(j).start()
+        return carry
+
+    lax.fori_loop(0, QUAD, far_step, 0)
+    for j in range(2):
+        far_copy(j).wait_send()
+    for copy in (total_two.one, total_two.two, total_two.for_a, total_two.for_b):
+        copy.wait_send()
+        mail.sent = [c for c in mail.sent if c is not copy]
+
+    def near_step(i, carry):
+        j = QUAD - 1 - i
+        part = attend_block(j)
+        far_copy(j).wait_recv()
+        own_sum[...] = part + core_in[j].astype(f32)
+        near[j] = own_sum[...].astype(bf16)
+        return carry
+
+    lax.fori_loop(0, QUAD, near_step, 0)
+    total_one = Total(mail, near, own_sum, half_a, half_b, in_a, in_b)
+    total_one.first()
+
+    collect_o = Collect(
+        mail, bits, by_place(p_o, rows), land_o, sum_o, lambda piece: out_o, add_near
+    )
+    collect_qkv = Collect(
+        mail, bits, by_runs(p_qkv), land_qkv, sum_qkv,
+        lambda piece: fin_qkv.at[pl.ds(piece * run_rows, run_rows)], add_near,
+    )
+    p_o[...] = p_o_sum[...].astype(bf16)
+    collect_o.start()
+    cut = acts.shape[3]
+    cuts = width // cut
+    shift = (1 - flat // (ring.count // 2)) * (cuts // 2)
+
+    def chunk_at(i):
+        return pl.multiple_of(((i + shift) % cuts) * cut, cut)
+
+    def act_copy(i):
+        return pltpu.make_async_copy(
+            act_one.at[:, :, pl.ds(chunk_at(i), cut)], acts.at[i % 2], act_sems.at[i % 2]
+        )
+
+    act_copy(0).start()
+
+    def chunk_step(i, carry):
+        act_copy(i).wait()
+
+        @pl.when(i + 1 < cuts)
+        def _():
+            act_copy(i + 1).start()
+
+        left = acts[i % 2].reshape(2 * QUAD * size, cut)
+        right = d_qkv[...].reshape(2 * QUAD * size, 3 * narrow)
+        p_qkv[pl.ds(chunk_at(i), cut), :] = dot(left, right, 0, 0).astype(bf16)
+        return carry
+
+    lax.fori_loop(0, cuts // 2, chunk_step, 0)
+    collect_qkv.start()
+    total_one.second()
+    lax.fori_loop(cuts // 2, cuts, chunk_step, 0)
+
+    for piece in range(collect_gu.pieces):
+        collect_gu.finish_piece(piece)
+    block = ring.span * hidden_rows
+    gu_swap = []
+    team = ring.team(flat)
+    for delta in ring.deltas:
+        other = ring.team(ring.flip(flat, delta))
+        part = pl.ds(pl.multiple_of(other * rows, 16), rows)
+        for j, ref in enumerate((out_gate, out_up)):
+            for y in range(ring.upper_size):
+                for o in range(ring.across):
+                    target = ((y * 2 + team // QUAD) * ring.across + o) * QUAD + team % QUAD
+                    source = j * hidden + (y * ring.across + o) * block
+                    src = fin_gu.at[part, pl.ds(source, block)]
+                    dst = ref.at[:, pl.ds(pl.multiple_of(target * block, 128), block)]
+                    if delta:
+                        gu_swap.append(mail.post(src, dst, delta))
+                    else:
+                        mail.keep(src, dst)
+
+    total_one.arrive()
+
+    def first_norm(part):
+        x = x_ref[part, :].astype(f32)
+        grads, terms = norm_back(total_one.value(part), x, gains_ref[0:1, :])
+        grad_tokens[part, :] = grad_resid[part, :] + grads
+        gain_grads[0:1, :] = gain_grads[0:1, :] + jnp.sum(terms, axis=0, keepdims=True)
+
+    strips(first_norm)
+    collect_d.finish_piece(0)
+
+    collect_o.take_away(top_stage, 0)
+    for piece in range(collect_qkv.pieces):
+        collect_qkv.take_away(top_stage, piece)
+    for step, bit in enumerate([ring.bit_core, ring.bit_a, ring.bit_b] + bits):
+        copy = mail.post(gain_grads, gain_in.at[step], bit)
+        copy.wait()
+        mail.sent = [c for c in mail.sent if c is not copy]
+        gain_grads[...] = gain_grads[...] + gain_in[step]
+    for piece in range(collect_qkv.pieces):
+        collect_qkv.finish_piece(piece)
+    collect_o.finish_piece(0)
+
+    swaps = []
+    for delta in ring.deltas:
+        other = ring.team(ring.flip(flat, delta))
+        src = fin_qkv.at[pl.ds(pl.multiple_of(other * rows, 16), rows)]
+        dst = qkv_in.at[team]
+        if delta:
+            swaps.append(mail.post(src, dst, delta))
+        else:
+            kept = mail.keep(src, dst)
+    kept.wait()
+    mail.kept = [c for c in mail.kept if c is not kept]
+    for copy in swaps:
+        copy.wait_recv()
+    for j, ref in enumerate((out_q, out_k, out_v)):
+        parts = []
+        for y in range(ring.upper_size):
+            for c in range(2):
+                for o in range(ring.across):
+                    for q in range(QUAD):
+                        start = j * narrow + (y * ring.across + o) * HEAD_DIM
+                        parts.append(qkv_in[c * QUAD + q, :, start : start + HEAD_DIM])
+        ref[...] = jnp.concatenate(parts, axis=1).astype(f32)
+    for copy in gu_swap:
+        copy.wait_recv()
+    mail.finish()
+
+
+def back(outer, inner, seq_len, near_args, far_args):
+    tokens, w_qkv, w_o = near_args[0], near_args[8], near_args[9]
+    p_gu, p_d = far_args[0], far_args[1]
+    size, width = tokens.shape
+    narrow = w_o.shape[0]
+    hidden = p_d.shape[0]
+    places = outer * inner // (2 * QUAD)
+    rows = width // (outer * inner)
+    hidden_rows = hidden // places
+    span = max(1, HEAD_DIM // rows)
+    pieces = 2 if span == 1 else 2 * QUAD
+    run_rows = 2 * QUAD * rows // pieces
+    remote = 2 * (places - 1) * (pieces + 1) + 7 + 14 * places // span + 8 + 24
+    local = 8 + 2 * places // span
+    vm = pl.BlockSpec(memory_space=pltpu.VMEM)
+    hbm = pl.BlockSpec(memory_space=pl.ANY)
+    sds = jax.ShapeDtypeStruct
+    out_shape = (
+        sds((size, width), f32),
+        sds((rows, width), f32),
+        sds((rows, width), f32),
+        sds((rows, width), f32),
+        sds((rows, width), f32),
+        sds((8, width), f32),
+        sds((rows, 2 * QUAD * hidden), bf16),
+        sds((rows, 2 * QUAD * hidden), bf16),
+        sds((hidden_rows, width), f32),
+        sds(((places - 1) * pieces, run_rows, 2 * hidden), bf16),
+        sds((places - 1, hidden_rows, width), bf16),
+        sds((places // 2 * pieces, run_rows, 2 * hidden), bf16),
+        sds((places // 2, hidden_rows, width), bf16),
+        sds((2 * QUAD * rows, 2 * hidden), bf16),
+    )
+    wide = pltpu.VMEM((size, width), bf16)
+    half = pltpu.VMEM((size // 2, width), bf16)
+    four = pltpu.VMEM((QUAD, size, width), bf16)
+    cut = min(256, width // 2)
+    four_sems = pltpu.SemaphoreType.DMA((QUAD,))
+    return pl.pallas_call(
+        functools.partial(back_kernel, outer, inner, seq_len),
+        out_shape=out_shape,
+        in_specs=[vm] * len(near_args) + [hbm] * len(far_args),
+        out_specs=tuple([vm] * 6 + [hbm] * 8),
+        scratch_shapes=[
+            four, four, pltpu.VMEM((2, size, width), bf16),
+            pltpu.VMEM((size, width), f32),
+            pltpu.VMEM((size, width), f32),
+            pltpu.VMEM((2 * QUAD, size, width), bf16),
+            half, half, wide, wide,
+            pltpu.VMEM((2, 2 * QUAD, size, cut), bf16),
+            pltpu.VMEM((2 * QUAD, size, 3 * narrow), bf16),
+            pltpu.VMEM((width, 3 * narrow), bf16),
+            pltpu.VMEM((narrow, width), bf16),
+            pltpu.VMEM((narrow, width), f32),
+            pltpu.VMEM(((places - 1) * pieces, run_rows, 3 * narrow), bf16),
+            pltpu.VMEM((places - 1, rows, width), bf16),
+            pltpu.VMEM((places // 2 * pieces, run_rows, 3 * narrow), bf16),
+            pltpu.VMEM((places // 2, rows, width), bf16),
+            pltpu.VMEM((2 * QUAD * rows, 3 * narrow), bf16),
+            pltpu.VMEM((2 * QUAD, rows, 3 * narrow), bf16),
+            pltpu.VMEM((8, 8, width), f32),
+            pltpu.SemaphoreType.DMA((remote,)),
+            pltpu.SemaphoreType.DMA((remote,)),
+            pltpu.SemaphoreType.DMA((local,)),
+            four_sems, four_sems, four_sems, four_sems,
+            pltpu.SemaphoreType.DMA((2,)),
+            four_sems,
+        ],
+        compiler_params=pltpu.CompilerParams(
+            collective_id=1, has_side_effects=True, vmem_limit_bytes=63 * 1024 * 1024
+        ),
+        name="back",
+    )(*near_args, *far_args)
+
+
 def on_device(
     tokens,
     labels,
@@ -764,18 +1281,18 @@
     rows = w_query.shape[0]
     hidden_rows = w_down.shape[0]
     plan = Plan(outer_count, inner_count, rows)
-    x_rows = tokens.reshape(-1, width).astype(f32)
+    x_rows = tokens.reshape(-1, width)
 
     token_total = float(seq_len * batch_size * outer_count * inner_count)
     picked_counts = jnp.sum(
         jnp.where(labels[:, None] == jnp.arange(3)[None, :], counts[None, :], 0), axis=1
     ).astype(f32)
     factor = token_total / (3.0 * picked_counts)
-    cotangent = (grad_out.astype(f32) * factor[:, None, None]).reshape(-1, width)
     cosine, sine = rope_tables(seq_len, HEAD_DIM)
     head_count = width // (2 * QUAD) // HEAD_DIM
-    four_shape = (-1, seq_len, head_count, HEAD_DIM)
     sign = jnp.where(jnp.arange(HEAD_DIM) < HEAD_DIM // 2, -1.0, 1.0)
+    wide_cosine = jnp.tile(cosine, (1, head_count))
+    wide_sine = jnp.tile(sine * sign, (1, head_count))
     gain_rows = lax.dynamic_update_slice(
         jnp.zeros((8, width), f32),
         jnp.stack([gain_attn, gain_mlp]).astype(f32),
@@ -786,20 +1303,14 @@
         act_one, w_qkv, w_o, q_rot, k_rot, values, attended, resid, gains, act_two, dy, w_gu, w_d,
     ) = front(
         outer_count, inner_count, batch_size, seq_len,
-        tokens.reshape(-1, width), grad_out.reshape(-1, width), factor_rows, gain_rows,
+        x_rows, grad_out.reshape(-1, width), factor_rows, gain_rows,
         w_query, w_key, w_value,
-        jnp.tile(cosine, (1, head_count)), jnp.tile(sine * sign, (1, head_count)),
+        wide_cosine, wide_sine,
         w_out, w_gate, w_up, w_down,
     )
     narrow = w_o.shape[0]
     hidden = w_d.shape[0]
-    gain_one, gain_two = gains[0:1], gains[1:2]
-    act_one, act_two, dy = (a.reshape(-1, width) for a in (act_one, act_two, dy))
-    attended = attended.reshape(-1, narrow)
-    q_rot, k_rot, values = (a.reshape(four_shape) for a in (q_rot, k_rot, values))
-    inv_one = lax.rsqrt(jnp.mean(x_rows * x_rows, axis=-1, keepdims=True) + epsilon)
-    inv_two = lax.rsqrt(jnp.mean(resid * resid, axis=-1, keepdims=True) + epsilon)
-
+    act_two, dy = (a.reshape(-1, width) for a in (act_two, dy))
     gu = mm(act_two, w_gu)
     gate_pre, up_proj = gu[:, :hidden], gu[:, hidden:]
     sigmoid_gate = jax.nn.sigmoid(gate_pre)
@@ -812,54 +1323,32 @@
     grad_up_proj = (grad_middle * gate_pre * sigmoid_gate).astype(bf16)
     grad_gu_cols = jnp.concatenate([grad_gate_pre, grad_up_proj], axis=1)
 
-    added = plan.sum_tokens(grad_gu_cols, lambda part: times_transposed(part, w_gu))
-    down_grad = plan.scatter(outer_sum(middle, dy), hidden_rows, False)
-    gu_grad = plan.swap(plan.scatter(outer_sum(act_two, grad_gu_cols), rows, True).astype(bf16))
-    gate_grad = plan.join_columns(gu_grad[:, :, :hidden]).astype(f32)
-    up_grad = plan.join_columns(gu_grad[:, :, hidden:]).astype(f32)
-
+    count = middle.shape[0] // 2
+    four_blocks = (QUAD, -1, width)
+    far_two = times_transposed(grad_gu_cols[count:], w_gu).astype(bf16).reshape(four_blocks)
+    near_two = times_transposed(grad_gu_cols[:count], w_gu).astype(bf16).reshape(four_blocks)
+    p_d = outer_sum(middle, dy).astype(bf16)
+    p_gu = outer_sum(act_two, grad_gu_cols).astype(bf16)
     layer_out = (
         (resid + plan.sum_tokens(middle, lambda part: mm(part, w_d)))
         .astype(bf16)
         .reshape(tokens.shape)
     )
-
-    grad_gain_two = jnp.sum(added * resid * inv_two, axis=0, keepdims=True)
-    scaled_two = gain_two * added
-    grad_resid = (
-        cotangent
-        + inv_two * scaled_two
-        - resid * inv_two**3 * jnp.mean(scaled_two * resid, axis=-1, keepdims=True)
-    )
-    grad_branch = plan.share_tokens(grad_resid.astype(bf16))
-    grad_attended = times_transposed(grad_branch, w_o).astype(bf16).reshape(four_shape)
-    out_grad = plan.scatter(outer_sum(attended, grad_branch), rows, False)
-    grad_q_rot, grad_k_rot, grad_v = attend_back(q_rot, k_rot, values, grad_attended)
-    grad_qkv_cols = jnp.concatenate(
-        [
-            unrotate(grad_q_rot, cosine, sine).reshape(-1, narrow).astype(bf16),
-            unrotate(grad_k_rot, cosine, sine).reshape(-1, narrow).astype(bf16),
-            grad_v.reshape(-1, narrow).astype(bf16),
-        ],
-        axis=1,
-    )
-    qkv_grad = plan.swap(plan.scatter(outer_sum(act_one, grad_qkv_cols), rows, True).astype(bf16))
-    query_grad, key_grad, value_grad = (
-        plan.join_columns(qkv_grad[:, :, i * narrow : (i + 1) * narrow]).astype(f32)
-        for i in range(3)
-    )
-    grad_act_one = plan.sum_tokens(grad_qkv_cols, lambda part: times_transposed(part, w_qkv))
-    grad_gain_one = jnp.sum(grad_act_one * x_rows * inv_one, axis=0, keepdims=True)
-    scaled_one = gain_one * grad_act_one
-    grad_rows = (
-        grad_resid
-        + inv_one * scaled_one
-        - x_rows * inv_one**3 * jnp.mean(scaled_one * x_rows, axis=-1, keepdims=True)
-    )
-    gain_grads = plan.scatter_gains(jnp.concatenate([grad_gain_one, grad_gain_two], axis=0))
+    p_gu, layer_out = lax.optimization_barrier((p_gu, layer_out))
+    results = back(
+        outer_count, inner_count, seq_len,
+        (
+            x_rows, grad_out.reshape(-1, width), factor_rows, gains, q_rot, k_rot, values, attended,
+            w_qkv, w_o, wide_cosine, wide_sine,
+        ),
+        (p_gu, p_d, far_two, near_two, act_one, resid),
+    )
+    grad_tokens, query_grad, key_grad, value_grad, out_grad, gain_grads = results[:6]
+    gate_grad, up_grad, down_grad = (a.astype(f32) for a in results[6:9])
+    gain_grads = lax.dynamic_slice(gain_grads, (0, plan.flat * rows), (2, rows))
     return (
         layer_out,
-        grad_rows.reshape(tokens.shape),
+        grad_tokens.reshape(tokens.shape),
         query_grad,
         key_grad,
         value_grad,

time: 1000 us -> 803 us (0.80)
  Pallas kernels: 344 us -> 633 us
  waiting for transfers between devices: 213 us -> 9.32 us
  local copies, waits for them, and re-layouts: 152 us -> 10.2 us
  matrix products: 179 us -> 121 us
  starting transfers between devices: 52.3 us -> 6.03 us
  other arithmetic: 45.6 us -> 10.7 us
    pallas_call x0 -> x1, Pallas kernels: none -> 289 us  [back(): pl.pallas_call(functools.partial(back_kernel, outer, inner, seq_len), out...]
    ppermute x47 -> x5, waiting for transfers between devices: 213 us -> 9.32 us  [send(): return lax.ppermute(array, AXES, [(r, r ^ bit) for r in range(self.count)])]
    convert_element_type x29 -> x0, local copies, waits for them, and re-layouts: 79 us -> none  [the longest x9 20.1 us: on_device(): plan.join_columns(qkv_grad[:, :, i * narrow:(i + 1) * narrow]).astype(f32)]
    ppermute x47 -> x5, starting transfers between devices: 52.3 us -> 6.03 us  [send(): return lax.ppermute(array, AXES, [(r, r ^ bit) for r in range(self.count)])]
    dot_general x3 -> x0, local copies, waits for them, and re-layouts: 26.1 us -> none  [outer_sum(): lax.dot_general(left, right, (((0,), (0,)), ((), ())), preferred_element_...]
    dot_general x4 -> x2, matrix products: 52.8 us -> 32.5 us  [outer_sum(): lax.dot_general(left, right, (((0,), (0,)), ((), ())), preferred_element_...]
    dot_general x6 -> x3, matrix products: 66 us -> 49.1 us  [times_transposed(): lax.dot_general(left, weight, (((1,), (1,)), ((), ())), preferred_element...]
    dot_general x4 -> x0, matrix products: 14 us -> none  [the longest x1 6.14 us: attend_back(): jnp.einsum('bhqk,bqhd->bkhd', soft.astype(bf16), grad_mixed, preferred_el...]
  transfers between devices with their start and end apart: 47 -> 5, of which waited for: 18 -> 2; matrix products, arithmetic and copies ran while one was open for 31% -> 8% of each run, Pallas kernels for 0% -> 0%
where the time goes in v3:
time: 803 us; the launch traced here: 793 us
  Pallas kernels  633 us (79%)
  matrix products  121 us (15%)
  other arithmetic  10.7 us (1%)
  local copies, waits for them, and re-layouts  10.2 us (1%)
  waiting for transfers between devices  9.32 us (1%)
    pallas_call x1, Pallas kernels, front(): pl.pallas_call(functools.partial(front_kernel, outer, inner, seq_len), ou...  344 us
    pallas_call x1, Pallas kernels, back(): pl.pallas_call(functools.partial(back_kernel, outer, inner, seq_len), out...  289 us
    dot_general x3, matrix products, times_transposed(): lax.dot_general(left, weight, (((1,), (1,)), ((), ())), preferred_element...  49.1 us
    dot_general x3, matrix products, mm(): return jnp.dot(left, right, preferred_element_type=f32)  39.4 us
    dot_general x2, matrix products, outer_sum(): lax.dot_general(left, right, (((0,), (0,)), ((), ())), preferred_element_...  32.5 us
  transfers between devices with their start and end apart: 5, of which 2 were waited for; matrix products, arithmetic and copies ran while one was open for 8% of the time, Pallas kernels for 0%

profile of v3, /device:TPU:1, one launch (start us, length us, event | category | flops | bytes accessed | tf_op | source)
XLA Modules:
  0.0 793.3 jit_solution(3774043967123411000)
XLA Ops:
  1.3 1.3 fusion.28
  3.5 0.8 copy.25.sin_ref
  4.4 0.8 copy.24.cos_ref
  5.3 0.7 maximum_convert_fusion
  6.3 0.7 broadcast_in_dim_reshape.3.factor_ref
  7.0 344.4 %front.1 = (bf16[8,256,2048]{2,1,0:T(8,128)(2,1)}, bf16[2048,768]{1,0:T(8,128)(2,1)}, bf16[256,2048]{1,0:T(8,128)(2,1)}, bf16[8,256,256]{2,1,0:T(8,128)(2,1)}, b...) custom-call(bf16[256,2048]{1,0:T(8,128)(2,1)} %bitcast.32, ...), custom_call_target="tpu_custom_call" | custom-call | tf_op jit(solution)/shard_map/front/pallas_call | solution.py:715
  351.4 24.5 %fusion.34 = f32[2048,2048]{0,1:T(8,128)} fusion(bf16[2048,2048]{1,0:T(8,128)(2,1)} %bitcast.41, bf16[2048,2048]{1,0:T(8,128)(2,1)} %get-tuple-element.38), kind=kOutput, calls=%fused_computation.53 | convolution fusion | flops 17179869184 | bytes 33554432 | tf_op jit(solution)/shard_map/dot_general | solution.py:44
  375.9 19.7 %multiply_convert_fusion.2 = (bf16[2048,1024]{0,1:T(8,128)(2,1)}, bf16[2048,1024]{0,1:T(8,128)(2,1)}, bf16[2048,1024]{0,1:T(8,128)(2,1)}) fusion(f32[2048,2048]{0,1:T(8,128)} %fusion.34, bf16[2048,2048]{1,0:T(8,128)(2,1)} %bitcast.45, bf16[1024,2048]{1,0:T(8,128)(2,1)S(1)} %copy-done.9), kind=kOutput, calls=%fused_computation.9 | convolution fusion | flops 8623489024 | bytes 41943040 | tf_op jit(solution)/shard_map/dot_general | solution.py:52
  395.6 7.9 convolution_convert_fusion.1
  403.5 3.0 collective-permute-start
  406.5 10.4 %convolution_convert_fusion.p_d = bf16[1024,2048]{1,0:T(8,128)(2,1)} fusion(bf16[2048,1024]{0,1:T(8,128)(2,1)S(1)} %copy-done.10, bf16[2048,2048]{1,0:T(8,128)(2,1)S(1)} %bitcast.46), kind=kOutput, calls=%fused_computation.16 | convolution fusion | flops 8592031744 | bytes 16777216 | tf_op jit(solution)/shard_map/dot_general | solution.py:48
  416.9 22.1 %fusion.1.p_gu = bf16[2048,2048]{1,0:T(8,128)(2,1)} fusion(bf16[2048,2048]{1,0:T(8,128)(2,1)S(1)} %bitcast.44, bf16[2048,1024]{0,1:T(8,128)(2,1)} %get-tuple-element.60, bf16[2048,1024]{0,1:T(8,128)(2,1)} %get-tuple-element.59), kind=kOutput, calls=%fused_computation.11 | convolution fusion | flops 17200840704 | bytes 25165824 | tf_op jit(solution)/shard_map/dot_general | solution.py:48
  439.0 7.0 fusion.33
  446.6 1.1 collective-permute-start.3
  447.7 14.8 %fusion.11 = bf16[1024,2048]{1,0:T(8,128)(2,1)} fusion(bf16[2048,2048]{1,0:T(8,128)(2,1)} %get-tuple-element.38, bf16[2048,1024]{0,1:T(8,128)(2,1)} %get-tuple-element.59, bf16[2048,1024]{0,1:T(8,128)(2,1)} %get-tuple-element.60), kind=kOutput, calls=%fused_computation.19 | convolution fusion | flops 8600420352 | bytes 20971520 | tf_op jit(solution)/shard_map/dot_general | solution.py:52
  462.9 1.4 collective-permute-start.4
  464.4 1.0 pad_maximum_fusion.4
  465.4 14.7 %fusion.8 = bf16[1024,2048]{1,0:T(8,128)(2,1)} fusion(bf16[2048,2048]{1,0:T(8,128)(2,1)} %get-tuple-element.38, bf16[2048,1024]{0,1:T(8,128)(2,1)} %get-tuple-element.59, bf16[2048,1024]{0,1:T(8,128)(2,1)} %get-tuple-element.60), kind=kOutput, calls=%fused_computation.18 | convolution fusion | flops 8600420352 | bytes 20971520 | tf_op jit(solution)/shard_map/dot_general | solution.py:52
  480.1 7.3 collective-permute-done.4
  487.4 2.0 collective-permute-done.2
  489.4 1.6 fusion.22
  491.0 289.1 %back.1 = (f32[256,2048]{1,0:T(8,128)}, f32[64,2048]{1,0:T(8,128)}, f32[64,2048]{1,0:T(8,128)}, f32[64,2048]{1,0:T(8,128)}, f32[64,2048]{1,0:T(8,128)}, /*index=...) custom-call(bf16[256,2048]{1,0:T(8,128)(2,1)} %bitcast.33, ...), custom_call_target="tpu_custom_call" | custom-call | tf_op jit(solution)/shard_map/back/pallas_call | solution.py:1226
  780.1 0.9 constant_dynamic-slice_fusion
  781.0 0.5 slice_bitcast_fusion
  781.5 2.7 convert_element_type.95
  784.2 2.8 convert_element_type.96
  787.0 1.3 copy.36
  788.3 0.8 copy.37
  789.1 0.8 copy.38
  789.9 0.8 copy.39
  790.7 0.8 copy.40
  791.5 1.3 copy.41
  (44 shorter events, 1.7 us)
Async XLA Ops:
  6.3 0.7 copy-start.7
  351.4 24.5 %copy-start.9 = (bf16[1024,2048]{1,0:T(8,128)(2,1)S(1)}, bf16[1024,2048]{1,0:T(8,128)(2,1)}, u32[]{:S(2)}) copy-start(bf16[1024,2048]{1,0:T(8,128)(2,1)} %get-tuple-element.37) | copy-start | bytes 12582916
  395.6 10.9 %copy-start.8 = (bf16[8,256,2048]{2,1,0:T(8,128)(2,1)S(1)}, bf16[8,256,2048]{2,1,0:T(8,128)(2,1)}, u32[]{:S(2)}) copy-start(bf16[8,256,2048]{2,1,0:T(8,128)(2,1)} %get-tuple-element.36) | copy-start | bytes 25165828
  395.6 10.9 %copy-start.10 = (bf16[2048,1024]{0,1:T(8,128)(2,1)S(1)}, bf16[2048,1024]{0,1:T(8,128)(2,1)}, u32[]{:S(2)}) copy-start(bf16[2048,1024]{0,1:T(8,128)(2,1)} %get-tuple-element.61) | copy-start | bytes 12582916
  395.6 21.3 %slice-start = ((s8[8388608]{0:T(1024)(128)(4,1)}), s8[4194304]{0:T(1024)(128)(4,1)S(1)}, s32[]{:S(2)}) async-start(s8[8388608]{0:T(1024)(128)(4,1)} %bitcast.42), calls=%async_computation | async-start | bytes 8388608
  403.5 13.4 %slice-start.1 = ((s8[8388608]{0:T(1024)(128)(4,1)}), s8[4194304]{0:T(1024)(128)(4,1)S(1)}, s32[]{:S(2)}) async-start(s8[8388608]{0:T(1024)(128)(4,1)} %bitcast.42), calls=%async_computation.1 | async-start | bytes 8388608
  403.5 35.5 %collective-permute-start = (bf16[1024,2048]{1,0:T(8,128)(2,1)}, bf16[1024,2048]{1,0:T(8,128)(2,1)}, u32[]{:S(2)}, u32[]{:S(2)}) collective-permute-start(bf16[1024,2048]{1,0:T(8,128)(2,1)} %convolution_convert_fusion.1), channel_id=1, source_target_pairs={{0,8},{1,9},{2,10},{3,11},{4,12},{5,13},{6,14},{7,15},{8,0},{9,1},... | collective-permute-start | bytes 12582920 | tf_op jit(solution)/shard_map/ppermute | solution.py:122
  446.2 16.3 %collective-permute-start.1 = (bf16[128,2048]{1,0:T(8,128)(2,1)S(1)}, bf16[128,2048]{1,0:T(8,128)(2,1)S(1)}, u32[]{:S(2)}, u32[]{:S(2)}) collective-permute-start(bf16[128,2048]{1,0:T(8,128)(2,1)S(1)} %get-tuple-element.64), channel_id=1, source_target_pairs={{0,2},{1,3},{2,0},{3,1},{4,6},{5,7},{6,4},{7,5},{8,10},{9,11},{10,... | collective-permute-start | bytes 1572872 | tf_op jit(solution)/shard_map/ppermute | solution.py:122
  446.6 15.9 %collective-permute-start.3 = (bf16[128,2048]{1,0:T(8,128)(2,1)S(1)}, bf16[128,2048]{1,0:T(8,128)(2,1)S(1)}, u32[]{:S(2)}, u32[]{:S(2)}) collective-permute-start(bf16[128,2048]{1,0:T(8,128)(2,1)S(1)} %get-tuple-element.65), channel_id=1, source_target_pairs={{0,1},{1,0},{2,3},{3,2},{4,5},{5,4},{6,7},{7,6},{8,9},{9,8},{10,11... | collective-permute-start | bytes 1572872 | tf_op jit(solution)/shard_map/ppermute | solution.py:122
  462.9 24.5 %collective-permute-start.4 = (bf16[256,2048]{1,0:T(8,128)(2,1)S(1)}, bf16[256,2048]{1,0:T(8,128)(2,1)S(1)}, u32[]{:S(2)}, u32[]{:S(2)}) collective-permute-start(bf16[256,2048]{1,0:T(8,128)(2,1)S(1)} %pad_maximum_fusion.5), channel_id=1, source_target_pairs={{0,2},{1,3},{2,0},{3,1},{4,6},{5,7},{6,4},{7,5},{8,10},{9,11},{10,... | collective-permute-start | bytes 3145736 | tf_op jit(solution)/shard_map/ppermute | solution.py:122
  465.4 24.0 %copy-start = (f32[256,2048]{1,0:T(8,128)S(1)}, f32[256,2048]{1,0:T(8,128)}, u32[]{:S(2)}) copy-start(f32[256,2048]{1,0:T(8,128)} %get-tuple-element.39.resid_ref) | copy-start | bytes 6291460
  465.4 24.0 %collective-permute-start.2 = (bf16[256,2048]{1,0:T(8,128)(2,1)}, bf16[256,2048]{1,0:T(8,128)(2,1)S(1)}, u32[]{:S(2)}, u32[]{:S(2)}) collective-permute-start(bf16[256,2048]{1,0:T(8,128)(2,1)} %pad_maximum_fusion.4), channel_id=1, source_target_pairs={{0,1},{1,0},{2,3},{3,2},{4,5},{5,4},{6,7},{7,6},{8,9},{9,8},{10,11... | collective-permute-start | bytes 3145736 | tf_op jit(solution)/shard_map/ppermute | solution.py:122
  780.1 6.9 copy-start.2
  784.2 4.1 copy-start.6
  784.2 4.9 copy-start.5
  784.2 5.7 copy-start.4
  787.0 3.7 copy-start.3
  787.0 4.5 copy-start.1

commit v4 on v3

v4 whole, which is shorter than its diff:
```python
import functools

import jax
import jax.numpy as jnp
from jax import lax
from jax.experimental import pallas as pl
from jax.experimental.pallas import tpu as pltpu
from jax.sharding import PartitionSpec as P

HEAD_DIM = 64
AXES = ("dp", "fsdp")
QUAD = 4

epsilon = 1e-05
rope_base = 130000.0
bf16 = jnp.bfloat16
f32 = jnp.float32
MESH = pl.DeviceIdType.MESH


def rope_tables(seq_len, head_dim):
    half_dim = head_dim // 2
    frequency = rope_base ** (-(jnp.arange(half_dim).astype(f32) * 2.0) / head_dim)
    angles = jnp.arange(seq_len).astype(f32)[:, None] * frequency[None, :]
    angles = jnp.concatenate([angles, angles], axis=1)
    return (jnp.cos(angles), jnp.sin(angles))


def mm(left, right):
    return jnp.dot(left, right, preferred_element_type=f32)


def outer_sum(left, right):
    return lax.dot_general(left, right, (((0,), (0,)), ((), ())), preferred_element_type=f32)


def times_transposed(left, weight):
    return lax.dot_general(left, weight, (((1,), (1,)), ((), ())), preferred_element_type=f32)


class Plan:
    def __init__(self, outer, inner, rows):
        self.count = outer * inner
        self.bit_a = max(1, HEAD_DIM // rows)
        self.bit_b = 2 * self.bit_a
        self.bit_core = inner
        self.flat = lax.axis_index("dp") * inner + lax.axis_index("fsdp")

    def send(self, array, bit):
        return lax.ppermute(array, AXES, [(r, r ^ bit) for r in range(self.count)])

    def sum_upper(self, total):
        bit = self.count // 2
        rows = total.shape[0] // 2
        here = (self.flat // bit) % 2
        away = lax.dynamic_slice_in_dim(total, (1 - here) * rows, rows, 0)
        kept = lax.dynamic_slice_in_dim(total, here * rows, rows, 0)
        return (kept.astype(f32) + self.send(away, bit).astype(f32)).astype(bf16)

    def sum_four(self, near, core):
        size = near.shape[0] // QUAD
        half = size // 2
        own, for_a, for_b, for_ab = (
            near[i * size : (i + 1) * size] + core[i * size : (i + 1) * size].astype(f32)
            for i in range(QUAD)
        )
        first = self.send(for_ab[:half].astype(bf16), self.bit_b)
        second = self.send(for_ab[half:].astype(bf16), self.bit_a)
        for_a = jnp.concatenate([for_a[:half] + first.astype(f32), for_a[half:]]).astype(bf16)
        for_b = jnp.concatenate([for_b[:half], for_b[half:] + second.astype(f32)]).astype(bf16)
        return (
            own
            + self.send(for_a, self.bit_a).astype(f32)
            + self.send(for_b, self.bit_b).astype(f32)
        )


class Ring:
    def __init__(self, outer, inner, rows):
        self.count = outer * inner
        self.inner = inner
        self.span = max(1, HEAD_DIM // rows)
        self.bit_a = self.span
        self.bit_b = 2 * self.span
        self.bit_core = inner
        self.low = powers(1, self.span)
        self.mid = powers(QUAD * self.span, inner)
        self.upper = powers(2 * inner, self.count)
        self.data_bits = self.low + self.mid + self.upper
        self.deltas = [
            (self.bit_core if t // QUAD else 0) + (t % QUAD) * self.span for t in range(2 * QUAD)
        ]
        self.across = inner // (QUAD * self.span)
        self.upper_size = outer // 2
        self.flat = lax.axis_index("dp") * inner + lax.axis_index("fsdp")

    def flip(self, flat, bits):
        bit = 1
        while bit <= bits:
            if bits & bit:
                flat = flat + bit * (1 - 2 * ((flat // bit) % 2))
            bit *= 2
        return flat

    def where(self, bits):
        other = self.flip(self.flat, bits)
        return (other // self.inner, other % self.inner)

    def team(self, flat):
        return ((flat // self.inner) % 2) * QUAD + (flat // self.span) % QUAD

    def place(self, flat):
        return (
            (flat // (2 * self.inner)) * self.across + (flat % self.inner) // (QUAD * self.span)
        ) * self.span + flat % self.span

    def runs(self, flat, rows):
        lowest = flat - self.span * ((flat // self.span) % QUAD)
        lowest = lowest - self.inner * ((flat // self.inner) % 2)
        found = []
        for core in range(2):
            start = lowest + core * self.inner
            if self.span == 1:
                found.append((start * rows, QUAD * rows))
            else:
                found += [((start + q * self.span) * rows, rows) for q in range(QUAD)]
        return found

    def greet(self):
        partners = self.deltas[1:] + self.data_bits
        barrier = pltpu.get_barrier_semaphore()
        for bits in partners:
            pl.semaphore_signal(barrier, 1, device_id=self.where(bits), device_id_type=MESH)
        pl.semaphore_wait(barrier, len(partners))


def powers(first, end):
    found = []
    while first < end:
        found.append(first)
        first *= 2
    return found


class Mail:
    def __init__(self, ring, send_sems, recv_sems, local_sems):
        self.ring, self.send_sems, self.recv_sems, self.local_sems = ring, send_sems, recv_sems, local_sems
        self.used = 0
        self.used_local = 0
        self.sent = []
        self.kept = []

    def post(self, src, dst, bits):
        copy = pltpu.make_async_remote_copy(
            src_ref=src,
            dst_ref=dst,
            send_sem=self.send_sems.at[self.used],
            recv_sem=self.recv_sems.at[self.used],
            device_id=self.ring.where(bits),
            device_id_type=MESH,
        )
        self.used += 1
        copy.start()
        self.sent.append(copy)
        return copy

    def keep(self, src, dst):
        copy = pltpu.make_async_copy(src, dst, self.local_sems.at[self.used_local])
        self.used_local += 1
        copy.start()
        self.kept.append(copy)
        return copy

    def drop(self, copy):
        self.sent = [c for c in self.sent if c is not copy]

    def finish(self):
        for copy in self.sent:
            copy.wait_send()
        for copy in self.kept:
            copy.wait()


class Spread:
    def __init__(self, mail, views, bits):
        self.mail, self.views, self.bits = mail, views, bits
        self.pieces = len(views(0))
        self.came = {}

    def start(self, key, piece, first):
        ref = self.views(key)[piece]
        for bit in self.bits[first:]:
            self.came[key + bit, piece] = self.mail.post(ref, ref, bit)

    def begin(self, piece=None):
        for p in range(self.pieces) if piece is None else (piece,):
            self.start(0, p, 0)

    def pass_on(self, stage, piece=None):
        for p in range(self.pieces) if piece is None else (piece,):
            for key in keys_below(self.bits, stage):
                key += self.bits[stage]
                self.came.pop((key, p)).wait_recv()
                self.start(key, p, stage + 1)

    def pass_all(self, piece=None):
        for stage in range(len(self.bits) - 1):
            self.pass_on(stage, piece)

    def done(self):
        for copy in self.came.values():
            copy.wait_recv()


def keys_below(bits, stage):
    return [
        sum(b for i, b in enumerate(bits[:stage]) if low >> i & 1) for low in range(2**stage)
    ]


class Adding:
    def __init__(self, mail, ref, came_in, bits):
        self.mail, self.ref, self.came_in, self.bits = mail, ref, came_in, bits
        self.step = 0

    def post(self):
        self.copy = self.mail.post(
            self.ref, self.came_in.at[self.step], self.bits[self.step]
        )

    def take(self):
        self.copy.wait()
        self.mail.drop(self.copy)
        self.ref[...] = self.ref[...] + self.came_in[self.step]
        self.step += 1


class Share:
    def __init__(self, mail, whole, own):
        self.mail, self.whole, self.own = mail, whole, own
        self.core = []

    def first_core(self):
        self.to_core(self.own, 0)

    def first_a(self):
        self.from_a = self.mail.post(self.own, self.whole.at[1], self.mail.ring.bit_a)

    def first_b(self):
        self.from_b = self.mail.post(self.own, self.whole.at[2], self.mail.ring.bit_b)

    def first(self):
        self.first_a()
        self.first_b()
        self.first_core()

    def to_core(self, ref, place):
        self.core.append(
            self.mail.post(ref, self.whole.at[QUAD + place], self.mail.ring.bit_core)
        )

    def second_a(self):
        self.from_a.wait_recv()
        self.to_core(self.whole.at[1], 1)

    def second_b(self):
        self.from_b.wait_recv()
        self.both = self.mail.post(self.whole.at[2], self.whole.at[3], self.mail.ring.bit_a)
        self.to_core(self.whole.at[2], 2)

    def second(self):
        self.second_a()
        self.second_b()

    def third(self):
        self.both.wait_recv()
        self.to_core(self.whole.at[3], 3)

    def done(self, places=range(QUAD)):
        for place in places:
            self.core[place].wait_recv()


def add_near(target, left, right):
    rows = left.shape[0]
    strip = min(32, rows)

    def step(i, carry):
        part = pl.ds(pl.multiple_of(i * strip, strip), strip)
        target[part, :] = (left[part, :].astype(f32) + right[part, :].astype(f32)).astype(
            target.dtype
        )
        return carry

    lax.fori_loop(0, rows // strip, step, 0)


class Total:
    def __init__(self, mail, near, own, mid, in_a, in_b):
        self.mail, self.near, self.own = mail, near, own
        self.mid, self.in_a, self.in_b = mid, in_a, in_b

    def first(self):
        self.over = self.mail.post(self.near.at[3], self.mid, self.mail.ring.bit_a)

    def first_a(self):
        self.for_a = self.mail.post(self.near.at[1], self.in_a, self.mail.ring.bit_a)

    def second(self):
        self.over.wait_recv()
        add_near(self.near.at[2], self.near.at[2], self.mid)
        self.for_b = self.mail.post(self.near.at[2], self.in_b, self.mail.ring.bit_b)

    def arrive(self):
        self.for_a.wait_recv()
        self.for_b.wait_recv()

    def value(self, part):
        return self.own[part, :] + self.in_a[part, :].astype(f32) + self.in_b[part, :].astype(f32)


def head_mask(width, head):
    lanes = lax.broadcasted_iota(jnp.int32, (1, width), 1)
    return (lanes >= head * HEAD_DIM) & (lanes < (head + 1) * HEAD_DIM)


def turn(u, cosine, signed_sine):
    width = u.shape[-1]
    half = HEAD_DIM // 2
    lanes = lax.broadcasted_iota(jnp.int32, (1, width), 1)
    lower = lanes % HEAD_DIM < half
    turned = jnp.where(lower, pltpu.roll(u, width - half, 1), pltpu.roll(u, half, 1))
    return u * cosine + turned * signed_sine


def front_kernel(
    outer, inner, seq_len,
    x_ref, gain_ref, wq_ref, wk_ref, wv_ref, cos_ref, sin_ref,
    wo_ref, wg_ref, wu_ref, wd_ref,
    act_one, w_qkv, w_o, q_out, k_out, v_out, att_out, resid_out, gains_out,
    act_two, w_g, w_u, w_d,
    cut, gain_in, x_all, far, core_in, near, own_sum, mid, in_a, in_b, act_two_own,
    send_sems, recv_sems, local_sems, far_send, far_recv,
):
    rows = wq_ref.shape[0]
    width = wq_ref.shape[1]
    hidden_rows = wd_ref.shape[0]
    narrow = width // (2 * QUAD)
    ring = Ring(outer, inner, rows)
    mail = Mail(ring, send_sems, recv_sems, local_sems)
    ring.greet()
    bits = ring.data_bits
    flat = ring.flat

    def by_place(ref, size, pieces):
        step = size // pieces
        return lambda key: [
            ref.at[
                pl.ds(
                    pl.multiple_of(ring.place(ring.flip(flat, key)) * size + p * step, 16), step
                )
            ]
            for p in range(pieces)
        ]

    def by_runs(ref):
        return lambda key: [
            ref.at[pl.ds(pl.multiple_of(start, 16), size)]
            for start, size in ring.runs(ring.flip(flat, key), rows)
        ]

    def settle(copy):
        copy.wait()
        mail.kept = [c for c in mail.kept if c is not copy]

    mine_o = w_o.at[pl.ds(pl.multiple_of(ring.place(flat) * rows, 16), rows)]
    mine_d = w_d.at[pl.ds(pl.multiple_of(ring.place(flat) * hidden_rows, 16), hidden_rows)]
    keep_o = mail.keep(wo_ref, mine_o)
    keep_d = mail.keep(wd_ref, mine_d)
    keep_x = mail.keep(x_ref, x_all.at[0])

    chunk = HEAD_DIM
    for t in range(2 * QUAD):
        for j, ref in enumerate((wq_ref, wk_ref, wv_ref)):
            parts = []
            for y in range(ring.upper_size):
                for o in range(ring.across):
                    head = ((y * 2 + t // QUAD) * ring.across + o) * QUAD + t % QUAD
                    parts.append(ref[:, head * chunk : (head + 1) * chunk])
            cut[t, :, j * narrow : (j + 1) * narrow] = jnp.concatenate(parts, axis=1)
    here = pl.ds(pl.multiple_of(flat * rows, 16), rows)
    keep_qkv = mail.keep(cut.at[ring.team(flat)], w_qkv.at[here])
    qkv_swap = []
    for delta in ring.deltas[1:]:
        other = ring.flip(flat, delta)
        qkv_swap.append(mail.post(cut.at[ring.team(other)], w_qkv.at[here], delta))

    gains_out[...] = gain_ref[...]
    gains = Adding(
        mail, gains_out, gain_in, [ring.bit_core, ring.bit_a, ring.bit_b] + bits
    )
    gains.post()
    settle(keep_o)
    spread_o = Spread(mail, by_place(w_o, rows, 1), bits)
    spread_o.begin()
    gains.take()
    gains.post()
    share_x = Share(mail, x_all, x_ref)
    share_x.first_core()
    share_x.first_a()
    settle(keep_qkv)
    for copy in qkv_swap:
        copy.wait_recv()
    spread_qkv = Spread(mail, by_runs(w_qkv), bits)
    spread_qkv.begin()
    gains.take()
    gains.post()
    share_x.first_b()
    spread_o.pass_all()

    gains.take()
    gains.post()
    share_x.second_a()
    for piece in range(spread_qkv.pieces):
        spread_qkv.pass_all(piece)
    while gains.step < len(gains.bits) - 1:
        gains.take()
        gains.post()
    spread_d = Spread(mail, by_place(w_d, hidden_rows, 2), bits)
    settle(keep_d)
    share_x.second_b()
    block = ring.span * hidden_rows
    gate_swap, up_swap = [], []
    for ref, whole, swap in ((wg_ref, w_g, gate_swap), (wu_ref, w_u, up_swap)):
        for delta in ring.deltas:
            team = ring.team(ring.flip(flat, delta))
            for y in range(ring.upper_size):
                for o in range(ring.across):
                    source = ((y * 2 + team // QUAD) * ring.across + o) * QUAD + team % QUAD
                    src = ref.at[:, pl.ds(pl.multiple_of(source * block, 128), block)]
                    dst = whole.at[here, pl.ds((y * ring.across + o) * block, block)]
                    if delta:
                        swap.append((mail.post(src, dst, delta), True))
                    else:
                        swap.append((mail.keep(src, dst), False))

    def swapped(swap):
        for copy, remote in swap:
            if remote:
                copy.wait_recv()
            else:
                settle(copy)

    spread_d.begin()
    gains.take()

    size = act_one.shape[1]
    strip = 32

    def norm_block(place):
        def norm_one(i, carry):
            part = pl.ds(pl.multiple_of(i * strip, strip), strip)
            x = x_all[place, part, :].astype(f32)
            inv = lax.rsqrt(jnp.mean(x * x, axis=-1, keepdims=True) + epsilon)
            act_one[place, part, :] = (x * inv * gains_out[0:1, :]).astype(bf16)
            return carry

        lax.fori_loop(0, size // strip, norm_one, 0)

    settle(keep_x)
    share_x.done(range(QUAD - 1))

    def norm_early(i, carry):
        norm_block(lax.rem(i, QUAD - 1) + QUAD * (i // (QUAD - 1)))
        return carry

    lax.fori_loop(0, 2 * (QUAD - 1), norm_early, 0)
    spread_o.done()
    spread_qkv.done()

    scale = HEAD_DIM**-0.5
    cosine, sine = cos_ref[...], sin_ref[...]
    per_block = act_one.shape[1] // seq_len

    def attend_block(place):
        qkv = jnp.dot(act_one[place], w_qkv[...], preferred_element_type=f32)
        causal = lax.broadcasted_iota(jnp.int32, (seq_len, seq_len), 1) <= lax.broadcasted_iota(
            jnp.int32, (seq_len, seq_len), 0
        )
        for b in range(per_block):
            span = slice(b * seq_len, (b + 1) * seq_len)
            q = turn(qkv[span, :narrow], cosine, sine).astype(bf16)
            k = turn(qkv[span, narrow : 2 * narrow], cosine, sine).astype(bf16)
            v = qkv[span, 2 * narrow :].astype(bf16)
            q_out[place, span] = q
            k_out[place, span] = k
            v_out[place, span] = v
            mixed = jnp.zeros((seq_len, narrow), f32)
            for head in range(narrow // HEAD_DIM):
                mask = head_mask(narrow, head)
                kh = jnp.where(mask, k, jnp.zeros_like(k))
                vh = jnp.where(mask, v, jnp.zeros_like(v))
                scores = lax.dot_general(
                    q, kh, (((1,), (1,)), ((), ())), preferred_element_type=f32
                )
                scores = jnp.where(causal, scores * scale, -1e30)
                top = jnp.max(scores, axis=-1, keepdims=True)
                grown = jnp.exp(scores - top)
                soft = (grown / jnp.sum(grown, axis=-1, keepdims=True)).astype(bf16)
                mixed = mixed + jnp.dot(soft, vh, preferred_element_type=f32)
            att_out[place, span] = mixed.astype(bf16)
        return jnp.dot(att_out[place], w_o[...], preferred_element_type=f32)

    def far_copy(j):
        return pltpu.make_async_remote_copy(
            src_ref=far.at[j],
            dst_ref=core_in.at[j],
            send_sem=far_send.at[j],
            recv_sem=far_recv.at[j],
            device_id=ring.where(ring.bit_core),
            device_id_type=MESH,
        )

    def far_step(j, carry):
        far[j] = attend_block(QUAD + j).astype(bf16)
        far_copy(j).start()
        return carry

    def near_step(j, carry):
        part = attend_block(j)
        far_copy(j).wait_recv()
        total = part + core_in[j].astype(f32)
        near[j] = total.astype(bf16)

        @pl.when(j == 0)
        def _():
            own_sum[...] = total

        return carry

    lax.fori_loop(0, QUAD - 1, far_step, 0)
    spread_g = Spread(mail, by_runs(w_g), bits)
    spread_u = Spread(mail, by_runs(w_u), bits)
    swapped(gate_swap)
    spread_g.begin()
    share_x.third()
    lax.fori_loop(0, QUAD - 1, near_step, 0)
    norm_block(QUAD - 1)
    share_x.done((QUAD - 1,))
    norm_block(2 * QUAD - 1)
    far_step(QUAD - 1, 0)
    near_step(QUAD - 1, 0)
    for j in range(QUAD):
        far_copy(j).wait_send()
    total = Total(mail, near, own_sum, mid, in_a, in_b)
    total.first()
    total.first_a()
    swapped(up_swap)
    spread_u.begin()
    for piece in range(spread_d.pieces):
        spread_d.pass_on(0, piece)
    total.second()
    spread_g.pass_on(0, 0)
    total.arrive()

    def norm_two(i, carry):
        part = pl.ds(pl.multiple_of(i * strip, strip), strip)
        resid = (
            x_ref[part, :].astype(f32) + total.value(part)
        )
        resid_out[part, :] = resid
        inv = lax.rsqrt(jnp.mean(resid * resid, axis=-1, keepdims=True) + epsilon)
        act_two_own[part, :] = (resid * inv * gains_out[1:2, :]).astype(bf16)
        return carry

    lax.fori_loop(0, size // strip, norm_two, 0)
    mail.keep(act_two_own, act_two.at[0])
    share_two = Share(mail, act_two, act_two_own)
    share_two.first()
    for piece in range(1, spread_g.pieces):
        spread_g.pass_on(0, piece)
    share_two.second()
    spread_u.pass_on(0)
    share_two.third()
    for stage in range(1, len(bits) - 1):
        for spread in (spread_d, spread_g, spread_u):
            spread.pass_on(stage)
    spread_d.done()
    spread_g.done()
    spread_u.done()
    share_two.done()
    mail.finish()


def front(outer, inner, seq_len, tokens, gain_rows, w_query, w_key, w_value, cosine, signed_sine, w_out, w_gate, w_up, w_down):
    size, width = tokens.shape
    rows, hidden_all = w_gate.shape
    hidden_rows = w_down.shape[0]
    narrow, hidden = width // (2 * QUAD), hidden_all // (2 * QUAD)
    span = max(1, HEAD_DIM // rows)
    places = outer * inner // (2 * QUAD)
    pieces = 2 if span == 1 else 2 * QUAD
    remote = (places - 1) * (3 * pieces + 3) + 7 + 14 * places // span + 8 + 24
    local = 8 + 2 * places // span
    vm = pl.BlockSpec(memory_space=pltpu.VMEM)
    hbm = pl.BlockSpec(memory_space=pl.ANY)
    eight = (2 * QUAD, size)
    sds = jax.ShapeDtypeStruct
    out_shape = (
        sds(eight + (width,), bf16),
        sds((width, 3 * narrow), bf16),
        sds((narrow, width), bf16),
        sds(eight + (narrow,), bf16),
        sds(eight + (narrow,), bf16),
        sds(eight + (narrow,), bf16),
        sds(eight + (narrow,), bf16),
        sds((size, width), f32),
        sds((8, width), f32),
        sds(eight + (width,), bf16),
        sds((width, hidden), bf16),
        sds((width, hidden), bf16),
        sds((hidden, width), bf16),
    )
    return pl.pallas_call(
        functools.partial(front_kernel, outer, inner, seq_len),
        out_shape=out_shape,
        in_specs=[vm] * 7 + [hbm] * 4,
        out_specs=tuple([vm] * 9 + [hbm] * 4),
        scratch_shapes=[
            pltpu.VMEM((2 * QUAD, rows, 3 * narrow), bf16),
            pltpu.VMEM((8, 8, width), f32),
            pltpu.VMEM((2 * QUAD, size, width), bf16),
            pltpu.VMEM((QUAD, size, width), bf16),
            pltpu.VMEM((QUAD, size, width), bf16),
            pltpu.VMEM((QUAD, size, width), bf16),
            pltpu.VMEM((size, width), f32),
            pltpu.VMEM((size, width), bf16),
            pltpu.VMEM((size, width), bf16),
            pltpu.VMEM((size, width), bf16),
            pltpu.VMEM((size, width), bf16),
            pltpu.SemaphoreType.DMA((remote,)),
            pltpu.SemaphoreType.DMA((remote,)),
            pltpu.SemaphoreType.DMA((local,)),
            pltpu.SemaphoreType.DMA((QUAD,)),
            pltpu.SemaphoreType.DMA((QUAD,)),
        ],
        compiler_params=pltpu.CompilerParams(
            collective_id=0, has_side_effects=True, vmem_limit_bytes=60 * 1024 * 1024
        ),
        name="front",
    )(tokens, gain_rows, w_query, w_key, w_value, cosine, signed_sine, w_out, w_gate, w_up, w_down)


def add_far(target, left, right):
    rows, width = left.shape
    strip = min(64, rows)

    def body(left_ref, right_ref, target_ref):
        target_ref[...] = (left_ref[...].astype(f32) + right_ref[...].astype(f32)).astype(
            target_ref.dtype
        )

    spec = pl.BlockSpec((strip, width), lambda i: (i, 0))
    pltpu.emit_pipeline(body, grid=(rows // strip,), in_specs=[spec, spec], out_specs=[spec])(
        left, right, target
    )


class Collect:
    def __init__(self, mail, bits, views, landed, sums, last, add):
        self.mail, self.bits, self.views = mail, bits, views
        self.landed, self.sums, self.last, self.add = landed, sums, last, add
        self.came = {}
        self.added = set()
        self.pieces = len(views(0))

    def slot(self, stage, sub, piece):
        return (2**stage - 1 + keys_below(self.bits, stage).index(sub)) * self.pieces + piece

    def current(self, sub, piece):
        if (sub, piece) not in self.added:
            return self.views(sub)[piece]
        return self.sums.at[keys_below(self.bits, len(self.bits)).index(sub) * self.pieces + piece]

    def send(self, stage, sub, piece):
        bit = self.bits[stage]
        self.came[stage, sub, piece] = self.mail.post(
            self.current(bit + sub, piece), self.landed.at[self.slot(stage, sub, piece)], bit
        )

    def start(self, which=None):
        stage = len(self.bits) - 1
        for sub in reversed(keys_below(self.bits, stage)):
            if which is None or (sub != 0) == which:
                for piece in range(self.pieces):
                    self.send(stage, sub, piece)

    def take(self, stage, sub, piece):
        self.came[stage, sub, piece].wait_recv()
        here = self.current(sub, piece)
        landed = self.landed.at[self.slot(stage, sub, piece)]
        if stage == 0:
            self.add(self.last(piece), here, landed)
            return
        place = keys_below(self.bits, len(self.bits)).index(sub) * self.pieces + piece
        self.add(self.sums.at[place], here, landed)
        self.added.add((sub, piece))
        below = self.bits[stage - 1]
        if (sub // below) % 2:
            self.send(stage - 1, sub - below, piece)

    def take_away(self, stage, piece):
        below = self.bits[stage - 1]
        for sub in keys_below(self.bits, stage):
            if (sub // below) % 2:
                self.take(stage, sub, piece)

    def take_here(self, stage, piece):
        below = self.bits[stage - 1] if stage else 0
        for sub in keys_below(self.bits, stage):
            if not stage or not (sub // below) % 2:
                self.take(stage, sub, piece)

    def finish_piece(self, piece):
        top = len(self.bits) - 1
        for stage in range(top, -1, -1):
            if stage and stage != top:
                self.take_away(stage, piece)
            self.take_here(stage, piece)


def norm_back(total, base, gain):
    inv = lax.rsqrt(jnp.mean(base * base, axis=-1, keepdims=True) + epsilon)
    scaled = gain * total
    grads = inv * scaled - base * inv**3 * jnp.mean(scaled * base, axis=-1, keepdims=True)
    return grads, total * base * inv


def back_kernel(
    outer, inner, seq_len,
    x_ref, go_ref, factor_ref, gains_ref, q_ref, k_ref, v_ref, att_ref, w_qkv, w_o, cos_ref, sin_ref,
    p_g, p_u, half_d, act_one, resid_ref, two_ref,
    out_q, out_k, out_v, out_o, gain_grads,
    out_gate, out_up, out_d, land_g, land_u, land_d, sum_g, sum_u, sum_d, fin_g, fin_u, land_qkv, land_o, grad_tokens,
    near, core_in, far, own_sum, grad_resid, branch,
    mid, in_a, in_b,
    acts, d_qkv, p_qkv, p_o, p_o_sum, sum_qkv, sum_o, fin_qkv, qkv_in, gain_in,
    send_sems, recv_sems, local_sems, far_send, far_recv, act_sems, add_buf, add_sem,
):
    size, width = x_ref.shape
    rows = out_q.shape[0]
    hidden_rows = out_d.shape[0]
    narrow = w_o.shape[0]
    hidden = p_g.shape[1]
    ring = Ring(outer, inner, rows)
    mail = Mail(ring, send_sems, recv_sems, local_sems)
    ring.greet()
    bits = ring.data_bits
    flat = ring.flat
    strip = 32
    core_partner = ring.where(ring.bit_core)

    def strips(step):
        def run(i, carry):
            step(pl.ds(pl.multiple_of(i * strip, strip), strip))
            return carry

        lax.fori_loop(0, size // strip, run, 0)

    def by_place(ref, count):
        return lambda key: [
            ref.at[pl.ds(pl.multiple_of(ring.place(ring.flip(flat, key)) * count, 16), count)]
        ]

    def by_runs(ref):
        return lambda key: [
            ref.at[pl.ds(pl.multiple_of(start, 16), count)]
            for start, count in ring.runs(ring.flip(flat, key), rows)
        ]

    def dot(left, right, left_dim, right_dim):
        return lax.dot_general(
            left, right, (((left_dim,), (right_dim,)), ((), ())), preferred_element_type=f32
        )

    run_rows = ring.runs(flat, rows)[0][1]
    top_stage = len(bits) - 1
    collect_g, collect_u = (
        Collect(
            mail, bits, by_runs(partial), landed, sums,
            lambda piece, last=last: last.at[pl.ds(piece * run_rows, run_rows)], add_far,
        )
        for partial, landed, sums, last in (
            (p_g, land_g, sum_g, fin_g), (p_u, land_u, sum_u, fin_u)
        )
    )
    share_count = half_d.shape[0] // hidden_rows

    def half_place(key):
        place = ring.place(ring.flip(flat, key)) % share_count
        return [half_d.at[pl.ds(pl.multiple_of(place * hidden_rows, 16), hidden_rows)]]

    collect_d = Collect(mail, bits[:-1], half_place, land_d, sum_d, lambda piece: out_d, add_far)

    load_resid = mail.keep(resid_ref, grad_resid)
    load_two = mail.keep(two_ref, own_sum)
    collect_d.start()
    for which in (True, False):
        collect_g.start(which)
        collect_u.start(which)
    gain_grads[...] = jnp.zeros_like(gain_grads)
    for copy in (load_resid, load_two):
        copy.wait()
        mail.kept = [c for c in mail.kept if c is not copy]

    def second_norm(part):
        resid = grad_resid[part, :]
        grads, terms = norm_back(own_sum[part, :], resid, gains_ref[1:2, :])
        grads = grads + go_ref[part, :].astype(f32) * factor_ref[part, :]
        grad_resid[part, :] = grads
        branch[0, part, :] = grads.astype(bf16)
        gain_grads[1:2, :] = gain_grads[1:2, :] + jnp.sum(terms, axis=0, keepdims=True)

    strips(second_norm)
    share = Share(mail, branch, branch.at[0])
    share.first()
    for piece in range(collect_g.pieces):
        collect_g.take_away(top_stage, piece)
    share.second()
    for piece in range(collect_u.pieces):
        collect_u.take_away(top_stage, piece)
    share.third()
    p_o_sum[...] = jnp.zeros_like(p_o_sum)
    share.done()

    scale = HEAD_DIM**-0.5
    cosine, sine = cos_ref[...], sin_ref[...]
    per_block = size // seq_len

    def attend_block(place):
        grads = branch[place]
        grad_att = dot(grads, w_o[...], 1, 1).astype(bf16)
        p_o_sum[...] = p_o_sum[...] + dot(att_ref[place], grads, 0, 0)
        causal = lax.broadcasted_iota(jnp.int32, (seq_len, seq_len), 1) <= lax.broadcasted_iota(
            jnp.int32, (seq_len, seq_len), 0
        )
        for b in range(per_block):
            span = slice(b * seq_len, (b + 1) * seq_len)
            q, k, v = q_ref[place, span], k_ref[place, span], v_ref[place, span]
            ga = grad_att[span]
            dq = jnp.zeros((seq_len, narrow), f32)
            dk = jnp.zeros((seq_len, narrow), f32)
            dv = jnp.zeros((seq_len, narrow), f32)
            for head in range(narrow // HEAD_DIM):
                mask = head_mask(narrow, head)
                kh = jnp.where(mask, k, jnp.zeros_like(k))
                vh = jnp.where(mask, v, jnp.zeros_like(v))
                qh = jnp.where(mask, q, jnp.zeros_like(q))
                gh = jnp.where(mask, ga, jnp.zeros_like(ga))
                scores = jnp.where(causal, dot(q, kh, 1, 1) * scale, -1e30)
                grown = jnp.exp(scores - jnp.max(scores, axis=-1, keepdims=True))
                soft = grown / jnp.sum(grown, axis=-1, keepdims=True)
                grad_soft = dot(ga, vh, 1, 1)
                grad_scores = (
                    soft * (grad_soft - jnp.sum(soft * grad_soft, axis=-1, keepdims=True))
                ).astype(bf16)
                dq = dq + dot(grad_scores, kh, 1, 0)
                dk = dk + dot(grad_scores, qh, 0, 0)
                dv = dv + dot(soft.astype(bf16), gh, 0, 0)
            d_qkv[place, span, :narrow] = turn(dq * scale, cosine, -sine).astype(bf16)
            d_qkv[place, span, narrow : 2 * narrow] = turn(dk * scale, cosine, -sine).astype(bf16)
            d_qkv[place, span, 2 * narrow :] = dv.astype(bf16)
        return dot(d_qkv[place], w_qkv[...], 1, 1)

    def far_copy(j):
        return pltpu.make_async_remote_copy(
            src_ref=far.at[j % 2],
            dst_ref=core_in.at[j],
            send_sem=far_send.at[j],
            recv_sem=far_recv.at[j],
            device_id=core_partner,
            device_id_type=MESH,
        )

    def far_step(i, carry):
        j = QUAD - 1 - i
        part = attend_block(QUAD + j).astype(bf16)

        @pl.when(i >= 2)
        def _():
            far_copy(j + 2).wait_send()

        far[j % 2] = part
        far_copy(j).start()
        return carry

    lax.fori_loop(0, QUAD, far_step, 0)
    for j in range(2):
        far_copy(j).wait_send()
    def near_step(i, carry):
        j = QUAD - 1 - i
        part = attend_block(j)
        far_copy(j).wait_recv()
        own_sum[...] = part + core_in[j].astype(f32)
        near[j] = own_sum[...].astype(bf16)
        return carry

    lax.fori_loop(0, QUAD, near_step, 0)
    total_one = Total(mail, near, own_sum, mid, in_a, in_b)
    total_one.first()
    total_one.first_a()

    def add_mixed(target, left, landed):
        count, across = landed.shape
        buffer = add_buf.at[pl.ds(0, count), pl.ds(0, across)]
        copy = pltpu.make_async_copy(landed, buffer, add_sem.at[0])
        copy.start()
        copy.wait()
        add_near(target, left, buffer)

    collect_o = Collect(
        mail, bits, by_place(p_o, rows), land_o, sum_o, lambda piece: out_o, add_mixed
    )
    collect_qkv = Collect(
        mail, bits, by_runs(p_qkv), land_qkv, sum_qkv,
        lambda piece: fin_qkv.at[pl.ds(piece * run_rows, run_rows)], add_mixed,
    )
    p_o[...] = p_o_sum[...].astype(bf16)
    collect_o.start()
    cut = acts.shape[3]
    cuts = width // cut
    shift = (1 - flat // (ring.count // 2)) * (cuts // 2)

    def chunk_at(i):
        return pl.multiple_of(((i + shift) % cuts) * cut, cut)

    def act_copy(i):
        return pltpu.make_async_copy(
            act_one.at[:, :, pl.ds(chunk_at(i), cut)], acts.at[i % 2], act_sems.at[i % 2]
        )

    act_copy(0).start()

    def chunk_step(i, carry):
        act_copy(i).wait()

        @pl.when(i + 1 < cuts)
        def _():
            act_copy(i + 1).start()

        left = acts[i % 2].reshape(2 * QUAD * size, cut)
        right = d_qkv[...].reshape(2 * QUAD * size, 3 * narrow)
        p_qkv[pl.ds(chunk_at(i), cut), :] = dot(left, right, 0, 0).astype(bf16)
        return carry

    lax.fori_loop(0, cuts // 2, chunk_step, 0)
    collect_qkv.start()
    total_one.second()
    lax.fori_loop(cuts // 2, cuts, chunk_step, 0)
    if len(bits) > 2:
        collect_d.take_away(top_stage - 1, 0)
    collect_d.finish_piece(0)

    block = ring.span * hidden_rows
    gu_swap = []
    team = ring.team(flat)

    def hand_out(last, ref):
        for delta in ring.deltas:
            other = ring.team(ring.flip(flat, delta))
            part = pl.ds(pl.multiple_of(other * rows, 16), rows)
            for y in range(ring.upper_size):
                for o in range(ring.across):
                    target = ((y * 2 + team // QUAD) * ring.across + o) * QUAD + team % QUAD
                    src = last.at[part, pl.ds((y * ring.across + o) * block, block)]
                    dst = ref.at[:, pl.ds(pl.multiple_of(target * block, 128), block)]
                    if delta:
                        gu_swap.append(mail.post(src, dst, delta))
                    else:
                        mail.keep(src, dst)

    for piece in range(collect_g.pieces):
        collect_g.finish_piece(piece)
    hand_out(fin_g, out_gate)
    collect_o.take_away(top_stage, 0)
    for piece in range(collect_qkv.pieces):
        collect_qkv.take_away(top_stage, piece)
    for piece in range(collect_u.pieces):
        collect_u.finish_piece(piece)
    hand_out(fin_u, out_up)
    total_one.arrive()

    def first_norm(part):
        x = x_ref[part, :].astype(f32)
        grads, terms = norm_back(total_one.value(part), x, gains_ref[0:1, :])
        grad_resid[part, :] = grad_resid[part, :] + grads
        gain_grads[0:1, :] = gain_grads[0:1, :] + jnp.sum(terms, axis=0, keepdims=True)

    strips(first_norm)
    mail.keep(grad_resid, grad_tokens)
    for step, bit in enumerate([ring.bit_core, ring.bit_a, ring.bit_b] + bits):
        copy = mail.post(gain_grads, gain_in.at[step], bit)
        copy.wait()
        mail.sent = [c for c in mail.sent if c is not copy]
        gain_grads[...] = gain_grads[...] + gain_in[step]
    for piece in range(collect_qkv.pieces):
        collect_qkv.finish_piece(piece)
    collect_o.finish_piece(0)

    swaps = []
    for delta in ring.deltas:
        other = ring.team(ring.flip(flat, delta))
        src = fin_qkv.at[pl.ds(pl.multiple_of(other * rows, 16), rows)]
        dst = qkv_in.at[team]
        if delta:
            swaps.append(mail.post(src, dst, delta))
        else:
            kept = mail.keep(src, dst)
    kept.wait()
    mail.kept = [c for c in mail.kept if c is not kept]
    for copy in swaps:
        copy.wait_recv()
    for j, ref in enumerate((out_q, out_k, out_v)):
        parts = []
        for y in range(ring.upper_size):
            for c in range(2):
                for o in range(ring.across):
                    for q in range(QUAD):
                        start = j * narrow + (y * ring.across + o) * HEAD_DIM
                        parts.append(qkv_in[c * QUAD + q, :, start : start + HEAD_DIM])
        ref[...] = jnp.concatenate(parts, axis=1).astype(f32)
    for copy in gu_swap:
        copy.wait_recv()
    mail.finish()


def back(outer, inner, seq_len, near_args, far_args):
    tokens, w_qkv, w_o = near_args[0], near_args[8], near_args[9]
    size, width = tokens.shape
    narrow = w_o.shape[0]
    hidden = far_args[0].shape[1]
    places = outer * inner // (2 * QUAD)
    rows = width // (outer * inner)
    hidden_rows = hidden // places
    span = max(1, HEAD_DIM // rows)
    pieces = 2 if span == 1 else 2 * QUAD
    run_rows = 2 * QUAD * rows // pieces
    remote = (places - 1) * (3 * pieces + 2) + 7 + 14 * places // span + 8 + 24
    local = 8 + 2 * places // span
    vm = pl.BlockSpec(memory_space=pltpu.VMEM)
    hbm = pl.BlockSpec(memory_space=pl.ANY)
    sds = jax.ShapeDtypeStruct
    out_shape = (
        sds((rows, width), f32),
        sds((rows, width), f32),
        sds((rows, width), f32),
        sds((rows, width), f32),
        sds((8, width), f32),
        sds((rows, 2 * QUAD * hidden), bf16),
        sds((rows, 2 * QUAD * hidden), bf16),
        sds((hidden_rows, width), f32),
        sds(((places - 1) * pieces, run_rows, hidden), bf16),
        sds(((places - 1) * pieces, run_rows, hidden), bf16),
        sds((places // 2, hidden_rows, width), bf16),
        sds((places // 2 * pieces, run_rows, hidden), bf16),
        sds((places // 2 * pieces, run_rows, hidden), bf16),
        sds((places // 2, hidden_rows, width), bf16),
        sds((2 * QUAD * rows, hidden), bf16),
        sds((2 * QUAD * rows, hidden), bf16),
        sds(((places - 1) * pieces, run_rows, 3 * narrow), bf16),
        sds((places - 1, rows, width), bf16),
        sds((size, width), f32),
    )
    wide = pltpu.VMEM((size, width), bf16)
    four = pltpu.VMEM((QUAD, size, width), bf16)
    cut = min(256, width // 2)
    four_sems = pltpu.SemaphoreType.DMA((QUAD,))
    return pl.pallas_call(
        functools.partial(back_kernel, outer, inner, seq_len),
        out_shape=out_shape,
        in_specs=[vm] * len(near_args) + [hbm] * len(far_args),
        out_specs=tuple([vm] * 5 + [hbm] * 14),
        scratch_shapes=[
            four, four, pltpu.VMEM((2, size, width), bf16),
            pltpu.VMEM((size, width), f32),
            pltpu.VMEM((size, width), f32),
            pltpu.VMEM((2 * QUAD, size, width), bf16),
            wide, wide, wide,
            pltpu.VMEM((2, 2 * QUAD, size, cut), bf16),
            pltpu.VMEM((2 * QUAD, size, 3 * narrow), bf16),
            pltpu.VMEM((width, 3 * narrow), bf16),
            pltpu.VMEM((narrow, width), bf16),
            pltpu.VMEM((narrow, width), f32),
            pltpu.VMEM((places // 2 * pieces, run_rows, 3 * narrow), bf16),
            pltpu.VMEM((places // 2, rows, width), bf16),
            pltpu.VMEM((2 * QUAD * rows, 3 * narrow), bf16),
            pltpu.VMEM((2 * QUAD, rows, 3 * narrow), bf16),
            pltpu.VMEM((8, 8, width), f32),
            pltpu.SemaphoreType.DMA((remote,)),
            pltpu.SemaphoreType.DMA((remote,)),
            pltpu.SemaphoreType.DMA((local,)),
            four_sems, four_sems,
            pltpu.SemaphoreType.DMA((2,)),
            pltpu.VMEM((run_rows, width), bf16),
            pltpu.SemaphoreType.DMA((1,)),
        ],
        compiler_params=pltpu.CompilerParams(
            collective_id=1, has_side_effects=True, vmem_limit_bytes=63 * 1024 * 1024
        ),
        name="back",
    )(*near_args, *far_args)


def on_device(
    tokens,
    labels,
    counts,
    grad_out,
    w_query,
    w_key,
    w_value,
    w_out,
    gain_attn,
    gain_mlp,
    w_gate,
    w_up,
    w_down,
):
    batch_size, seq_len, width = tokens.shape
    outer_count = lax.axis_size("dp")
    inner_count = lax.axis_size("fsdp")
    rows = w_query.shape[0]
    hidden_rows = w_down.shape[0]
    plan = Plan(outer_count, inner_count, rows)
    x_rows = tokens.reshape(-1, width)

    token_total = float(seq_len * batch_size * outer_count * inner_count)
    picked_counts = jnp.sum(
        jnp.where(labels[:, None] == jnp.arange(3)[None, :], counts[None, :], 0), axis=1
    ).astype(f32)
    factor = token_total / (3.0 * picked_counts)
    cosine, sine = rope_tables(seq_len, HEAD_DIM)
    head_count = width // (2 * QUAD) // HEAD_DIM
    sign = jnp.where(jnp.arange(HEAD_DIM) < HEAD_DIM // 2, -1.0, 1.0)
    wide_cosine = jnp.tile(cosine, (1, head_count))
    wide_sine = jnp.tile(sine * sign, (1, head_count))
    gain_rows = lax.dynamic_update_slice(
        jnp.zeros((8, width), f32),
        jnp.stack([gain_attn, gain_mlp]).astype(f32),
        (0, plan.flat * rows),
    )
    factor_rows = jnp.repeat(factor, seq_len)[:, None]
    (
        act_one, w_qkv, w_o, q_rot, k_rot, values, attended, resid, gains, act_two, w_g, w_u, w_d,
    ) = front(
        outer_count, inner_count, seq_len,
        x_rows, gain_rows,
        w_query, w_key, w_value,
        wide_cosine, wide_sine,
        w_out, w_gate, w_up, w_down,
    )
    narrow = w_o.shape[0]
    hidden = w_d.shape[0]
    act_two = act_two.reshape(-1, width)
    dy_own = (grad_out.reshape(-1, width).astype(f32) * factor_rows).astype(bf16)
    dy_own, act_two = lax.optimization_barrier((dy_own, act_two))
    held = lax.optimization_barrier
    count = act_two.shape[0] // 2
    dy_a, dy_b = plan.send(dy_own, plan.bit_a), plan.send(dy_own, plan.bit_b)
    gate_pre, up_proj = mm(act_two, w_g), mm(act_two, w_u)
    gate_pre, up_proj, dy_a, dy_b = held((gate_pre, up_proj, dy_a, dy_b))

    half = dy_a.shape[0] // 2
    dy_first, dy_second = plan.send(dy_a[:half], plan.bit_b), plan.send(dy_b[half:], plan.bit_a)
    sigmoid_gate = jax.nn.sigmoid(gate_pre)
    middle = (gate_pre * sigmoid_gate * up_proj).astype(bf16)
    down_far = mm(middle[count:], w_d).astype(bf16)
    down_far, dy_first, dy_second = held((down_far, dy_first, dy_second))

    dy_near = jnp.concatenate([dy_own, dy_a, dy_b, dy_first, dy_second], axis=0)
    dy_far = plan.send(dy_near, plan.bit_core)
    down_near = mm(middle[:count], w_d)
    down_near, dy_far = held((down_near, dy_far))
    dy = jnp.concatenate([dy_near, dy_far], axis=0)
    down_core = plan.send(down_far, plan.bit_core)
    grad_middle = times_transposed(dy, w_d)
    grad_gate_pre = (
        grad_middle * up_proj * sigmoid_gate * (1.0 + gate_pre * (1.0 - sigmoid_gate))
    ).astype(bf16)
    grad_up_proj = (grad_middle * gate_pre * sigmoid_gate).astype(bf16)
    grad_gate_pre, grad_up_proj, down_core = held((grad_gate_pre, grad_up_proj, down_core))

    def back_two(part):
        return times_transposed(grad_gate_pre[part], w_g) + times_transposed(
            grad_up_proj[part], w_u
        )

    down = plan.sum_four(down_near, down_core)
    two_far = back_two(slice(count, None)).astype(bf16)
    two_far, middle, dy = held((two_far, middle, dy))
    two_core = plan.send(two_far, plan.bit_core)
    p_d = outer_sum(middle, dy).astype(bf16)
    p_d, two_core = held((p_d, two_core))
    half_d = plan.sum_upper(p_d)
    added = plan.sum_four(back_two(slice(0, count)), two_core)
    p_g = outer_sum(act_two, grad_gate_pre).astype(bf16)
    p_u = outer_sum(act_two, grad_up_proj).astype(bf16)
    layer_out = (resid + down).astype(bf16).reshape(tokens.shape)
    added, layer_out = held((added, layer_out))
    results = back(
        outer_count, inner_count, seq_len,
        (
            x_rows, grad_out.reshape(-1, width), factor_rows, gains, q_rot, k_rot, values, attended,
            w_qkv, w_o, wide_cosine, wide_sine,
        ),
        (p_g, p_u, half_d, act_one, resid, added),
    )
    query_grad, key_grad, value_grad, out_grad, gain_grads = results[:5]
    gate_grad, up_grad, down_grad = (a.astype(f32) for a in results[5:8])
    grad_tokens = results[-1]
    gain_grads = lax.dynamic_slice(gain_grads, (0, plan.flat * rows), (2, rows))
    return (
        layer_out,
        grad_tokens.reshape(tokens.shape),
        query_grad,
        key_grad,
        value_grad,
        out_grad,
        gain_grads[0],
        gain_grads[1],
        gate_grad,
        up_grad,
        down_grad,
    )


def solution(mesh):
    rows = P(AXES, None)
    vector = P(AXES)
    three = P(AXES, None, None)
    in_specs = (three, vector, P(), three, rows, rows, rows, rows, vector, vector, rows, rows, rows)
    out_specs = (three, three, rows, rows, rows, rows, vector, vector, rows, rows, rows)
    return jax.shard_map(
        on_device, mesh=mesh, in_specs=in_specs, out_specs=out_specs, check_vma=False
    )
```

time: 803 us -> 785 us (0.978)
  Pallas kernels: 633 us -> 522 us
  matrix products: 121 us -> 150 us
  waiting for transfers between devices: 9.32 us -> 35 us
  other arithmetic: 10.7 us -> 30.2 us
  local copies, waits for them, and re-layouts: 10.2 us -> 24.1 us
    pallas_call x1, Pallas kernels: 344 us -> 279 us  [front(): pl.pallas_call(functools.partial(front_kernel, outer, inner, seq_len), ou...]
    pallas_call x1, Pallas kernels: 289 us -> 242 us  [back(): pl.pallas_call(functools.partial(back_kernel, outer, inner, seq_len), out...]
    ppermute x5 -> x16, waiting for transfers between devices: 9.32 us -> 35 us  [send(): return lax.ppermute(array, AXES, [(r, r ^ bit) for r in range(self.count)])]
    dot_general x3 -> x5, matrix products: 49.1 us -> 62.7 us  [times_transposed(): lax.dot_general(left, weight, (((1,), (1,)), ((), ())), preferred_element...]
    dot_general x2 -> x3, matrix products: 32.5 us -> 41.4 us  [outer_sum(): lax.dot_general(left, right, (((0,), (0,)), ((), ())), preferred_element_...]
    dot_general x3 -> x4, matrix products: 39.4 us -> 45.8 us  [mm(): return jnp.dot(left, right, preferred_element_type=f32)]
  transfers between devices with their start and end apart: 5 -> 16, of which waited for: 2 -> 5; matrix products, arithmetic and copies ran while one was open for 8% -> 18% of each run, Pallas kernels for 0% -> 0%
where the time goes in v4:
time: 785 us; the launch traced here: 775 us
  Pallas kernels  522 us (66%)
  matrix products  150 us (19%)
  waiting for transfers between devices  35 us (4%)
  other arithmetic  30.2 us (4%)
  local copies, waits for them, and re-layouts  24.1 us (3%)
  starting transfers between devices  11 us (1%)
    pallas_call x1, Pallas kernels, front(): pl.pallas_call(functools.partial(front_kernel, outer, inner, seq_len), ou...  279 us
    pallas_call x1, Pallas kernels, back(): pl.pallas_call(functools.partial(back_kernel, outer, inner, seq_len), out...  242 us
    dot_general x5, matrix products, times_transposed(): lax.dot_general(left, weight, (((1,), (1,)), ((), ())), preferred_element...  62.7 us
    dot_general x4, matrix products, mm(): return jnp.dot(left, right, preferred_element_type=f32)  45.8 us
    dot_general x3, matrix products, outer_sum(): lax.dot_general(left, right, (((0,), (0,)), ((), ())), preferred_element_...  41.4 us
    ppermute x16, waiting for transfers between devices, send(): return lax.ppermute(array, AXES, [(r, r ^ bit) for r in range(self.count)])  35 us
  transfers between devices with their start and end apart: 16, of which 5 were waited for; matrix products, arithmetic and copies ran while one was open for 18% of the time, Pallas kernels for 0%

profile of v4, /device:TPU:1, one launch (start us, length us, event | category | flops | bytes accessed | tf_op | source)
XLA Modules:
  0.0 774.6 jit_solution(9412648655008258000)
XLA Ops:
  5.9 1.4 multiply_convert_fusion.3
  8.4 279.4 %front.1 = (bf16[8,256,2048]{2,1,0:T(8,128)(2,1)}, bf16[2048,768]{1,0:T(8,128)(2,1)}, bf16[256,2048]{1,0:T(8,128)(2,1)}, bf16[8,256,256]{2,1,0:T(8,128)(2,1)}, b...) custom-call(bf16[256,2048]{1,0:T(8,128)(2,1)} %bitcast.38, ...), custom_call_target="tpu_custom_call" | custom-call | tf_op jit(solution)/shard_map/front/pallas_call | solution.py:624
  288.2 12.8 %fusion.23 = f32[2048,1024]{1,0:T(8,128)S(1)} fusion(bf16[2048,2048]{1,0:T(8,128)(2,1)} %bitcast.45, bf16[2048,1024]{1,0:T(8,128)(2,1)} %get-tuple-element.57), kind=kOutput, calls=%fused_computation.77 | convolution fusion | flops 8589934592 | bytes 20971520 | tf_op jit(solution)/shard_map/dot_general | solution.py:30
  301.0 16.0 %fusion.24 = f32[2048,1024]{1,0:T(8,128)S(1)} fusion(bf16[2048,2048]{1,0:T(8,128)(2,1)S(1)} %bitcast.47, bf16[2048,1024]{1,0:T(8,128)(2,1)} %get-tuple-element.58), kind=kOutput, calls=%fused_computation.78 | convolution fusion | flops 8589934592 | bytes 20971520 | tf_op jit(solution)/shard_map/dot_general | solution.py:30
  317.0 1.8 constant_dynamic-update-slice_fusion.4
  318.9 1.5 collective-permute-start.2
  321.6 2.9 multiply_convert_fusion.2
  324.6 6.5 convolution_convert_fusion.1
  331.1 1.7 constant_dynamic-update-slice_fusion.3
  332.7 1.6 constant_dynamic-update-slice_fusion.2
  337.7 10.6 %fusion.3 = f32[1024,2048]{1,0:T(8,128)} fusion(bf16[1024,2048]{1,0:T(8,128)(2,1)} %get-tuple-element.63, bf16[2048,1024]{1,0:T(8,128)(2,1)} %copy-done.3), kind=kOutput, calls=%fused_computation.18 | convolution fusion | flops 4294967296 | bytes 14680064 | tf_op jit(solution)/shard_map/dot_general | solution.py:30
  348.3 2.5 collective-permute-done.4
  350.8 4.7 constant_dynamic-update-slice_fusion.5
  355.5 22.0 %multiply_convert_fusion = (bf16[2048,1024]{1,0:T(8,128)(2,1)}, bf16[2048,1024]{1,0:T(8,128)(2,1)}) fusion(f32[2048,1024]{1,0:T(8,128)} %copy-done, f32[2048,1024]{1,0:T(8,128)} %copy-done.1, bf16[2048,2048]{1,0:T(8,128)(2,1)} %constant_dynamic-update-slice_fusion.5, bf16[1024,2048]{1,0:T(8,128)(2,1)} %get-tuple-element.63), kind=kOutput, calls=%fused_computation.1 | convolution fusion | flops 8617197568 | bytes 37748736 | tf_op jit(solution)/shard_map/dot_general | solution.py:38
  377.6 12.2 %fusion.9 = f32[1024,2048]{1,0:T(8,128)} fusion(bf16[2048,1024]{1,0:T(8,128)(2,1)} %get-tuple-element.58, bf16[2048,1024]{1,0:T(8,128)(2,1)} %get-tuple-element.69), kind=kOutput, calls=%fused_computation.28 | convolution fusion | flops 4294967296 | bytes 14680064 | tf_op jit(solution)/shard_map/dot_general | solution.py:38
  389.8 6.9 fusion.6
  396.7 12.9 %convolution_convert_fusion.3.p_g = bf16[2048,1024]{1,0:T(8,128)(2,1)} fusion(bf16[2048,2048]{1,0:T(8,128)(2,1)S(1)} %bitcast.50, bf16[2048,1024]{1,0:T(8,128)(2,1)} %get-tuple-element.68), kind=kOutput, calls=%fused_computation.10 | convolution fusion | flops 8592031744 | bytes 16777216 | tf_op jit(solution)/shard_map/dot_general | solution.py:34
  409.6 11.8 %add_convert_fusion = bf16[1024,2048]{1,0:T(8,128)(2,1)} fusion(f32[1024,2048]{1,0:T(8,128)} %fusion.6, bf16[2048,1024]{1,0:T(8,128)(2,1)} %get-tuple-element.57, bf16[2048,1024]{1,0:T(8,128)(2,1)} %get-tuple-element.68), kind=kOutput, calls=%fused_computation | convolution fusion | flops 4299161600 | bytes 18874368 | tf_op jit(solution)/shard_map/dot_general | solution.py:38
  424.7 9.8 %convolution_add_fusion = f32[1024,2048]{1,0:T(8,128)S(1)} fusion(f32[1024,2048]{1,0:T(8,128)} %fusion.9, bf16[2048,1024]{1,0:T(8,128)(2,1)} %get-tuple-element.57, bf16[2048,1024]{1,0:T(8,128)(2,1)} %get-tuple-element.68), kind=kOutput, calls=%fused_computation.6 | convolution fusion | flops 4297064448 | bytes 23068672 | tf_op jit(solution)/shard_map/dot_general | solution.py:38
  434.5 14.4 %convolution_convert_fusion = bf16[1024,2048]{1,0:T(8,128)(2,1)} fusion(bf16[2048,1024]{1,0:T(8,128)(2,1)} %copy-done.3, bf16[2048,2048]{1,0:T(8,128)(2,1)} %constant_dynamic-update-slice_fusion.5), kind=kOutput, calls=%fused_computation.7 | convolution fusion | flops 8592031744 | bytes 16777216 | tf_op jit(solution)/shard_map/dot_general | solution.py:34
  452.7 3.0 slice_add_fusion.2
  459.4 9.1 %collective-permute-done.9 = bf16[128,2048]{1,0:T(8,128)(2,1)S(1)} collective-permute-done((bf16[128,2048]{1,0:T(8,128)(2,1)S(1)}, bf16[128,2048]{1,0:T(8,128)(2,1)S(1)}, u32[]{:S(2)}, u32[]{:S(2)}) %collective-permute-start.9) | collective-permute-done | bytes 524320 | tf_op jit(solution)/shard_map/ppermute | solution.py:50
  469.9 15.7 %collective-permute-done.7 = bf16[128,2048]{1,0:T(8,128)(2,1)S(1)} collective-permute-done((bf16[128,2048]{1,0:T(8,128)(2,1)S(1)}, bf16[128,2048]{1,0:T(8,128)(2,1)S(1)}, u32[]{:S(2)}, u32[]{:S(2)}) %collective-permute-start.7) | collective-permute-done | bytes 524320 | tf_op jit(solution)/shard_map/ppermute | solution.py:50
  487.8 14.1 %convolution_convert_fusion.2.p_u = bf16[2048,1024]{1,0:T(8,128)(2,1)} fusion(bf16[2048,2048]{1,0:T(8,128)(2,1)} %bitcast.46, bf16[2048,1024]{1,0:T(8,128)(2,1)} %get-tuple-element.69), kind=kOutput, calls=%fused_computation.9 | convolution fusion | flops 8592031744 | bytes 16777216 | tf_op jit(solution)/shard_map/dot_general | solution.py:34
  502.0 3.7 fusion.12
  505.7 2.3 collective-permute-done.10
  508.0 5.3 collective-permute-done.8
  513.3 3.2 fusion.2.two_ref
  516.5 2.1 add_convert_fusion.1.half_d
  519.3 242.3 %back.1 = (f32[64,2048]{1,0:T(8,128)}, f32[64,2048]{1,0:T(8,128)}, f32[64,2048]{1,0:T(8,128)}, f32[64,2048]{1,0:T(8,128)}, f32[8,2048]{1,0:T(8,128)}, /*index=5*...) custom-call(bf16[256,2048]{1,0:T(8,128)(2,1)} %bitcast.39, ...), custom_call_target="tpu_custom_call" | custom-call | tf_op jit(solution)/shard_map/back/pallas_call | solution.py:1078
  763.1 2.7 convert_element_type.163
  765.8 2.8 convert_element_type.164
  (112 shorter events, 32.2 us)
Async XLA Ops:
  287.8 31.0 %collective-permute-start = (bf16[256,2048]{1,0:T(8,128)(2,1)S(1)}, bf16[256,2048]{1,0:T(8,128)(2,1)S(1)}, u32[]{:S(2)}, u32[]{:S(2)}) collective-permute-start(bf16[256,2048]{1,0:T(8,128)(2,1)S(1)} %multiply_convert_fusion.3), channel_id=1, source_target_pairs={{0,1},{1,0},{2,3},{3,2},{4,5},{5,4},{6,7},{7,6},{8,9},{9,8},{10,11... | collective-permute-start | bytes 3145736 | tf_op jit(solution)/shard_map/ppermute | solution.py:50
  288.1 30.7 %collective-permute-start.1 = (bf16[256,2048]{1,0:T(8,128)(2,1)S(1)}, bf16[256,2048]{1,0:T(8,128)(2,1)S(1)}, u32[]{:S(2)}, u32[]{:S(2)}) collective-permute-start(bf16[256,2048]{1,0:T(8,128)(2,1)S(1)} %multiply_convert_fusion.3), channel_id=1, source_target_pairs={{0,2},{1,3},{2,0},{3,1},{4,6},{5,7},{6,4},{7,5},{8,10},{9,11},{10,... | collective-permute-start | bytes 3145736 | tf_op jit(solution)/shard_map/ppermute | solution.py:50
  288.2 12.8 %copy-start.13 = (bf16[8,256,2048]{2,1,0:T(8,128)(2,1)S(1)}, bf16[8,256,2048]{2,1,0:T(8,128)(2,1)}, u32[]{:S(2)}) copy-start(bf16[8,256,2048]{2,1,0:T(8,128)(2,1)} %get-tuple-element.54) | copy-start | bytes 25165828
  301.0 20.6 %copy-start = (f32[2048,1024]{1,0:T(8,128)}, f32[2048,1024]{1,0:T(8,128)S(1)}, u32[]{:S(2)}) copy-start(f32[2048,1024]{1,0:T(8,128)S(1)} %fusion.23) | copy-start | bytes 25165828
  317.0 7.5 copy-start.1
  318.9 15.5 %collective-permute-start.2 = (bf16[128,2048]{1,0:T(8,128)(2,1)S(1)}, bf16[128,2048]{1,0:T(8,128)(2,1)S(1)}, u32[]{:S(2)}, u32[]{:S(2)}) collective-permute-start(bf16[128,2048]{1,0:T(8,128)(2,1)S(1)} %slice.123), channel_id=1, source_target_pairs={{0,2},{1,3},{2,0},{3,1},{4,6},{5,7},{6,4},{7,5},{8,10},{9,11},{10,... | collective-permute-start | bytes 1572872 | tf_op jit(solution)/shard_map/ppermute | solution.py:50
  320.4 14.0 %collective-permute-start.3 = (bf16[128,2048]{1,0:T(8,128)(2,1)S(1)}, bf16[128,2048]{1,0:T(8,128)(2,1)S(1)}, u32[]{:S(2)}, u32[]{:S(2)}) collective-permute-start(bf16[128,2048]{1,0:T(8,128)(2,1)S(1)} %slice.124), channel_id=1, source_target_pairs={{0,1},{1,0},{2,3},{3,2},{4,5},{5,4},{6,7},{7,6},{8,9},{9,8},{10,11... | collective-permute-start | bytes 1572872 | tf_op jit(solution)/shard_map/ppermute | solution.py:50
  324.5 6.5 copy-start.3
  336.6 14.2 %collective-permute-start.4 = (bf16[1024,2048]{1,0:T(8,128)(2,1)}, bf16[1024,2048]{1,0:T(8,128)(2,1)}, u32[]{:S(2)}, u32[]{:S(2)}) collective-permute-start(bf16[1024,2048]{1,0:T(8,128)(2,1)} %get-tuple-element.115), channel_id=1, source_target_pairs={{0,8},{1,9},{2,10},{3,11},{4,12},{5,13},{6,14},{7,15},{8,0},{9,1},... | collective-permute-start | bytes 12582920 | tf_op jit(solution)/shard_map/ppermute | solution.py:50
  337.7 39.9 %collective-permute-start.5 = (bf16[1024,2048]{1,0:T(8,128)(2,1)}, bf16[1024,2048]{1,0:T(8,128)(2,1)S(1)}, u32[]{:S(2)}, u32[]{:S(2)}) collective-permute-start(bf16[1024,2048]{1,0:T(8,128)(2,1)} %convolution_convert_fusion.1), channel_id=1, source_target_pairs={{0,8},{1,9},{2,10},{3,11},{4,12},{5,13},{6,14},{7,15},{8,0},{9,1},... | collective-permute-start | bytes 12582920 | tf_op jit(solution)/shard_map/ppermute | solution.py:50
  377.6 44.1 %copy-start.5 = (bf16[1024,2048]{1,0:T(8,128)(2,1)}, bf16[1024,2048]{1,0:T(8,128)(2,1)S(1)}, u32[]{:S(2)}) copy-start(bf16[1024,2048]{1,0:T(8,128)(2,1)S(1)} %collective-permute-done.5) | copy-start | bytes 12582916
  377.6 12.2 %copy-start.14 = (bf16[2048,1024]{1,0:T(8,128)(2,1)S(1)}, bf16[2048,1024]{1,0:T(8,128)(2,1)}, u32[]{:S(2)}) copy-start(bf16[2048,1024]{1,0:T(8,128)(2,1)} %get-tuple-element.58) | copy-start | bytes 12582916
  377.6 12.2 %copy-start.16 = (bf16[2048,1024]{1,0:T(8,128)(2,1)S(1)}, bf16[2048,1024]{1,0:T(8,128)(2,1)}, u32[]{:S(2)}) copy-start(bf16[2048,1024]{1,0:T(8,128)(2,1)} %get-tuple-element.69) | copy-start | bytes 12582916
  377.6 19.1 %slice-start.2 = ((s8[8388608]{0:T(1024)(128)(4,1)}), s8[4194304]{0:T(1024)(128)(4,1)S(1)}, s32[]{:S(2)}) async-start(s8[8388608]{0:T(1024)(128)(4,1)} %bitcast.48), calls=%async_computation.2 | async-start | bytes 8388608
  389.8 6.9 slice-start.3
  389.8 31.9 %slice-start = ((s8[8388608]{0:T(1024)(128)(4,1)}), s8[4194304]{0:T(1024)(128)(4,1)S(1)}, s32[]{:S(2)}) async-start(s8[8388608]{0:T(1024)(128)(4,1)} %bitcast.35), calls=%async_computation | async-start | bytes 8388608
  396.7 25.0 %slice-start.1 = ((s8[8388608]{0:T(1024)(128)(4,1)}), s8[4194304]{0:T(1024)(128)(4,1)S(1)}, s32[]{:S(2)}) async-start(s8[8388608]{0:T(1024)(128)(4,1)} %bitcast.35), calls=%async_computation.1 | async-start | bytes 8388608
  421.3 31.4 %collective-permute-start.6 = (bf16[1024,2048]{1,0:T(8,128)(2,1)}, bf16[1024,2048]{1,0:T(8,128)(2,1)}, u32[]{:S(2)}, u32[]{:S(2)}) collective-permute-start(bf16[1024,2048]{1,0:T(8,128)(2,1)} %add_convert_fusion), channel_id=1, source_target_pairs={{0,8},{1,9},{2,10},{3,11},{4,12},{5,13},{6,14},{7,15},{8,0},{9,1},... | collective-permute-start | bytes 12582920 | tf_op jit(solution)/shard_map/ppermute | solution.py:50
  423.8 25.2 %collective-permute-start.13 = (bf16[128,2048]{1,0:T(8,128)(2,1)}, bf16[128,2048]{1,0:T(8,128)(2,1)}, u32[]{:S(2)}, u32[]{:S(2)}) collective-permute-start(bf16[128,2048]{1,0:T(8,128)(2,1)} %get-tuple-element.106), channel_id=1, source_target_pairs={{0,1},{1,0},{2,3},{3,2},{4,5},{5,4},{6,7},{7,6},{8,9},{9,8},{10,11... | collective-permute-start | bytes 1572872 | tf_op jit(solution)/shard_map/ppermute | solution.py:50
  424.4 27.2 %collective-permute-start.11 = (bf16[128,2048]{1,0:T(8,128)(2,1)S(1)}, bf16[128,2048]{1,0:T(8,128)(2,1)}, u32[]{:S(2)}, u32[]{:S(2)}) collective-permute-start(bf16[128,2048]{1,0:T(8,128)(2,1)S(1)} %get-tuple-element.105), channel_id=1, source_target_pairs={{0,2},{1,3},{2,0},{3,1},{4,6},{5,7},{6,4},{7,5},{8,10},{9,11},{10,... | collective-permute-start | bytes 1572872 | tf_op jit(solution)/shard_map/ppermute | solution.py:50
  450.3 51.7 %collective-permute-start.14 = (bf16[256,2048]{1,0:T(8,128)(2,1)S(1)}, bf16[256,2048]{1,0:T(8,128)(2,1)}, u32[]{:S(2)}, u32[]{:S(2)}) collective-permute-start(bf16[256,2048]{1,0:T(8,128)(2,1)S(1)} %pad_maximum_fusion.3), channel_id=1, source_target_pairs={{0,2},{1,3},{2,0},{3,1},{4,6},{5,7},{6,4},{7,5},{8,10},{9,11},{10,... | collective-permute-start | bytes 3145736 | tf_op jit(solution)/shard_map/ppermute | solution.py:50
  455.9 12.6 %collective-permute-start.9 = (bf16[128,2048]{1,0:T(8,128)(2,1)S(1)}, bf16[128,2048]{1,0:T(8,128)(2,1)S(1)}, u32[]{:S(2)}, u32[]{:S(2)}) collective-permute-start(bf16[128,2048]{1,0:T(8,128)(2,1)S(1)} %get-tuple-element.108), channel_id=1, source_target_pairs={{0,1},{1,0},{2,3},{3,2},{4,5},{5,4},{6,7},{7,6},{8,9},{9,8},{10,11... | collective-permute-start | bytes 1572872 | tf_op jit(solution)/shard_map/ppermute | solution.py:50
  457.0 45.0 %collective-permute-start.12 = (bf16[256,2048]{1,0:T(8,128)(2,1)S(1)}, bf16[256,2048]{1,0:T(8,128)(2,1)}, u32[]{:S(2)}, u32[]{:S(2)}) collective-permute-start(bf16[256,2048]{1,0:T(8,128)(2,1)S(1)} %pad_maximum_fusion.2), channel_id=1, source_target_pairs={{0,1},{1,0},{2,3},{3,2},{4,5},{5,4},{6,7},{7,6},{8,9},{9,8},{10,11... | collective-permute-start | bytes 3145736 | tf_op jit(solution)/shard_map/ppermute | solution.py:50
  457.7 28.0 %collective-permute-start.7 = (bf16[128,2048]{1,0:T(8,128)(2,1)S(1)}, bf16[128,2048]{1,0:T(8,128)(2,1)S(1)}, u32[]{:S(2)}, u32[]{:S(2)}) collective-permute-start(bf16[128,2048]{1,0:T(8,128)(2,1)S(1)} %get-tuple-element.107), channel_id=1, source_target_pairs={{0,2},{1,3},{2,0},{3,1},{4,6},{5,7},{6,4},{7,5},{8,10},{9,11},{10,... | collective-permute-start | bytes 1572872 | tf_op jit(solution)/shard_map/ppermute | solution.py:50
  458.2 58.3 %collective-permute-start.15 = (bf16[512,2048]{1,0:T(8,128)(2,1)S(1)}, bf16[512,2048]{1,0:T(8,128)(2,1)S(1)}, u32[]{:S(2)}, u32[]{:S(2)}) collective-permute-start(bf16[512,2048]{1,0:T(8,128)(2,1)S(1)} %constant_dynamic-slice_fusion.1), channel_id=1, source_target_pairs={{0,16},{1,17},{2,18},{3,19},{4,20},{5,21},{6,22},{7,23},{8,24},{9,... | collective-permute-start | bytes 6291464 | tf_op jit(solution)/shard_map/ppermute | solution.py:50
  469.7 38.4 %collective-permute-start.10 = (bf16[256,2048]{1,0:T(8,128)(2,1)}, bf16[256,2048]{1,0:T(8,128)(2,1)S(1)}, u32[]{:S(2)}, u32[]{:S(2)}) collective-permute-start(bf16[256,2048]{1,0:T(8,128)(2,1)} %pad_maximum_fusion.1), channel_id=1, source_target_pairs={{0,2},{1,3},{2,0},{3,1},{4,6},{5,7},{6,4},{7,5},{8,10},{9,11},{10,... | collective-permute-start | bytes 3145736 | tf_op jit(solution)/shard_map/ppermute | solution.py:50
  486.9 15.1 %copy-start.2 = (f32[256,2048]{1,0:T(8,128)S(1)}, f32[256,2048]{1,0:T(8,128)}, u32[]{:S(2)}) copy-start(f32[256,2048]{1,0:T(8,128)} %get-tuple-element.74.resid_ref) | copy-start | bytes 6291460
  486.9 26.4 %collective-permute-start.8 = (bf16[256,2048]{1,0:T(8,128)(2,1)}, bf16[256,2048]{1,0:T(8,128)(2,1)S(1)}, u32[]{:S(2)}, u32[]{:S(2)}) collective-permute-start(bf16[256,2048]{1,0:T(8,128)(2,1)} %pad_maximum_fusion), channel_id=1, source_target_pairs={{0,1},{1,0},{2,3},{3,2},{4,5},{5,4},{6,7},{7,6},{8,9},{9,8},{10,11... | collective-permute-start | bytes 3145736 | tf_op jit(solution)/shard_map/ppermute | solution.py:50
  761.6 6.9 copy-start.7
  765.8 4.9 copy-start.10
  765.8 5.7 copy-start.9
  768.6 4.5 copy-start.6
  (5 other events, 14.9 us)

commit v5 on v4

--- a/solution.py
+++ b/solution.py
@@ -26,57 +26,9 @@
     return (jnp.cos(angles), jnp.sin(angles))
 
 
-def mm(left, right):
-    return jnp.dot(left, right, preferred_element_type=f32)
-
-
-def outer_sum(left, right):
-    return lax.dot_general(left, right, (((0,), (0,)), ((), ())), preferred_element_type=f32)
-
-
-def times_transposed(left, weight):
-    return lax.dot_general(left, weight, (((1,), (1,)), ((), ())), preferred_element_type=f32)
-
-
-class Plan:
-    def __init__(self, outer, inner, rows):
-        self.count = outer * inner
-        self.bit_a = max(1, HEAD_DIM // rows)
-        self.bit_b = 2 * self.bit_a
-        self.bit_core = inner
-        self.flat = lax.axis_index("dp") * inner + lax.axis_index("fsdp")
-
-    def send(self, array, bit):
-        return lax.ppermute(array, AXES, [(r, r ^ bit) for r in range(self.count)])
-
-    def sum_upper(self, total):
-        bit = self.count // 2
-        rows = total.shape[0] // 2
-        here = (self.flat // bit) % 2
-        away = lax.dynamic_slice_in_dim(total, (1 - here) * rows, rows, 0)
-        kept = lax.dynamic_slice_in_dim(total, here * rows, rows, 0)
-        return (kept.astype(f32) + self.send(away, bit).astype(f32)).astype(bf16)
-
-    def sum_four(self, near, core):
-        size = near.shape[0] // QUAD
-        half = size // 2
-        own, for_a, for_b, for_ab = (
-            near[i * size : (i + 1) * size] + core[i * size : (i + 1) * size].astype(f32)
-            for i in range(QUAD)
-        )
-        first = self.send(for_ab[:half].astype(bf16), self.bit_b)
-        second = self.send(for_ab[half:].astype(bf16), self.bit_a)
-        for_a = jnp.concatenate([for_a[:half] + first.astype(f32), for_a[half:]]).astype(bf16)
-        for_b = jnp.concatenate([for_b[:half], for_b[half:] + second.astype(f32)]).astype(bf16)
-        return (
-            own
-            + self.send(for_a, self.bit_a).astype(f32)
-            + self.send(for_b, self.bit_b).astype(f32)
-        )
-
-
 class Ring:
     def __init__(self, outer, inner, rows):
+        self.known = {}
         self.count = outer * inner
         self.inner = inner
         self.span = max(1, HEAD_DIM // rows)
@@ -103,8 +55,10 @@
         return flat
 
     def where(self, bits):
-        other = self.flip(self.flat, bits)
-        return (other // self.inner, other % self.inner)
+        if bits not in self.known:
+            other = self.flip(self.flat, bits)
+            self.known[bits] = (other // self.inner, other % self.inner)
+        return self.known[bits]
 
     def team(self, flat):
         return ((flat // self.inner) % 2) * QUAD + (flat // self.span) % QUAD
@@ -1111,6 +1065,381 @@
     )(*near_args, *far_args)
 
 
+def mid_kernel(
+    outer, inner, hidden_rows,
+    go_ref, factor_ref,
+    act_two, wg_ref, wu_ref, wd_ref, resid_ref,
+    p_g, p_u, half_d, added, layer_out, dy, p_d, land_d, land_down, land_two, a_down, b_down, a_two, b_two,
+    w_g, w_u, w_d, middle, cols, act_in, dy_in, act_cut, dy_cut, stage_d, dy_own,
+    far_down, far_two, tmp_down, tmp_two, near_down, near_two, own_down, own_two, halves, stage,
+    send_sems, recv_sems, local_sems, down_send, down_recv, two_send, two_recv, act_sems, dy_sem, tmp_sems, cut_sems, out_sems,
+):
+    size, width = go_ref.shape
+    hidden = w_g.shape[1]
+    ring = Ring(outer, inner, width // (outer * inner))
+    mail = Mail(ring, send_sems, recv_sems, local_sems)
+    ring.greet()
+    flat = ring.flat
+    strip = 32
+    top_bit = ring.count // 2
+
+    def strips(step):
+        def run(i, carry):
+            step(pl.ds(pl.multiple_of(i * strip, strip), strip))
+            return carry
+
+        lax.fori_loop(0, size // strip, run, 0)
+
+    def dot(left, right, left_dim, right_dim):
+        return lax.dot_general(
+            left, right, (((left_dim,), (right_dim,)), ((), ())), preferred_element_type=f32
+        )
+
+    def settle(copy):
+        copy.wait()
+        mail.kept = [c for c in mail.kept if c is not copy]
+
+    def pair_at(i):
+        pair = i // 2
+        return pair + (pair // 2) * (5 - 2 * pair)
+
+    def block_at(i):
+        return pair_at(i) + QUAD * (1 - i % 2)
+
+    def act_copy(i):
+        return pltpu.make_async_copy(
+            act_two.at[block_at(i)], act_in.at[i % 2], act_sems.at[i % 2]
+        )
+
+    act_copy(0).start()
+    loads = [mail.keep(wg_ref, w_g), mail.keep(wu_ref, w_u), mail.keep(wd_ref, w_d)]
+    load_resid = mail.keep(resid_ref, own_down)
+
+    def cotangent(part):
+        dy_own[part, :] = (go_ref[part, :].astype(f32) * factor_ref[part, :]).astype(bf16)
+
+    strips(cotangent)
+    keep_dy = mail.keep(dy_own, dy.at[0])
+    half = size // 2
+    top, end = pl.ds(0, half), pl.ds(half, half)
+    share = Share(mail, dy, dy_own)
+    share.first()
+    for copy in loads:
+        settle(copy)
+    settle(load_resid)
+    settle(keep_dy)
+    share.done((0,))
+
+    def core_copy(kind, i):
+        pair = i // 2
+        source, target, send, recv = (
+            (far_down, land_down, down_send, down_recv),
+            (far_two, land_two, two_send, two_recv),
+        )[kind]
+        return pltpu.make_async_remote_copy(
+            src_ref=source,
+            dst_ref=target.at[pair_at(i)],
+            send_sem=send.at[pair],
+            recv_sem=recv.at[pair],
+            device_id=ring.where(ring.bit_core),
+            device_id_type=MESH,
+        )
+
+    def tmp_copy(kind, i):
+        source, target = ((land_down, tmp_down), (land_two, tmp_two))[kind]
+        return pltpu.make_async_copy(source.at[pair_at(i)], target, tmp_sems.at[kind])
+
+    base = mail.used
+    mail.used += 9
+
+    def late(n):
+        src, dst, bit = (
+            (dy.at[1, top], dy.at[3, top], ring.bit_b),
+            (dy.at[2, end], dy.at[3, end], ring.bit_a),
+            (dy.at[1], dy.at[QUAD + 1], ring.bit_core),
+            (dy.at[2], dy.at[QUAD + 2], ring.bit_core),
+            (dy.at[3], dy.at[QUAD + 3], ring.bit_core),
+            (near_two.at[2, top], halves.at[1, 0], ring.bit_b),
+            (near_two.at[2, end], halves.at[1, 1], ring.bit_a),
+            (near_down.at[2, top], halves.at[0, 0], ring.bit_b),
+            (near_down.at[2, end], halves.at[0, 1], ring.bit_a),
+        )[n]
+        return pltpu.make_async_remote_copy(
+            src_ref=src,
+            dst_ref=dst,
+            send_sem=send_sems.at[base + n],
+            recv_sem=recv_sems.at[base + n],
+            device_id=ring.where(bit),
+            device_id_type=MESH,
+        )
+
+    def block(i, carry):
+        place = block_at(i)
+        other = i % 2 == 0
+        pair = pair_at(i)
+
+        @pl.when(i == 2)
+        def _():
+            share.from_a.wait_recv()
+            late(0).start()
+            late(2).start()
+            share.from_b.wait_recv()
+            late(1).start()
+            late(3).start()
+            late(2).wait_recv()
+
+        @pl.when(i == 4)
+        def _():
+            late(0).wait_recv()
+            late(1).wait_recv()
+            late(4).start()
+            late(3).wait_recv()
+            late(4).wait_recv()
+
+        @pl.when(i == 6)
+        def _():
+            for n in range(5, 9):
+                late(n).start()
+
+        dy_copy = pltpu.make_async_copy(dy.at[place], dy_in, dy_sem.at[0])
+        dy_copy.start()
+
+        @pl.when(jnp.logical_not(other))
+        def _():
+            for kind in range(2):
+                core_copy(kind, i).wait_recv()
+                tmp_copy(kind, i).start()
+
+        act_copy(i).wait()
+
+        @pl.when(i + 1 < 2 * QUAD)
+        def _():
+            act_copy(i + 1).start()
+
+        act = act_in[i % 2]
+        gate_pre = dot(act, w_g[...], 1, 0)
+        up_proj = dot(act, w_u[...], 1, 0)
+        sigmoid_gate = jax.nn.sigmoid(gate_pre)
+        swish = gate_pre * sigmoid_gate
+        middle[place] = (swish * up_proj).astype(bf16)
+        dy_copy.wait()
+        grad_middle = dot(dy_in[...], w_d[...], 1, 1)
+        cols[place, :, hidden:] = (grad_middle * swish).astype(bf16)
+        cols[place, :, :hidden] = (
+            grad_middle * up_proj * sigmoid_gate * (1.0 + gate_pre * (1.0 - sigmoid_gate))
+        ).astype(bf16)
+        down = dot(middle[place], w_d[...], 1, 0)
+
+        def give(kind, part, far, tmp, near, own):
+            @pl.when(other)
+            def _():
+                @pl.when(i >= 2)
+                def _():
+                    core_copy(kind, i - 2).wait_send()
+
+                far[...] = part.astype(bf16)
+                core_copy(kind, i).start()
+
+            @pl.when(jnp.logical_not(other))
+            def _():
+                tmp_copy(kind, i).wait()
+                total = part + tmp[...].astype(f32)
+
+                @pl.when(pair == 0)
+                def _():
+                    own[...] = total + own[...] if kind == 0 else total
+
+                @pl.when(pair > 0)
+                def _():
+                    near[jnp.maximum(pair, 1) - 1] = total.astype(bf16)
+
+        give(0, down, far_down, tmp_down, near_down, own_down)
+        two = dot(cols[place, :, :hidden], w_g[...], 1, 1) + dot(
+            cols[place, :, hidden:], w_u[...], 1, 1
+        )
+        give(1, two, far_two, tmp_two, near_two, own_two)
+        return carry
+
+    lax.fori_loop(0, 2 * QUAD, block, 0)
+    for kind in range(2):
+        core_copy(kind, 2 * QUAD - 2).wait_send()
+
+    cut = act_cut.shape[3]
+    cuts = width // cut
+    tokens = 2 * QUAD * size
+
+    def cut_copy(source, target, i):
+        start = pl.multiple_of(i * cut, cut)
+        return pltpu.make_async_copy(
+            source.at[:, :, pl.ds(start, cut)], target.at[i % 2], cut_sems.at[i % 2]
+        )
+
+    def down_out(i):
+        start = pl.multiple_of(i * cut, cut)
+        return pltpu.make_async_copy(
+            stage_d.at[i % 2], p_d.at[:, pl.ds(start, cut)], out_sems.at[i % 2]
+        )
+
+    cut_copy(dy, dy_cut, 0).start()
+
+    def down_step(i, carry):
+        cut_copy(dy, dy_cut, i).wait()
+
+        @pl.when(i + 1 < cuts)
+        def _():
+            cut_copy(dy, dy_cut, i + 1).start()
+
+        turned = dot(
+            dy_cut[i % 2].reshape(tokens, cut), middle[...].reshape(tokens, hidden), 0, 0
+        )
+
+        @pl.when(i >= 2)
+        def _():
+            down_out(i - 2).wait()
+
+        stage_d[i % 2] = turned.T.astype(bf16)
+        down_out(i).start()
+        return carry
+
+    lax.fori_loop(0, cuts, down_step, 0)
+    cut_copy(act_two, act_cut, 0).start()
+    for i in (cuts - 2, cuts - 1):
+        down_out(i).wait()
+    upper = flat // top_bit
+    rows_half = hidden // 2
+    away = pl.ds(pl.multiple_of((1 - upper) * rows_half, 16), rows_half)
+    kept = pl.ds(pl.multiple_of(upper * rows_half, 16), rows_half)
+    sum_d = mail.post(p_d.at[away], land_d, top_bit)
+
+    second = {}
+    for kind, near, to_a, to_b in ((1, near_two, a_two, b_two), (0, near_down, a_down, b_down)):
+        late(7 - 2 * kind).wait_recv()
+        add_near(near.at[0, top], near.at[0, top], halves.at[kind, 0])
+        second["a", kind] = mail.post(near.at[0], to_a, ring.bit_a)
+        late(8 - 2 * kind).wait_recv()
+        add_near(near.at[1, end], near.at[1, end], halves.at[kind, 1])
+        second["b", kind] = mail.post(near.at[1], to_b, ring.bit_b)
+
+    def stage_out(i):
+        rows = pl.ds(pl.multiple_of(i * cut, cut), cut)
+        return [
+            pltpu.make_async_copy(
+                stage.at[i % 2, :, pl.ds(j * hidden, hidden)],
+                target.at[rows],
+                out_sems.at[2 + 2 * j + i % 2],
+            )
+            for j, target in enumerate((p_g, p_u))
+        ]
+
+    def gate_step(i, carry):
+        cut_copy(act_two, act_cut, i).wait()
+
+        @pl.when(i + 1 < cuts)
+        def _():
+            cut_copy(act_two, act_cut, i + 1).start()
+
+        @pl.when(i >= 2)
+        def _():
+            for copy in stage_out(i - 2):
+                copy.wait()
+
+        stage[i % 2] = dot(
+            act_cut[i % 2].reshape(tokens, cut), cols[...].reshape(tokens, 2 * hidden), 0, 0
+        ).astype(bf16)
+        for copy in stage_out(i):
+            copy.start()
+        return carry
+
+    lax.fori_loop(0, cuts, gate_step, 0)
+    for i in (cuts - 2, cuts - 1):
+        for copy in stage_out(i):
+            copy.wait()
+
+    for kind, own, in_a, in_b in ((1, own_two, a_two, b_two), (0, own_down, a_down, b_down)):
+        second["a", kind].wait_recv()
+        second["b", kind].wait_recv()
+        first = mail.keep(in_a, tmp_down)
+        other = mail.keep(in_b, tmp_two)
+        settle(first)
+        settle(other)
+
+        def finish(part, own=own, kind=kind):
+            total = own[part, :] + tmp_down[part, :].astype(f32) + tmp_two[part, :].astype(f32)
+            if kind:
+                own_two[part, :] = total
+            else:
+                far_down[part, :] = total.astype(bf16)
+
+        strips(finish)
+        if kind:
+            mail.keep(own_two, added)
+        else:
+            mail.keep(far_down, layer_out)
+    sum_d.wait_recv()
+    add_far(half_d, p_d.at[kept], land_d)
+    for n in range(9):
+        late(n).wait_send()
+    mail.finish()
+
+
+def mid(outer, inner, hidden_rows, grad_out, factor_rows, act_two, w_g, w_u, w_d, resid):
+    size, width = grad_out.shape
+    hidden = w_g.shape[1]
+    vm = pl.BlockSpec(memory_space=pltpu.VMEM)
+    hbm = pl.BlockSpec(memory_space=pl.ANY)
+    sds = jax.ShapeDtypeStruct
+    wide = sds((size, width), bf16)
+    out_shape = (
+        sds((width, hidden), bf16),
+        sds((width, hidden), bf16),
+        sds((hidden // 2, width), bf16),
+        sds((size, width), f32),
+        wide,
+        sds((2 * QUAD, size, width), bf16),
+        sds((hidden, width), bf16),
+        sds((hidden // 2, width), bf16),
+        sds((QUAD, size, width), bf16),
+        sds((QUAD, size, width), bf16),
+        wide, wide, wide, wide,
+    )
+    cut = min(256, width // 2)
+    vw = pltpu.VMEM((size, width), bf16)
+    dma = pltpu.SemaphoreType.DMA
+    return pl.pallas_call(
+        functools.partial(mid_kernel, outer, inner, hidden_rows),
+        out_shape=out_shape,
+        in_specs=[vm] * 2 + [hbm] * 5,
+        out_specs=tuple([hbm] * len(out_shape)),
+        scratch_shapes=[
+            pltpu.VMEM((width, hidden), bf16),
+            pltpu.VMEM((width, hidden), bf16),
+            pltpu.VMEM((hidden, width), bf16),
+            pltpu.VMEM((2 * QUAD, size, hidden), bf16),
+            pltpu.VMEM((2 * QUAD, size, 2 * hidden), bf16),
+            pltpu.VMEM((2, size, width), bf16),
+            vw,
+            pltpu.VMEM((2, 2 * QUAD, size, cut), bf16),
+            pltpu.VMEM((2, 2 * QUAD, size, cut), bf16),
+            pltpu.VMEM((2, hidden, cut), bf16),
+            vw,
+            vw, vw, vw, vw,
+            pltpu.VMEM((QUAD - 1, size, width), bf16),
+            pltpu.VMEM((QUAD - 1, size, width), bf16),
+            pltpu.VMEM((size, width), f32),
+            pltpu.VMEM((size, width), f32),
+            pltpu.VMEM((2, 2, size // 2, width), bf16),
+            pltpu.VMEM((2, cut, 2 * hidden), bf16),
+            dma((32,)), dma((32,)), dma((16,)),
+            dma((QUAD,)), dma((QUAD,)), dma((QUAD,)), dma((QUAD,)),
+            dma((2,)), dma((1,)), dma((2,)), dma((2,)), dma((6,)),
+        ],
+        compiler_params=pltpu.CompilerParams(
+            collective_id=2, has_side_effects=True, vmem_limit_bytes=63 * 1024 * 1024
+        ),
+        name="mid",
+    )(grad_out, factor_rows, act_two, w_g, w_u, w_d, resid)
+
+
 def on_device(
     tokens,
     labels,
@@ -1131,7 +1460,7 @@
     inner_count = lax.axis_size("fsdp")
     rows = w_query.shape[0]
     hidden_rows = w_down.shape[0]
-    plan = Plan(outer_count, inner_count, rows)
+    flat = lax.axis_index("dp") * inner_count + lax.axis_index("fsdp")
     x_rows = tokens.reshape(-1, width)
 
     token_total = float(seq_len * batch_size * outer_count * inner_count)
@@ -1147,7 +1476,7 @@
     gain_rows = lax.dynamic_update_slice(
         jnp.zeros((8, width), f32),
         jnp.stack([gain_attn, gain_mlp]).astype(f32),
-        (0, plan.flat * rows),
+        (0, flat * rows),
     )
     factor_rows = jnp.repeat(factor, seq_len)[:, None]
     (
@@ -1159,54 +1488,11 @@
         wide_cosine, wide_sine,
         w_out, w_gate, w_up, w_down,
     )
-    narrow = w_o.shape[0]
-    hidden = w_d.shape[0]
-    act_two = act_two.reshape(-1, width)
-    dy_own = (grad_out.reshape(-1, width).astype(f32) * factor_rows).astype(bf16)
-    dy_own, act_two = lax.optimization_barrier((dy_own, act_two))
-    held = lax.optimization_barrier
-    count = act_two.shape[0] // 2
-    dy_a, dy_b = plan.send(dy_own, plan.bit_a), plan.send(dy_own, plan.bit_b)
-    gate_pre, up_proj = mm(act_two, w_g), mm(act_two, w_u)
-    gate_pre, up_proj, dy_a, dy_b = held((gate_pre, up_proj, dy_a, dy_b))
-
-    half = dy_a.shape[0] // 2
-    dy_first, dy_second = plan.send(dy_a[:half], plan.bit_b), plan.send(dy_b[half:], plan.bit_a)
-    sigmoid_gate = jax.nn.sigmoid(gate_pre)
-    middle = (gate_pre * sigmoid_gate * up_proj).astype(bf16)
-    down_far = mm(middle[count:], w_d).astype(bf16)
-    down_far, dy_first, dy_second = held((down_far, dy_first, dy_second))
-
-    dy_near = jnp.concatenate([dy_own, dy_a, dy_b, dy_first, dy_second], axis=0)
-    dy_far = plan.send(dy_near, plan.bit_core)
-    down_near = mm(middle[:count], w_d)
-    down_near, dy_far = held((down_near, dy_far))
-    dy = jnp.concatenate([dy_near, dy_far], axis=0)
-    down_core = plan.send(down_far, plan.bit_core)
-    grad_middle = times_transposed(dy, w_d)
-    grad_gate_pre = (
-        grad_middle * up_proj * sigmoid_gate * (1.0 + gate_pre * (1.0 - sigmoid_gate))
-    ).astype(bf16)
-    grad_up_proj = (grad_middle * gate_pre * sigmoid_gate).astype(bf16)
-    grad_gate_pre, grad_up_proj, down_core = held((grad_gate_pre, grad_up_proj, down_core))
-
-    def back_two(part):
-        return times_transposed(grad_gate_pre[part], w_g) + times_transposed(
-            grad_up_proj[part], w_u
-        )
-
-    down = plan.sum_four(down_near, down_core)
-    two_far = back_two(slice(count, None)).astype(bf16)
-    two_far, middle, dy = held((two_far, middle, dy))
-    two_core = plan.send(two_far, plan.bit_core)
-    p_d = outer_sum(middle, dy).astype(bf16)
-    p_d, two_core = held((p_d, two_core))
-    half_d = plan.sum_upper(p_d)
-    added = plan.sum_four(back_two(slice(0, count)), two_core)
-    p_g = outer_sum(act_two, grad_gate_pre).astype(bf16)
-    p_u = outer_sum(act_two, grad_up_proj).astype(bf16)
-    layer_out = (resid + down).astype(bf16).reshape(tokens.shape)
-    added, layer_out = held((added, layer_out))
+    p_g, p_u, half_d, added, layer_out = mid(
+        outer_count, inner_count, w_down.shape[0], grad_out.reshape(-1, width), factor_rows,
+        act_two, w_g, w_u, w_d, resid,
+    )[:5]
+    layer_out = layer_out.reshape(tokens.shape)
     results = back(
         outer_count, inner_count, seq_len,
         (
@@ -1218,7 +1504,7 @@
     query_grad, key_grad, value_grad, out_grad, gain_grads = results[:5]
     gate_grad, up_grad, down_grad = (a.astype(f32) for a in results[5:8])
     grad_tokens = results[-1]
-    gain_grads = lax.dynamic_slice(gain_grads, (0, plan.flat * rows), (2, rows))
+    gain_grads = lax.dynamic_slice(gain_grads, (0, flat * rows), (2, rows))
     return (
         layer_out,
         grad_tokens.reshape(tokens.shape),

time: 785 us -> 713 us (0.908)
  Pallas kernels: 522 us -> 679 us
  matrix products: 150 us -> 0 us
  waiting for transfers between devices: 35 us -> 0 us
  other arithmetic: 30.2 us -> 6.34 us
  local copies, waits for them, and re-layouts: 24.1 us -> 11.4 us
  starting transfers between devices: 11 us -> 0 us
    pallas_call x0 -> x1, Pallas kernels: none -> 160 us  [mid(): pl.pallas_call(functools.partial(mid_kernel, outer, inner, hidden_rows),...]
    dot_general x12 -> x0, matrix products: 150 us -> none  [the longest x5 62.7 us: times_transposed(): lax.dot_general(left, weight, (((1,), (1,)), ((), ())), preferred_element...]
    ppermute x16 -> x0, waiting for transfers between devices: 35 us -> none  [send(): return lax.ppermute(array, AXES, [(r, r ^ bit) for r in range(self.count)])]
    ppermute x16 -> x0, starting transfers between devices: 11 us -> none  [send(): return lax.ppermute(array, AXES, [(r, r ^ bit) for r in range(self.count)])]
  transfers between devices with their start and end apart: 16 -> 0, of which waited for: 5 -> 0; matrix products, arithmetic and copies ran while one was open for 18% -> 0% of each run, Pallas kernels for 0% -> 0%
where the time goes in v5:
time: 713 us; the launch traced here: 700 us
  Pallas kernels  679 us (95%)
  local copies, waits for them, and re-layouts  11.4 us (2%)
    pallas_call x1, Pallas kernels, front(): pl.pallas_call(functools.partial(front_kernel, outer, inner, seq_len), ou...  280 us
    pallas_call x1, Pallas kernels, back(): pl.pallas_call(functools.partial(back_kernel, outer, inner, seq_len), out...  240 us
    pallas_call x1, Pallas kernels, mid(): pl.pallas_call(functools.partial(mid_kernel, outer, inner, hidden_rows),...  160 us

profile of v5, /device:TPU:1, one launch (start us, length us, event | category | flops | bytes accessed | tf_op | source)
XLA Modules:
  0.0 699.6 jit_solution(18436787485353727766)
XLA Ops:
  1.3 1.3 fusion.3
  3.3 0.7 maximum_convert_fusion
  4.0 0.1 broadcast_multiply_fusion
  4.1 0.4 dynamic_update_slice.3.gain_ref
  4.4 0.0 copy-start.8
  4.5 0.1 fusion.2
  4.6 0.7 broadcast_in_dim_reshape.3.factor_ref
  5.3 0.8 copy.25.sin_ref
  6.1 0.8 copy.24.cos_ref
  7.0 0.0 copy-done.8
  7.0 279.6 %front.1 = (bf16[8,256,2048]{2,1,0:T(8,128)(2,1)}, bf16[2048,768]{1,0:T(8,128)(2,1)}, bf16[256,2048]{1,0:T(8,128)(2,1)}, bf16[8,256,256]{2,1,0:T(8,128)(2,1)}, b...) custom-call(bf16[256,2048]{1,0:T(8,128)(2,1)} %bitcast.16, ...), custom_call_target="tpu_custom_call" | custom-call | tf_op jit(solution)/shard_map/front/pallas_call | solution.py:578
  286.6 160.0 %mid.1 = (bf16[2048,1024]{1,0:T(8,128)(2,1)}, bf16[2048,1024]{1,0:T(8,128)(2,1)}, bf16[512,2048]{1,0:T(8,128)(2,1)}, f32[256,2048]{1,0:T(8,128)}, bf16[256,2048]...) custom-call(bf16[256,2048]{1,0:T(8,128)(2,1)} %bitcast.14, ...), custom_call_target="tpu_custom_call" | custom-call | tf_op jit(solution)/shard_map/mid/pallas_call | solution.py:1408
  446.6 239.8 %back.1 = (f32[64,2048]{1,0:T(8,128)}, f32[64,2048]{1,0:T(8,128)}, f32[64,2048]{1,0:T(8,128)}, f32[64,2048]{1,0:T(8,128)}, f32[8,2048]{1,0:T(8,128)}, /*index=5*...) custom-call(bf16[256,2048]{1,0:T(8,128)(2,1)} %bitcast.17, ...), custom_call_target="tpu_custom_call" | custom-call | tf_op jit(solution)/shard_map/back/pallas_call | solution.py:1032
  686.4 0.0 copy-start.2
  686.4 0.8 constant_dynamic-slice_fusion
  687.2 0.5 slice_bitcast_fusion
  687.8 2.7 convert_element_type.35
  690.4 0.0 copy-done.2
  690.4 1.5 convert_element_type.36
  691.9 0.1 copy-done.3
  692.0 1.0 copy.37
  693.0 0.3 copy-done.1
  693.3 1.3 copy.38
  694.7 0.0 copy-done.7
  694.7 0.8 copy.39
  695.5 0.0 copy-done.6
  695.5 0.8 copy.40
  696.3 0.0 copy-done.5
  696.3 0.8 copy.41
  697.1 0.0 copy-done.4
  697.1 0.8 copy.42
  697.9 1.3 copy.43
  (14 shorter events, 0.1 us)
Async XLA Ops:
  4.4 2.5 copy-start.8
  686.4 4.1 copy-start.2
  690.4 1.6 copy-start.3
  690.4 2.9 copy-start.1
  693.3 1.4 copy-start.7
  693.3 2.2 copy-start.6
  693.3 3.0 copy-start.5
  694.7 2.4 copy-start.4
  694.7 3.2 copy-start

commit v6 on v5

--- a/solution.py
+++ b/solution.py
@@ -333,6 +333,12 @@
     keep_d = mail.keep(wd_ref, mine_d)
     keep_x = mail.keep(x_ref, x_all.at[0])
 
+    gains_out[...] = gain_ref[...]
+    gains = Adding(
+        mail, gains_out, gain_in, [ring.bit_a, ring.bit_b, ring.bit_core] + bits
+    )
+    gains.post()
+
     chunk = HEAD_DIM
     for t in range(2 * QUAD):
         for j, ref in enumerate((wq_ref, wk_ref, wv_ref)):
@@ -344,48 +350,38 @@
             cut[t, :, j * narrow : (j + 1) * narrow] = jnp.concatenate(parts, axis=1)
     here = pl.ds(pl.multiple_of(flat * rows, 16), rows)
     keep_qkv = mail.keep(cut.at[ring.team(flat)], w_qkv.at[here])
+    gains.take()
+    gains.post()
     qkv_swap = []
     for delta in ring.deltas[1:]:
         other = ring.flip(flat, delta)
         qkv_swap.append(mail.post(cut.at[ring.team(other)], w_qkv.at[here], delta))
-
-    gains_out[...] = gain_ref[...]
-    gains = Adding(
-        mail, gains_out, gain_in, [ring.bit_core, ring.bit_a, ring.bit_b] + bits
-    )
+    share_x = Share(mail, x_all, x_ref)
+    share_x.first_core()
+    share_x.first_a()
+    gains.take()
     gains.post()
     settle(keep_o)
     spread_o = Spread(mail, by_place(w_o, rows, 1), bits)
-    spread_o.begin()
     gains.take()
     gains.post()
-    share_x = Share(mail, x_all, x_ref)
-    share_x.first_core()
-    share_x.first_a()
+    spread_o.begin()
+    share_x.first_b()
     settle(keep_qkv)
     for copy in qkv_swap:
         copy.wait_recv()
     spread_qkv = Spread(mail, by_runs(w_qkv), bits)
     spread_qkv.begin()
-    gains.take()
-    gains.post()
-    share_x.first_b()
-    spread_o.pass_all()
-
-    gains.take()
-    gains.post()
-    share_x.second_a()
-    for piece in range(spread_qkv.pieces):
-        spread_qkv.pass_all(piece)
     while gains.step < len(gains.bits) - 1:
         gains.take()
         gains.post()
-    spread_d = Spread(mail, by_place(w_d, hidden_rows, 2), bits)
-    settle(keep_d)
-    share_x.second_b()
+    spread_o.pass_all()
+    gains.take()
+
     block = ring.span * hidden_rows
-    gate_swap, up_swap = [], []
-    for ref, whole, swap in ((wg_ref, w_g, gate_swap), (wu_ref, w_u, up_swap)):
+
+    def swap_columns(ref, whole):
+        swap = []
         for delta in ring.deltas:
             team = ring.team(ring.flip(flat, delta))
             for y in range(ring.upper_size):
@@ -397,6 +393,7 @@
                         swap.append((mail.post(src, dst, delta), True))
                     else:
                         swap.append((mail.keep(src, dst), False))
+        return swap
 
     def swapped(swap):
         for copy, remote in swap:
@@ -404,9 +401,6 @@
                 copy.wait_recv()
             else:
                 settle(copy)
-
-    spread_d.begin()
-    gains.take()
 
     size = act_one.shape[1]
     strip = 32
@@ -421,14 +415,22 @@
 
         lax.fori_loop(0, size // strip, norm_one, 0)
 
+    share_x.second_a()
+    gate_swap = swap_columns(wg_ref, w_g)
+    settle(keep_d)
+    spread_d = Spread(mail, by_place(w_d, hidden_rows, 2), bits)
+    spread_d.begin()
     settle(keep_x)
-    share_x.done(range(QUAD - 1))
-
-    def norm_early(i, carry):
-        norm_block(lax.rem(i, QUAD - 1) + QUAD * (i // (QUAD - 1)))
-        return carry
-
-    lax.fori_loop(0, 2 * (QUAD - 1), norm_early, 0)
+    share_x.done((0, 1))
+    for place in (0, QUAD, 1, QUAD + 1):
+        norm_block(place)
+    share_x.second_b()
+    for piece in range(spread_qkv.pieces):
+        spread_qkv.pass_all(piece)
+    up_swap = swap_columns(wu_ref, w_u)
+    share_x.done((2,))
+    for place in (2, QUAD + 2):
+        norm_block(place)
     spread_o.done()
     spread_qkv.done()
 
@@ -492,12 +494,12 @@
 
         return carry
 
-    lax.fori_loop(0, QUAD - 1, far_step, 0)
     spread_g = Spread(mail, by_runs(w_g), bits)
     spread_u = Spread(mail, by_runs(w_u), bits)
+    lax.fori_loop(0, QUAD - 1, far_step, 0)
+    share_x.third()
     swapped(gate_swap)
     spread_g.begin()
-    share_x.third()
     lax.fori_loop(0, QUAD - 1, near_step, 0)
     norm_block(QUAD - 1)
     share_x.done((QUAD - 1,))
@@ -1072,7 +1074,7 @@
     p_g, p_u, half_d, added, layer_out, dy, p_d, land_d, land_down, land_two, a_down, b_down, a_two, b_two,
     w_g, w_u, w_d, middle, cols, act_in, dy_in, act_cut, dy_cut, stage_d, dy_own,
     far_down, far_two, tmp_down, tmp_two, near_down, near_two, own_down, own_two, halves, stage,
-    send_sems, recv_sems, local_sems, down_send, down_recv, two_send, two_recv, act_sems, dy_sem, tmp_sems, cut_sems, out_sems,
+    send_sems, recv_sems, local_sems, down_send, down_recv, two_send, two_recv, act_sems, dy_sem, tmp_sems, cut_sems, out_sems, pd_send, pd_recv,
 ):
     size, width = go_ref.shape
     hidden = w_g.shape[1]
@@ -1100,18 +1102,20 @@
         mail.kept = [c for c in mail.kept if c is not copy]
 
     def pair_at(i):
-        pair = i // 2
-        return pair + (pair // 2) * (5 - 2 * pair)
-
-    def block_at(i):
-        return pair_at(i) + QUAD * (1 - i % 2)
-
-    def act_copy(i):
-        return pltpu.make_async_copy(
-            act_two.at[block_at(i)], act_in.at[i % 2], act_sems.at[i % 2]
-        )
-
-    act_copy(0).start()
+        return i + (i // 2) * (5 - 2 * i)
+
+    def pair_copies(source, target, sems, i):
+        pair = pair_at(i)
+        return [
+            pltpu.make_async_copy(source.at[pair], target.at[pl.ds(0, size)], sems.at[0]),
+            pltpu.make_async_copy(source.at[QUAD + pair], target.at[pl.ds(size, size)], sems.at[1]),
+        ]
+
+    def act_copies(i):
+        return pair_copies(act_two, act_in.at[i % 2], act_sems.at[i % 2], i)
+
+    for copy in act_copies(0):
+        copy.start()
     loads = [mail.keep(wg_ref, w_g), mail.keep(wu_ref, w_u), mail.keep(wd_ref, w_d)]
     load_resid = mail.keep(resid_ref, own_down)
 
@@ -1131,7 +1135,6 @@
     share.done((0,))
 
     def core_copy(kind, i):
-        pair = i // 2
         source, target, send, recv = (
             (far_down, land_down, down_send, down_recv),
             (far_two, land_two, two_send, two_recv),
@@ -1139,8 +1142,8 @@
         return pltpu.make_async_remote_copy(
             src_ref=source,
             dst_ref=target.at[pair_at(i)],
-            send_sem=send.at[pair],
-            recv_sem=recv.at[pair],
+            send_sem=send.at[i],
+            recv_sem=recv.at[i],
             device_id=ring.where(ring.bit_core),
             device_id_type=MESH,
         )
@@ -1173,9 +1176,68 @@
             device_id_type=MESH,
         )
 
-    def block(i, carry):
-        place = block_at(i)
-        other = i % 2 == 0
+    def join(kind, i):
+        pair = pair_at(i)
+        tmp, near, own = ((tmp_down, near_down, own_down), (tmp_two, near_two, own_two))[kind]
+        core_copy(kind, i).wait_recv()
+        tmp_copy(kind, i).start()
+        tmp_copy(kind, i).wait()
+
+        @pl.when(pair == 0)
+        def _():
+            add_near(own, own, tmp)
+
+        @pl.when(pair > 0)
+        def _():
+            here = near.at[jnp.maximum(pair, 1) - 1]
+            add_near(here, here, tmp)
+
+    wide = min(512, width)
+    piece = min(256, hidden)
+
+    def give(kind, i, left, product, far, near, own):
+        pair = pair_at(i)
+
+        @pl.when(i >= 1)
+        def _():
+            join(kind, i - 1)
+            core_copy(kind, i - 1).wait_send()
+
+        @pl.when(i == 3)
+        def _():
+            late(7 - 2 * kind).start()
+            late(8 - 2 * kind).start()
+
+        for c in range(width // wide):
+            part = slice(c * wide, (c + 1) * wide)
+            whole = product(left, part)
+            far[:, part] = whole[size:].astype(bf16)
+            mine = whole[:size]
+
+            @pl.when(pair == 0)
+            def _():
+                own[:, part] = mine + own[:, part] if kind == 0 else mine
+
+            @pl.when(pair > 0)
+            def _():
+                near[jnp.maximum(pair, 1) - 1, :, part] = mine.astype(bf16)
+
+        core_copy(kind, i).start()
+
+    second = {}
+
+    def pass_sums(kind):
+        near, to_a, to_b = ((near_down, a_down, b_down), (near_two, a_two, b_two))[kind]
+        join(kind, QUAD - 1)
+        late(7 - 2 * kind).wait_recv()
+        add_near(near.at[0, top], near.at[0, top], halves.at[kind, 0])
+        second["a", kind] = mail.post(near.at[0], to_a, ring.bit_a)
+        late(8 - 2 * kind).wait_recv()
+        add_near(near.at[1, end], near.at[1, end], halves.at[kind, 1])
+        second["b", kind] = mail.post(near.at[1], to_b, ring.bit_b)
+        core_copy(kind, QUAD - 1).wait_send()
+
+    def ahead(i, carry):
         pair = pair_at(i)
 
         @pl.when(i == 2)
@@ -1186,83 +1248,45 @@
             share.from_b.wait_recv()
             late(1).start()
             late(3).start()
-            late(2).wait_recv()
-
-        @pl.when(i == 4)
+
+        @pl.when(i == 3)
         def _():
             late(0).wait_recv()
             late(1).wait_recv()
             late(4).start()
-            late(3).wait_recv()
-            late(4).wait_recv()
-
-        @pl.when(i == 6)
+
+        for copy in act_copies(i):
+            copy.wait()
+
+        @pl.when(i + 1 < QUAD)
         def _():
-            for n in range(5, 9):
-                late(n).start()
-
-        dy_copy = pltpu.make_async_copy(dy.at[place], dy_in, dy_sem.at[0])
-        dy_copy.start()
-
-        @pl.when(jnp.logical_not(other))
-        def _():
-            for kind in range(2):
-                core_copy(kind, i).wait_recv()
-                tmp_copy(kind, i).start()
-
-        act_copy(i).wait()
-
-        @pl.when(i + 1 < 2 * QUAD)
-        def _():
-            act_copy(i + 1).start()
+            for copy in act_copies(i + 1):
+                copy.start()
 
         act = act_in[i % 2]
-        gate_pre = dot(act, w_g[...], 1, 0)
-        up_proj = dot(act, w_u[...], 1, 0)
-        sigmoid_gate = jax.nn.sigmoid(gate_pre)
-        swish = gate_pre * sigmoid_gate
-        middle[place] = (swish * up_proj).astype(bf16)
-        dy_copy.wait()
-        grad_middle = dot(dy_in[...], w_d[...], 1, 1)
-        cols[place, :, hidden:] = (grad_middle * swish).astype(bf16)
-        cols[place, :, :hidden] = (
-            grad_middle * up_proj * sigmoid_gate * (1.0 + gate_pre * (1.0 - sigmoid_gate))
-        ).astype(bf16)
-        down = dot(middle[place], w_d[...], 1, 0)
-
-        def give(kind, part, far, tmp, near, own):
-            @pl.when(other)
-            def _():
-                @pl.when(i >= 2)
-                def _():
-                    core_copy(kind, i - 2).wait_send()
-
-                far[...] = part.astype(bf16)
-                core_copy(kind, i).start()
-
-            @pl.when(jnp.logical_not(other))
-            def _():
-                tmp_copy(kind, i).wait()
-                total = part + tmp[...].astype(f32)
-
-                @pl.when(pair == 0)
-                def _():
-                    own[...] = total + own[...] if kind == 0 else total
-
-                @pl.when(pair > 0)
-                def _():
-                    near[jnp.maximum(pair, 1) - 1] = total.astype(bf16)
-
-        give(0, down, far_down, tmp_down, near_down, own_down)
-        two = dot(cols[place, :, :hidden], w_g[...], 1, 1) + dot(
-            cols[place, :, hidden:], w_u[...], 1, 1
-        )
-        give(1, two, far_two, tmp_two, near_two, own_two)
+        for c in range(hidden // piece):
+            part = slice(c * piece, (c + 1) * piece)
+            up_part = slice(hidden + c * piece, hidden + (c + 1) * piece)
+            gate_pre = dot(act, w_g[:, part], 1, 0)
+            up_proj = dot(act, w_u[:, part], 1, 0)
+            ready = (gate_pre * jax.nn.sigmoid(gate_pre) * up_proj).astype(bf16)
+            for rows, place in ((slice(0, size), pair), (slice(size, None), QUAD + pair)):
+                middle[place, :, part] = ready[rows]
+                cols[place, :, part] = gate_pre[rows].astype(bf16)
+                cols[place, :, up_part] = up_proj[rows].astype(bf16)
+
+        give(
+            0, i,
+            jnp.concatenate([middle[pair], middle[QUAD + pair]], axis=0),
+            lambda left, part: dot(left, w_d[:, part], 1, 0),
+            far_down, near_down, own_down,
+        )
         return carry
 
-    lax.fori_loop(0, 2 * QUAD, block, 0)
-    for kind in range(2):
-        core_copy(kind, 2 * QUAD - 2).wait_send()
+    lax.fori_loop(0, QUAD, ahead, 0)
+    pass_sums(0)
+    for n in (2, 3, 4):
+        late(n).wait_recv()
 
     cut = act_cut.shape[3]
     cuts = width // cut
@@ -1280,45 +1304,84 @@
             stage_d.at[i % 2], p_d.at[:, pl.ds(start, cut)], out_sems.at[i % 2]
         )
 
-    cut_copy(dy, dy_cut, 0).start()
-
-    def down_step(i, carry):
-        cut_copy(dy, dy_cut, i).wait()
-
-        @pl.when(i + 1 < cuts)
-        def _():
-            cut_copy(dy, dy_cut, i + 1).start()
-
-        turned = dot(
-            dy_cut[i % 2].reshape(tokens, cut), middle[...].reshape(tokens, hidden), 0, 0
-        )
-
-        @pl.when(i >= 2)
-        def _():
-            down_out(i - 2).wait()
-
-        stage_d[i % 2] = turned.T.astype(bf16)
-        down_out(i).start()
-        return carry
-
-    lax.fori_loop(0, cuts, down_step, 0)
-    cut_copy(act_two, act_cut, 0).start()
-    for i in (cuts - 2, cuts - 1):
-        down_out(i).wait()
     upper = flat // top_bit
     rows_half = hidden // 2
     away = pl.ds(pl.multiple_of((1 - upper) * rows_half, 16), rows_half)
     kept = pl.ds(pl.multiple_of(upper * rows_half, 16), rows_half)
-    sum_d = mail.post(p_d.at[away], land_d, top_bit)
-
-    second = {}
-    for kind, near, to_a, to_b in ((1, near_two, a_two, b_two), (0, near_down, a_down, b_down)):
-        late(7 - 2 * kind).wait_recv()
-        add_near(near.at[0, top], near.at[0, top], halves.at[kind, 0])
-        second["a", kind] = mail.post(near.at[0], to_a, ring.bit_a)
-        late(8 - 2 * kind).wait_recv()
-        add_near(near.at[1, end], near.at[1, end], halves.at[kind, 1])
-        second["b", kind] = mail.post(near.at[1], to_b, ring.bit_b)
+
+    def down_send_at(i):
+        part = pl.ds(pl.multiple_of(i * cut, cut), cut)
+        return pltpu.make_async_remote_copy(
+            src_ref=p_d.at[away, part],
+            dst_ref=land_d.at[:, part],
+            send_sem=pd_send.at[i],
+            recv_sem=pd_recv.at[i],
+            device_id=ring.where(top_bit),
+            device_id_type=MESH,
+        )
+
+    cut_copy(dy, dy_cut, 0).start()
+
+    def down_step(i, carry):
+        cut_copy(dy, dy_cut, i).wait()
+
+        @pl.when(i + 1 < cuts)
+        def _():
+            cut_copy(dy, dy_cut, i + 1).start()
+
+        turned = dot(
+            dy_cut[i % 2].reshape(tokens, cut), middle[...].reshape(tokens, hidden), 0, 0
+        )
+
+        stage_d[i % 2] = turned.T.astype(bf16)
+        down_out(i).start()
+
+        @pl.when(i >= 1)
+        def _():
+            down_out(i - 1).wait()
+            down_send_at(i - 1).start()
+
+        return carry
+
+    lax.fori_loop(0, cuts, down_step, 0)
+    cut_copy(act_two, act_cut, 0).start()
+    down_out(cuts - 1).wait()
+    down_send_at(cuts - 1).start()
+
+    def behind(i, carry):
+        pair = pair_at(i)
+        dy_copies = pair_copies(dy, dy_in, dy_sem, i)
+        for copy in dy_copies:
+            copy.start()
+        for copy in dy_copies:
+            copy.wait()
+        grads = dy_in[...]
+        for c in range(hidden // piece):
+            part = slice(c * piece, (c + 1) * piece)
+            up_part = slice(hidden + c * piece, hidden + (c + 1) * piece)
+            grad_middle = dot(grads, w_d[part, :], 1, 1)
+            for rows, place in ((slice(0, size), pair), (slice(size, None), QUAD + pair)):
+                gate_pre = cols[place, :, part].astype(f32)
+                up_proj = cols[place, :, up_part].astype(f32)
+                sigmoid_gate = jax.nn.sigmoid(gate_pre)
+                swish = gate_pre * sigmoid_gate
+                came = grad_middle[rows]
+                cols[place, :, up_part] = (came * swish).astype(bf16)
+                cols[place, :, part] = (
+                    came * up_proj * sigmoid_gate * (1.0 + gate_pre * (1.0 - sigmoid_gate))
+                ).astype(bf16)
+
+        give(
+            1, i,
+            jnp.concatenate([cols[pair], cols[QUAD + pair]], axis=0),
+            lambda left, part: dot(left[:, :hidden], w_g[part, :], 1, 1)
+            + dot(left[:, hidden:], w_u[part, :], 1, 1),
+            far_two, near_two, own_two,
+        )
+        return carry
+
+    lax.fori_loop(0, QUAD, behind, 0)
+    pass_sums(1)
 
     def stage_out(i):
         rows = pl.ds(pl.multiple_of(i * cut, cut), cut)
@@ -1375,7 +1438,8 @@
             mail.keep(own_two, added)
         else:
             mail.keep(far_down, layer_out)
-    sum_d.wait_recv()
+    for i in range(cuts):
+        down_send_at(i).wait()
     add_far(half_d, p_d.at[kept], land_d)
     for n in range(9):
         late(n).wait_send()
@@ -1416,8 +1480,8 @@
             pltpu.VMEM((hidden, width), bf16),
             pltpu.VMEM((2 * QUAD, size, hidden), bf16),
             pltpu.VMEM((2 * QUAD, size, 2 * hidden), bf16),
-            pltpu.VMEM((2, size, width), bf16),
-            vw,
+            pltpu.VMEM((2, 2 * size, width), bf16),
+            pltpu.VMEM((2 * size, width), bf16),
             pltpu.VMEM((2, 2 * QUAD, size, cut), bf16),
             pltpu.VMEM((2, 2 * QUAD, size, cut), bf16),
             pltpu.VMEM((2, hidden, cut), bf16),
@@ -1431,7 +1495,8 @@
             pltpu.VMEM((2, cut, 2 * hidden), bf16),
             dma((32,)), dma((32,)), dma((16,)),
             dma((QUAD,)), dma((QUAD,)), dma((QUAD,)), dma((QUAD,)),
-            dma((2,)), dma((1,)), dma((2,)), dma((2,)), dma((6,)),
+            dma((2, 2)), dma((2,)), dma((2,)), dma((2,)), dma((6,)),
+            dma((width // cut,)), dma((width // cut,)),
         ],
         compiler_params=pltpu.CompilerParams(
             collective_id=2, has_side_effects=True, vmem_limit_bytes=63 * 1024 * 1024

time: 713 us -> 692 us (0.971)
  Pallas kernels: 679 us -> 661 us
    pallas_call x1, Pallas kernels: 280 us -> 259 us  [front(): pl.pallas_call(functools.partial(front_kernel, outer, inner, seq_len), ou...]
where the time goes in v6:
time: 692 us; the launch traced here: 681 us
  Pallas kernels  661 us (96%)
  local copies, waits for them, and re-layouts  11.4 us (2%)
    pallas_call x1, Pallas kernels, front(): pl.pallas_call(functools.partial(front_kernel, outer, inner, seq_len), ou...  259 us
    pallas_call x1, Pallas kernels, back(): pl.pallas_call(functools.partial(back_kernel, outer, inner, seq_len), out...  244 us
    pallas_call x1, Pallas kernels, mid(): pl.pallas_call(functools.partial(mid_kernel, outer, inner, hidden_rows),...  157 us

profile of v6, /device:TPU:1, one launch (start us, length us, event | category | flops | bytes accessed | tf_op | source)
XLA Modules:
  0.0 681.0 jit_solution(4422726599799319141)
XLA Ops:
  1.3 1.3 fusion.3
  3.3 0.7 maximum_convert_fusion
  4.0 0.1 broadcast_multiply_fusion
  4.1 0.4 dynamic_update_slice.3.gain_ref
  4.4 0.0 copy-start.8
  4.5 0.1 fusion.2
  4.6 0.7 broadcast_in_dim_reshape.3.factor_ref
  5.3 0.8 copy.25.sin_ref
  6.1 0.8 copy.24.cos_ref
  7.0 0.0 copy-done.8
  7.0 259.3 %front.1 = (bf16[8,256,2048]{2,1,0:T(8,128)(2,1)}, bf16[2048,768]{1,0:T(8,128)(2,1)}, bf16[256,2048]{1,0:T(8,128)(2,1)}, bf16[8,256,256]{2,1,0:T(8,128)(2,1)}, b...) custom-call(bf16[256,2048]{1,0:T(8,128)(2,1)} %bitcast.16, ...), custom_call_target="tpu_custom_call" | custom-call | tf_op jit(solution)/shard_map/front/pallas_call | solution.py:580
  266.3 157.4 %mid.1 = (bf16[2048,1024]{1,0:T(8,128)(2,1)}, bf16[2048,1024]{1,0:T(8,128)(2,1)}, bf16[512,2048]{1,0:T(8,128)(2,1)}, f32[256,2048]{1,0:T(8,128)}, bf16[256,2048]...) custom-call(bf16[256,2048]{1,0:T(8,128)(2,1)} %bitcast.14, ...), custom_call_target="tpu_custom_call" | custom-call | tf_op jit(solution)/shard_map/mid/pallas_call | solution.py:1472
  423.8 243.9 %back.1 = (f32[64,2048]{1,0:T(8,128)}, f32[64,2048]{1,0:T(8,128)}, f32[64,2048]{1,0:T(8,128)}, f32[64,2048]{1,0:T(8,128)}, f32[8,2048]{1,0:T(8,128)}, /*index=5*...) custom-call(bf16[256,2048]{1,0:T(8,128)(2,1)} %bitcast.17, ...), custom_call_target="tpu_custom_call" | custom-call | tf_op jit(solution)/shard_map/back/pallas_call | solution.py:1034
  667.7 0.0 copy-start.2
  667.7 0.8 constant_dynamic-slice_fusion
  668.6 0.5 slice_bitcast_fusion
  669.1 2.7 convert_element_type.35
  671.8 0.0 copy-done.2
  671.8 1.5 convert_element_type.36
  673.2 0.1 copy-done.3
  673.4 1.0 copy.37
  674.3 0.3 copy-done.1
  674.7 1.3 copy.38
  676.0 0.0 copy-done.7
  676.0 0.8 copy.39
  676.8 0.0 copy-done.6
  676.8 0.8 copy.40
  677.6 0.0 copy-done.5
  677.6 0.8 copy.41
  678.4 0.8 copy.42
  679.2 0.0 copy-done
  679.2 1.3 copy.43
  (14 shorter events, 0.1 us)
Async XLA Ops:
  4.4 2.5 copy-start.8
  667.7 4.1 copy-start.2
  671.8 1.6 copy-start.3
  671.8 2.9 copy-start.1
  674.6 1.4 copy-start.7
  674.7 2.2 copy-start.6
  674.7 3.0 copy-start.5
  676.0 2.4 copy-start.4
  676.0 3.2 copy-start

commit v7 on v6

--- a/solution.py
+++ b/solution.py
@@ -291,8 +291,9 @@
     outer, inner, seq_len,
     x_ref, gain_ref, wq_ref, wk_ref, wv_ref, cos_ref, sin_ref,
     wo_ref, wg_ref, wu_ref, wd_ref,
-    act_one, w_qkv, w_o, q_out, k_out, v_out, att_out, resid_out, gains_out,
+    act_one_far, w_qkv_far, w_o_far, q_far, k_far, v_far, att_far, resid_far, gains_out,
     act_two, w_g, w_u, w_d,
+    act_one, w_qkv, w_o, q_out, k_out, v_out, att_out, resid_out,
     cut, gain_in, x_all, far, core_in, near, own_sum, mid, in_a, in_b, act_two_own,
     send_sems, recv_sems, local_sems, far_send, far_recv,
 ):
@@ -433,6 +434,8 @@
         norm_block(place)
     spread_o.done()
     spread_qkv.done()
+    mail.keep(w_o, w_o_far)
+    mail.keep(w_qkv, w_qkv_far)
 
     scale = HEAD_DIM**-0.5
     cosine, sine = cos_ref[...], sin_ref[...]
@@ -504,10 +507,13 @@
     norm_block(QUAD - 1)
     share_x.done((QUAD - 1,))
     norm_block(2 * QUAD - 1)
+    mail.keep(act_one, act_one_far)
     far_step(QUAD - 1, 0)
     near_step(QUAD - 1, 0)
     for j in range(QUAD):
         far_copy(j).wait_send()
+    for here, far_off in ((q_out, q_far), (k_out, k_far), (v_out, v_far), (att_out, att_far)):
+        mail.keep(here, far_off)
     total = Total(mail, near, own_sum, mid, in_a, in_b)
     total.first()
     total.first_a()
@@ -531,6 +537,7 @@
 
     lax.fori_loop(0, size // strip, norm_two, 0)
     mail.keep(act_two_own, act_two.at[0])
+    mail.keep(resid_out, resid_far)
     share_two = Share(mail, act_two, act_two_own)
     share_two.first()
     for piece in range(1, spread_g.pieces):
@@ -557,7 +564,7 @@
     places = outer * inner // (2 * QUAD)
     pieces = 2 if span == 1 else 2 * QUAD
     remote = (places - 1) * (3 * pieces + 3) + 7 + 14 * places // span + 8 + 24
-    local = 8 + 2 * places // span
+    local = 24 + 2 * places // span
     vm = pl.BlockSpec(memory_space=pltpu.VMEM)
     hbm = pl.BlockSpec(memory_space=pl.ANY)
     eight = (2 * QUAD, size)
@@ -581,8 +588,9 @@
         functools.partial(front_kernel, outer, inner, seq_len),
         out_shape=out_shape,
         in_specs=[vm] * 7 + [hbm] * 4,
-        out_specs=tuple([vm] * 9 + [hbm] * 4),
-        scratch_shapes=[
+        out_specs=tuple([hbm] * 8 + [vm] + [hbm] * 4),
+        scratch_shapes=[pltpu.VMEM(s.shape, s.dtype) for s in out_shape[:8]]
+        + [
             pltpu.VMEM((2 * QUAD, rows, 3 * narrow), bf16),
             pltpu.VMEM((8, 8, width), f32),
             pltpu.VMEM((2 * QUAD, size, width), bf16),
@@ -694,10 +702,12 @@
 
 def back_kernel(
     outer, inner, seq_len,
-    x_ref, go_ref, factor_ref, gains_ref, q_ref, k_ref, v_ref, att_ref, w_qkv, w_o, cos_ref, sin_ref,
+    x_ref, go_ref, factor_ref, gains_ref, cos_ref, sin_ref,
+    q_far, k_far, v_far, att_far, w_qkv_far, w_o_far,
     p_g, p_u, half_d, act_one, resid_ref, two_ref,
     out_q, out_k, out_v, out_o, gain_grads,
     out_gate, out_up, out_d, land_g, land_u, land_d, sum_g, sum_u, sum_d, fin_g, fin_u, land_qkv, land_o, grad_tokens,
+    q_ref, k_ref, v_ref, att_ref, w_qkv, w_o,
     near, core_in, far, own_sum, grad_resid, branch,
     mid, in_a, in_b,
     acts, d_qkv, p_qkv, p_o, p_o_sum, sum_qkv, sum_o, fin_qkv, qkv_in, gain_in,
@@ -760,6 +770,12 @@
 
     load_resid = mail.keep(resid_ref, grad_resid)
     load_two = mail.keep(two_ref, own_sum)
+    loads = [
+        mail.keep(far_off, here)
+        for far_off, here in (
+            (w_o_far, w_o), (att_far, att_ref), (q_far, q_ref), (k_far, k_ref), (v_far, v_ref), (w_qkv_far, w_qkv),
+        )
+    ]
     collect_d.start()
     for which in (True, False):
         collect_g.start(which)
@@ -787,6 +803,9 @@
         collect_u.take_away(top_stage, piece)
     share.third()
     p_o_sum[...] = jnp.zeros_like(p_o_sum)
+    for copy in loads:
+        copy.wait()
+        mail.kept = [c for c in mail.kept if c is not copy]
     share.done()
 
     scale = HEAD_DIM**-0.5
@@ -991,10 +1010,10 @@
 
 
 def back(outer, inner, seq_len, near_args, far_args):
-    tokens, w_qkv, w_o = near_args[0], near_args[8], near_args[9]
+    tokens, w_qkv, w_o = near_args[0], far_args[4], far_args[5]
     size, width = tokens.shape
     narrow = w_o.shape[0]
-    hidden = far_args[0].shape[1]
+    hidden = far_args[6].shape[1]
     places = outer * inner // (2 * QUAD)
     rows = width // (outer * inner)
     hidden_rows = hidden // places
@@ -1002,7 +1021,7 @@
     pieces = 2 if span == 1 else 2 * QUAD
     run_rows = 2 * QUAD * rows // pieces
     remote = (places - 1) * (3 * pieces + 2) + 7 + 14 * places // span + 8 + 24
-    local = 8 + 2 * places // span
+    local = 20 + 2 * places // span
     vm = pl.BlockSpec(memory_space=pltpu.VMEM)
     hbm = pl.BlockSpec(memory_space=pl.ANY)
     sds = jax.ShapeDtypeStruct
@@ -1036,7 +1055,8 @@
         out_shape=out_shape,
         in_specs=[vm] * len(near_args) + [hbm] * len(far_args),
         out_specs=tuple([vm] * 5 + [hbm] * 14),
-        scratch_shapes=[
+        scratch_shapes=[pltpu.VMEM(a.shape, a.dtype) for a in (*far_args[:4], w_qkv, w_o)]
+        + [
             four, four, pltpu.VMEM((2, size, width), bf16),
             pltpu.VMEM((size, width), f32),
             pltpu.VMEM((size, width), f32),
@@ -1071,10 +1091,10 @@
     outer, inner, hidden_rows,
     go_ref, factor_ref,
     act_two, wg_ref, wu_ref, wd_ref, resid_ref,
-    p_g, p_u, half_d, added, layer_out, dy, p_d, land_d, land_down, land_two, a_down, b_down, a_two, b_two,
+    p_g, p_u, half_d, added, layer_out, dy, p_d, land_d, a_down, b_down, a_two, b_two,
     w_g, w_u, w_d, middle, cols, act_in, dy_in, act_cut, dy_cut, stage_d, dy_own,
     far_down, far_two, tmp_down, tmp_two, near_down, near_two, own_down, own_two, halves, stage,
-    send_sems, recv_sems, local_sems, down_send, down_recv, two_send, two_recv, act_sems, dy_sem, tmp_sems, cut_sems, out_sems, pd_send, pd_recv,
+    send_sems, recv_sems, local_sems, down_send, down_recv, two_send, two_recv, act_sems, dy_sem, cut_sems, out_sems, pd_send, pd_recv,
 ):
     size, width = go_ref.shape
     hidden = w_g.shape[1]
@@ -1136,21 +1156,17 @@
 
     def core_copy(kind, i):
         source, target, send, recv = (
-            (far_down, land_down, down_send, down_recv),
-            (far_two, land_two, two_send, two_recv),
+            (far_down, tmp_down, down_send, down_recv),
+            (far_two, tmp_two, two_send, two_recv),
         )[kind]
         return pltpu.make_async_remote_copy(
             src_ref=source,
-            dst_ref=target.at[pair_at(i)],
+            dst_ref=target.at[i % 2],
             send_sem=send.at[i],
             recv_sem=recv.at[i],
             device_id=ring.where(ring.bit_core),
             device_id_type=MESH,
         )
-
-    def tmp_copy(kind, i):
-        source, target = ((land_down, tmp_down), (land_two, tmp_two))[kind]
-        return pltpu.make_async_copy(source.at[pair_at(i)], target, tmp_sems.at[kind])
 
     base = mail.used
     mail.used += 9
@@ -1180,8 +1196,7 @@
         pair = pair_at(i)
         tmp, near, own = ((tmp_down, near_down, own_down), (tmp_two, near_two, own_two))[kind]
         core_copy(kind, i).wait_recv()
-        tmp_copy(kind, i).start()
-        tmp_copy(kind, i).wait()
+        tmp = tmp.at[i % 2]
 
         @pl.when(pair == 0)
         def _():
@@ -1421,13 +1436,13 @@
     for kind, own, in_a, in_b in ((1, own_two, a_two, b_two), (0, own_down, a_down, b_down)):
         second["a", kind].wait_recv()
         second["b", kind].wait_recv()
-        first = mail.keep(in_a, tmp_down)
-        other = mail.keep(in_b, tmp_two)
+        first = mail.keep(in_a, tmp_down.at[0])
+        other = mail.keep(in_b, tmp_two.at[0])
         settle(first)
         settle(other)
 
         def finish(part, own=own, kind=kind):
-            total = own[part, :] + tmp_down[part, :].astype(f32) + tmp_two[part, :].astype(f32)
+            total = own[part, :] + tmp_down[0, part, :].astype(f32) + tmp_two[0, part, :].astype(f32)
             if kind:
                 own_two[part, :] = total
             else:
@@ -1462,8 +1477,6 @@
         sds((2 * QUAD, size, width), bf16),
         sds((hidden, width), bf16),
         sds((hidden // 2, width), bf16),
-        sds((QUAD, size, width), bf16),
-        sds((QUAD, size, width), bf16),
         wide, wide, wide, wide,
     )
     cut = min(256, width // 2)
@@ -1486,7 +1499,9 @@
             pltpu.VMEM((2, 2 * QUAD, size, cut), bf16),
             pltpu.VMEM((2, hidden, cut), bf16),
             vw,
-            vw, vw, vw, vw,
+            vw, vw,
+            pltpu.VMEM((2, size, width), bf16),
+            pltpu.VMEM((2, size, width), bf16),
             pltpu.VMEM((QUAD - 1, size, width), bf16),
             pltpu.VMEM((QUAD - 1, size, width), bf16),
             pltpu.VMEM((size, width), f32),
@@ -1495,7 +1510,7 @@
             pltpu.VMEM((2, cut, 2 * hidden), bf16),
             dma((32,)), dma((32,)), dma((16,)),
             dma((QUAD,)), dma((QUAD,)), dma((QUAD,)), dma((QUAD,)),
-            dma((2, 2)), dma((2,)), dma((2,)), dma((2,)), dma((6,)),
+            dma((2, 2)), dma((2,)), dma((2,)), dma((6,)),
             dma((width // cut,)), dma((width // cut,)),
         ],
         compiler_params=pltpu.CompilerParams(
@@ -1561,10 +1576,9 @@
     results = back(
         outer_count, inner_count, seq_len,
         (
-            x_rows, grad_out.reshape(-1, width), factor_rows, gains, q_rot, k_rot, values, attended,
-            w_qkv, w_o, wide_cosine, wide_sine,
+            x_rows, grad_out.reshape(-1, width), factor_rows, gains, wide_cosine, wide_sine,
         ),
-        (p_g, p_u, half_d, act_one, resid, added),
+        (q_rot, k_rot, values, attended, w_qkv, w_o, p_g, p_u, half_d, act_one, resid, added),
     )
     query_grad, key_grad, value_grad, out_grad, gain_grads = results[:5]
     gate_grad, up_grad, down_grad = (a.astype(f32) for a in results[5:8])

time: 692 us -> 679 us (0.981)
  Pallas kernels: 661 us -> 648 us
where the time goes in v7:
time: 679 us; the launch traced here: 668 us
  Pallas kernels  648 us (95%)
  local copies, waits for them, and re-layouts  11.4 us (2%)
    pallas_call x1, Pallas kernels, front(): pl.pallas_call(functools.partial(front_kernel, outer, inner, seq_len), ou...  254 us
    pallas_call x1, Pallas kernels, back(): pl.pallas_call(functools.partial(back_kernel, outer, inner, seq_len), out...  242 us
    pallas_call x1, Pallas kernels, mid(): pl.pallas_call(functools.partial(mid_kernel, outer, inner, hidden_rows),...  153 us

profile of v7, /device:TPU:1, one launch (start us, length us, event | category | flops | bytes accessed | tf_op | source)
XLA Modules:
  0.0 668.0 jit_solution(12871173121470221498)
XLA Ops:
  1.3 1.3 fusion.3
  3.3 0.7 maximum_convert_fusion
  4.0 0.1 broadcast_multiply_fusion
  4.1 0.4 dynamic_update_slice.3.gain_ref
  4.4 0.0 copy-start.8
  4.5 0.1 fusion.2
  4.6 0.7 broadcast_in_dim_reshape.3.factor_ref
  5.3 0.8 copy.25.sin_ref
  6.1 0.8 copy.24.cos_ref
  7.0 0.0 copy-done.8
  7.0 253.6 %front.1 = (bf16[8,256,2048]{2,1,0:T(8,128)(2,1)}, bf16[2048,768]{1,0:T(8,128)(2,1)}, bf16[256,2048]{1,0:T(8,128)(2,1)}, bf16[8,256,256]{2,1,0:T(8,128)(2,1)}, b...) custom-call(bf16[256,2048]{1,0:T(8,128)(2,1)} %bitcast.16, ...), custom_call_target="tpu_custom_call" | custom-call | tf_op jit(solution)/shard_map/front/pallas_call | solution.py:587
  260.6 152.5 %mid.1 = (bf16[2048,1024]{1,0:T(8,128)(2,1)}, bf16[2048,1024]{1,0:T(8,128)(2,1)}, bf16[512,2048]{1,0:T(8,128)(2,1)}, f32[256,2048]{1,0:T(8,128)}, bf16[256,2048]...) custom-call(bf16[256,2048]{1,0:T(8,128)(2,1)} %bitcast.14, ...), custom_call_target="tpu_custom_call" | custom-call | tf_op jit(solution)/shard_map/mid/pallas_call | solution.py:1485
  413.2 241.6 %back.1 = (f32[64,2048]{1,0:T(8,128)}, f32[64,2048]{1,0:T(8,128)}, f32[64,2048]{1,0:T(8,128)}, f32[64,2048]{1,0:T(8,128)}, f32[8,2048]{1,0:T(8,128)}, /*index=5*...) custom-call(bf16[256,2048]{1,0:T(8,128)(2,1)} %bitcast.17, ...), custom_call_target="tpu_custom_call" | custom-call | tf_op jit(solution)/shard_map/back/pallas_call | solution.py:1053
  654.8 0.0 copy-start.2
  654.8 0.8 constant_dynamic-slice_fusion
  655.6 0.5 slice_bitcast_fusion
  656.1 2.7 convert_element_type.35
  658.8 0.0 copy-done.2
  658.8 1.5 convert_element_type.36
  660.3 0.1 copy-done.3
  660.4 1.0 copy.37
  661.4 0.3 copy-done.1
  661.7 1.3 copy.38
  663.0 0.0 copy-done.7
  663.1 0.8 copy.39
  663.9 0.0 copy-done.6
  663.9 0.8 copy.40
  664.7 0.0 copy-done.5
  664.7 0.8 copy.41
  665.5 0.0 copy-done.4
  665.5 0.8 copy.42
  666.3 1.3 copy.43
  (14 shorter events, 0.1 us)
Async XLA Ops:
  4.4 2.5 copy-start.8
  654.8 4.1 copy-start.2
  658.8 1.6 copy-start.3
  658.8 2.9 copy-start.1
  661.7 1.4 copy-start.7
  661.7 2.2 copy-start.6
  661.7 3.0 copy-start.5
  663.1 2.4 copy-start.4
  663.1 3.2 copy-start

commit v8 on v7

--- a/solution.py
+++ b/solution.py
@@ -973,14 +973,18 @@
 
     strips(first_norm)
     mail.keep(grad_resid, grad_tokens)
-    for step, bit in enumerate([ring.bit_core, ring.bit_a, ring.bit_b] + bits):
-        copy = mail.post(gain_grads, gain_in.at[step], bit)
-        copy.wait()
-        mail.sent = [c for c in mail.sent if c is not copy]
-        gain_grads[...] = gain_grads[...] + gain_in[step]
+    gains = Adding(
+        mail, gain_grads, gain_in, [ring.bit_core] + bits[::-1] + [ring.bit_a, ring.bit_b]
+    )
+    gains.post()
+    collect_o.finish_piece(0)
+    gains.take()
+    gains.post()
     for piece in range(collect_qkv.pieces):
         collect_qkv.finish_piece(piece)
-    collect_o.finish_piece(0)
+        if gains.step < len(gains.bits) - 1:
+            gains.take()
+            gains.post()
 
     swaps = []
     for delta in ring.deltas:
@@ -993,6 +997,10 @@
             kept = mail.keep(src, dst)
     kept.wait()
     mail.kept = [c for c in mail.kept if c is not kept]
+    gains.take()
+    while gains.step < len(gains.bits):
+        gains.post()
+        gains.take()
     for copy in swaps:
         copy.wait_recv()
     for j, ref in enumerate((out_q, out_k, out_v)):

time: 679 us -> 668 us (0.984)
  Pallas kernels: 648 us -> 636 us
    pallas_call x1, Pallas kernels: 242 us -> 230 us  [back(): pl.pallas_call(functools.partial(back_kernel, outer, inner, seq_len), out...]
where the time goes in v8:
time: 668 us; the launch traced here: 657 us
  Pallas kernels  636 us (95%)
  local copies, waits for them, and re-layouts  11.4 us (2%)
    pallas_call x1, Pallas kernels, front(): pl.pallas_call(functools.partial(front_kernel, outer, inner, seq_len), ou...  254 us
    pallas_call x1, Pallas kernels, back(): pl.pallas_call(functools.partial(back_kernel, outer, inner, seq_len), out...  230 us
    pallas_call x1, Pallas kernels, mid(): pl.pallas_call(functools.partial(mid_kernel, outer, inner, hidden_rows),...  153 us

profile of v8, /device:TPU:1, one launch (start us, length us, event | category | flops | bytes accessed | tf_op | source)
XLA Modules:
  0.0 656.8 jit_solution(17629423500369908094)
XLA Ops:
  1.3 1.3 fusion.3
  3.3 0.7 maximum_convert_fusion
  4.0 0.1 broadcast_multiply_fusion
  4.1 0.4 dynamic_update_slice.3.gain_ref
  4.4 0.0 copy-start.8
  4.5 0.1 fusion.2
  4.6 0.7 broadcast_in_dim_reshape.3.factor_ref
  5.3 0.8 copy.25.sin_ref
  6.1 0.8 copy.24.cos_ref
  7.0 0.0 copy-done.8
  7.0 253.6 %front.1 = (bf16[8,256,2048]{2,1,0:T(8,128)(2,1)}, bf16[2048,768]{1,0:T(8,128)(2,1)}, bf16[256,2048]{1,0:T(8,128)(2,1)}, bf16[8,256,256]{2,1,0:T(8,128)(2,1)}, b...) custom-call(bf16[256,2048]{1,0:T(8,128)(2,1)} %bitcast.16, ...), custom_call_target="tpu_custom_call" | custom-call | tf_op jit(solution)/shard_map/front/pallas_call | solution.py:587
  260.6 152.5 %mid.1 = (bf16[2048,1024]{1,0:T(8,128)(2,1)}, bf16[2048,1024]{1,0:T(8,128)(2,1)}, bf16[512,2048]{1,0:T(8,128)(2,1)}, f32[256,2048]{1,0:T(8,128)}, bf16[256,2048]...) custom-call(bf16[256,2048]{1,0:T(8,128)(2,1)} %bitcast.14, ...), custom_call_target="tpu_custom_call" | custom-call | tf_op jit(solution)/shard_map/mid/pallas_call | solution.py:1493
  413.2 230.3 %back.1 = (f32[64,2048]{1,0:T(8,128)}, f32[64,2048]{1,0:T(8,128)}, f32[64,2048]{1,0:T(8,128)}, f32[64,2048]{1,0:T(8,128)}, f32[8,2048]{1,0:T(8,128)}, /*index=5*...) custom-call(bf16[256,2048]{1,0:T(8,128)(2,1)} %bitcast.17, ...), custom_call_target="tpu_custom_call" | custom-call | tf_op jit(solution)/shard_map/back/pallas_call | solution.py:1061
  643.5 0.0 copy-start.2
  643.5 0.8 constant_dynamic-slice_fusion
  644.3 0.5 slice_bitcast_fusion
  644.9 2.7 convert_element_type.35
  647.5 0.0 copy-done.2
  647.5 1.5 convert_element_type.36
  649.0 0.1 copy-done.3
  649.1 1.0 copy.37
  650.1 0.3 copy-done.1
  650.4 1.3 copy.38
  651.8 0.0 copy-done.7
  651.8 0.8 copy.39
  652.6 0.0 copy-done.6
  652.6 0.8 copy.40
  653.4 0.0 copy-done.5
  653.4 0.8 copy.41
  654.2 0.0 copy-done.4
  654.2 0.8 copy.42
  655.0 1.3 copy.43
  (14 shorter events, 0.1 us)
Async XLA Ops:
  4.4 2.5 copy-start.8
  643.5 4.1 copy-start.2
  647.5 1.6 copy-start.3
  647.5 2.9 copy-start.1
  650.4 1.4 copy-start.7
  650.4 2.2 copy-start.6
  650.4 3.0 copy-start.5
  651.8 2.4 copy-start.4
  651.8 3.2 copy-start

commit v9 on v8

--- a/solution.py
+++ b/solution.py
@@ -617,7 +617,7 @@
 
 def add_far(target, left, right):
     rows, width = left.shape
-    strip = min(64, rows)
+    strip = min(rows, max(16, 131072 // width))
 
     def body(left_ref, right_ref, target_ref):
         target_ref[...] = (left_ref[...].astype(f32) + right_ref[...].astype(f32)).astype(

time: 668 us -> 667 us (level)
  no operation moved by 1% of the time
where the time goes in v9:
time: 667 us; the launch traced here: 657 us
  Pallas kernels  637 us (96%)
  local copies, waits for them, and re-layouts  11.4 us (2%)
    pallas_call x1, Pallas kernels, front(): pl.pallas_call(functools.partial(front_kernel, outer, inner, seq_len), ou...  254 us
    pallas_call x1, Pallas kernels, back(): pl.pallas_call(functools.partial(back_kernel, outer, inner, seq_len), out...  230 us
    pallas_call x1, Pallas kernels, mid(): pl.pallas_call(functools.partial(mid_kernel, outer, inner, hidden_rows),...  153 us

profile of v9, /device:TPU:1, one launch (start us, length us, event | category | flops | bytes accessed | tf_op | source)
XLA Modules:
  0.0 656.9 jit_solution(10618073057057350135)
XLA Ops:
  1.3 1.3 fusion.3
  3.3 0.7 maximum_convert_fusion
  4.0 0.1 broadcast_multiply_fusion
  4.1 0.4 dynamic_update_slice.3.gain_ref
  4.4 0.0 copy-start.8
  4.5 0.1 fusion.2
  4.6 0.7 broadcast_in_dim_reshape.3.factor_ref
  5.3 0.8 copy.25.sin_ref
  6.1 0.8 copy.24.cos_ref
  7.0 0.0 copy-done.8
  7.0 253.6 %front.1 = (bf16[8,256,2048]{2,1,0:T(8,128)(2,1)}, bf16[2048,768]{1,0:T(8,128)(2,1)}, bf16[256,2048]{1,0:T(8,128)(2,1)}, bf16[8,256,256]{2,1,0:T(8,128)(2,1)}, b...) custom-call(bf16[256,2048]{1,0:T(8,128)(2,1)} %bitcast.16, ...), custom_call_target="tpu_custom_call" | custom-call | tf_op jit(solution)/shard_map/front/pallas_call | solution.py:587
  260.6 152.5 %mid.1 = (bf16[2048,1024]{1,0:T(8,128)(2,1)}, bf16[2048,1024]{1,0:T(8,128)(2,1)}, bf16[512,2048]{1,0:T(8,128)(2,1)}, f32[256,2048]{1,0:T(8,128)}, bf16[256,2048]...) custom-call(bf16[256,2048]{1,0:T(8,128)(2,1)} %bitcast.14, ...), custom_call_target="tpu_custom_call" | custom-call | tf_op jit(solution)/shard_map/mid/pallas_call | solution.py:1493
  413.2 230.4 %back.1 = (f32[64,2048]{1,0:T(8,128)}, f32[64,2048]{1,0:T(8,128)}, f32[64,2048]{1,0:T(8,128)}, f32[64,2048]{1,0:T(8,128)}, f32[8,2048]{1,0:T(8,128)}, /*index=5*...) custom-call(bf16[256,2048]{1,0:T(8,128)(2,1)} %bitcast.17, ...), custom_call_target="tpu_custom_call" | custom-call | tf_op jit(solution)/shard_map/back/pallas_call | solution.py:1061
  643.6 0.0 copy-start.2
  643.6 0.8 constant_dynamic-slice_fusion
  644.5 0.5 slice_bitcast_fusion
  645.0 2.7 convert_element_type.35
  647.7 0.0 copy-done.2
  647.7 1.5 convert_element_type.36
  649.1 0.1 copy-done.3
  649.3 1.0 copy.37
  650.2 0.3 copy-done.1
  650.6 1.3 copy.38
  651.9 0.0 copy-done.7
  651.9 0.8 copy.39
  652.7 0.0 copy-done.6
  652.7 0.8 copy.40
  653.5 0.0 copy-done.5
  653.5 0.8 copy.41
  654.3 0.0 copy-done.4
  654.3 0.8 copy.42
  655.1 1.3 copy.43
  (14 shorter events, 0.1 us)
Async XLA Ops:
  4.4 2.5 copy-start.8
  643.6 4.1 copy-start.2
  647.7 1.6 copy-start.3
  647.7 2.9 copy-start.1
  650.6 1.4 copy-start.7
  650.6 2.2 copy-start.6
  650.6 3.0 copy-start.5
  651.9 2.4 copy-start.4
  651.9 3.2 copy-start
